TPU v7x, 32 devices: a whole 2x2x4 slice. The times are simulated.
32 devices in a mesh: fsdp: 4 (over y, x), ctx: 2 (over core), tp: 4 (over z).
Axes of the slice: x: 2, y: 2, z: 4, core: 2. Of those that a mesh axis runs over, the one named last changes fastest.
Arguments:
- tokens: bfloat16 [8, 4096, 512], P('fsdp', ('ctx', 'tp')), may hold values from -6 to 6
- timesteps: int32 [8], P('fsdp'), may hold values from 0 to 49
- time_table: bfloat16 [50, 512], replicated, may hold values from -6 to 6
- prefix: int32 [8], P('fsdp'), may hold values from 409 to 2048, as said below
- encoder: bfloat16 [8, 256, 512], P('fsdp'), may hold values from -6 to 6
- self_qkv: bfloat16 [3, 512, 512], P(None, 'fsdp', 'tp'), may hold values from -0.375 to 0.375
- cross_q: bfloat16 [512, 512], P('fsdp', 'tp'), may hold values from -0.375 to 0.375
- cross_kv: bfloat16 [2, 512, 512], P(None, 'fsdp', 'tp'), may hold values from -0.375 to 0.375
- self_out: bfloat16 [512, 512], P('tp', 'fsdp'), may hold values from -2 to 2
- cross_out: bfloat16 [512, 512], P('tp', 'fsdp'), may hold values from -0.5 to 0.5
- ffn_up: bfloat16 [512, 2048], P('fsdp', 'tp'), may hold values from -0.25 to 0.25
- ffn_down: bfloat16 [2048, 512], P('tp', 'fsdp'), may hold values from -0.125 to 0.125
- norm_gain: float32 [3, 512], replicated, may hold values from 0.5 to 1.5
- norm_bias: float32 [3, 512], replicated, may hold values from -1.25 to 1.25
- cotangent: bfloat16 [8, 4096, 512], P('fsdp', ('ctx', 'tp')), may hold values from -6 to 6
Outputs:
- output: float32 [8, 4096, 512], P('fsdp', ('ctx', 'tp'))
- input_grad: float32 [8, 4096, 512], P('fsdp', ('ctx', 'tp'))
- encoder_grad: float32 [8, 256, 512], P('fsdp', ('ctx', 'tp'))
- self_qkv_grad: float32 [3, 512, 512], P(None, 'fsdp', 'tp')
- cross_q_grad: float32 [512, 512], P('fsdp', 'tp')
- cross_kv_grad: float32 [2, 512, 512], P(None, 'fsdp', 'tp')
- self_out_grad: float32 [512, 512], P('tp', 'fsdp')
- cross_out_grad: float32 [512, 512], P('tp', 'fsdp')
- ffn_up_grad: float32 [512, 2048], P('fsdp', 'tp')
- ffn_down_grad: float32 [2048, 512], P('tp', 'fsdp')
- gain_grad: float32 [3, 512], replicated
- bias_grad: float32 [2, 512], replicated
- ffn_bias_grad: float32 [512], replicated
- norms: float32 [4], replicated
Inputs may be any that keep to these rules, and one draw needn't show every extreme that they name: Each sequence's prefix; some sequence has exactly 409 and some exactly 2048.
All inputs are finite; a program needn't handle non-finite values.
Results may differ from a plain program's by a relative error of at most 0.035.
Values may be sent and summed in bfloat16 or wider, within the bound.
A program may use at most 192 MiB of HBM per device.

v0:
```python
import math

import jax
import jax.numpy as jnp
from jax import lax
from jax.sharding import PartitionSpec as P

HEAD_DIM = 64


EPS = 1e-05
NEG = -1e30
ROOT_HALF = 1.0 / math.sqrt(2.0)
INV_ROOT_TWO_PI = 1.0 / math.sqrt(2.0 * math.pi)


def norm_rows(hidden, scaling, offsets):
    centre = hidden - jnp.mean(hidden, -1, keepdims=True)
    inverse = lax.rsqrt(jnp.mean(centre * centre, -1, keepdims=True) + EPS)
    unit_rows = centre * inverse
    return (unit_rows * scaling + offsets, unit_rows, inverse)


def norm_back(upstream, unit_rows, inverse, scaling):
    scaled = upstream * scaling
    result = inverse * (
        scaled
        - jnp.mean(scaled, -1, keepdims=True)
        - unit_rows * jnp.mean(scaled * unit_rows, -1, keepdims=True)
    )
    return (result, jnp.sum(upstream * unit_rows, (0, 1)), jnp.sum(upstream, (0, 1)))


def gelu_parts(inputs):
    normal_cdf = 0.5 * (1.0 + lax.erf(inputs * ROOT_HALF))
    return (
        inputs * normal_cdf,
        normal_cdf + inputs * jnp.exp(-0.5 * inputs * inputs) * INV_ROOT_TWO_PI,
    )


def spread_rows(rows):
    return lax.all_gather(rows, "tp", axis=1, tiled=True)


def spread_grads(grad_rows):
    return lax.all_gather(grad_rows, "tp", axis=1, tiled=True)


def finish_branch(local_in, local_weight):
    return lax.psum_scatter(
        jnp.einsum("scw,wd->scd", local_in, local_weight, preferred_element_type=jnp.float32),
        "tp",
        scatter_dimension=1,
        tiled=True,
    )


def finish_grad(local_grad, local_weight):
    return lax.psum_scatter(
        jnp.einsum("scw,dw->scd", local_grad, local_weight, preferred_element_type=jnp.float32),
        "tp",
        scatter_dimension=1,
        tiled=True,
    )


def block_scores(queries, key_block, query_pos, key_pos, lengths, factor):
    scores = (
        jnp.einsum("sqhe,skhe->sqhk", queries, key_block, preferred_element_type=jnp.float32)
        * factor
    )
    visible = (key_pos[None, None, :] <= query_pos[None, :, None]) | (
        key_pos[None, None, :] < lengths[:, None, None]
    )
    return jnp.where(visible[:, :, None, :], scores, NEG)


def attend_forward(queries, key_rows, value_rows, query_pos, lengths, key_span, factor):
    length = key_rows.shape[1]

    def attend_advance(running, offset):
        highest, totals, summed = running
        key_block = lax.dynamic_slice_in_dim(key_rows, offset, key_span, 1)
        value_block = lax.dynamic_slice_in_dim(value_rows, offset, key_span, 1)
        scores = block_scores(
            queries, key_block, query_pos, offset + lax.iota(jnp.int32, key_span), lengths, factor
        )
        new_high = jnp.maximum(highest, jnp.max(scores, -1))
        weights = jnp.exp(scores - new_high[..., None])
        fading = jnp.exp(highest - new_high)
        totals = totals * fading + jnp.sum(weights, -1)
        summed = summed * fading[..., None] + jnp.einsum(
            "sqhk,skhe->sqhe",
            weights.astype(jnp.bfloat16),
            value_block,
            preferred_element_type=jnp.float32,
        )
        return ((new_high, totals, summed), None)

    stat_shape = queries.shape[:3]
    initial = (
        jnp.full(stat_shape, NEG, jnp.float32),
        jnp.zeros(stat_shape, jnp.float32),
        jnp.zeros(queries.shape, jnp.float32),
    )
    offsets = jnp.arange(length // key_span, dtype=jnp.int32) * key_span
    (highest, totals, summed), unused = lax.scan(attend_advance, initial, offsets)
    return (summed / totals[..., None], highest + jnp.log(totals))


def attend_block(
    queries,
    grad_out,
    log_rows,
    delta_rows,
    key_block,
    value_block,
    query_pos,
    key_pos,
    lengths,
    factor,
):
    scores = block_scores(queries, key_block, query_pos, key_pos, lengths, factor)
    probs = jnp.exp(scores - log_rows[..., None])
    grad_probs = jnp.einsum(
        "sqhe,skhe->sqhk", grad_out, value_block, preferred_element_type=jnp.float32
    )
    grad_scores = (probs * (grad_probs - delta_rows[..., None])).astype(jnp.bfloat16)
    return (probs.astype(jnp.bfloat16), grad_scores)


def key_sweep(
    queries,
    grad_out,
    log_rows,
    delta_rows,
    key_rows,
    value_rows,
    query_pos,
    lengths,
    key_span,
    factor,
):
    batches, row_count, head_count, head_depth = queries.shape
    length = key_rows.shape[1]

    def key_advance(grad_query, offset):
        key_block = lax.dynamic_slice_in_dim(key_rows, offset, key_span, 1)
        value_block = lax.dynamic_slice_in_dim(value_rows, offset, key_span, 1)
        key_pos = offset + lax.iota(jnp.int32, key_span)
        probs_low, grad_scores = attend_block(
            queries,
            grad_out,
            log_rows,
            delta_rows,
            key_block,
            value_block,
            query_pos,
            key_pos,
            lengths,
            factor,
        )
        grad_query = (
            grad_query
            + jnp.einsum(
                "sqhk,skhe->sqhe", grad_scores, key_block, preferred_element_type=jnp.float32
            )
            * factor
        )
        grad_key = (
            jnp.einsum("sqhk,sqhe->kshe", grad_scores, queries, preferred_element_type=jnp.float32)
            * factor
        )
        grad_value = jnp.einsum(
            "sqhk,sqhe->kshe", probs_low, grad_out, preferred_element_type=jnp.float32
        )
        return (grad_query, (grad_key, grad_value))

    offsets = jnp.arange(length // key_span, dtype=jnp.int32) * key_span
    grad_query, stacked = lax.scan(key_advance, jnp.zeros(queries.shape, jnp.float32), offsets)
    flat_shape = (length, batches, head_count * head_depth)
    return (grad_query, stacked[0].reshape(flat_shape), stacked[1].reshape(flat_shape))


def local(
    tokens,
    timesteps,
    time_table,
    prefix,
    encoder,
    self_qkv,
    cross_q,
    cross_kv,
    self_out,
    cross_out,
    ffn_up,
    ffn_down,
    norm_gain,
    norm_bias,
    cotangent,
):
    proj_self, proj_query, proj_pair, back_self, back_cross, expand_full, shrink_full = (
        lax.all_gather(self_qkv, "fsdp", axis=1, tiled=True),
        lax.all_gather(cross_q, "fsdp", axis=0, tiled=True),
        lax.all_gather(cross_kv, "fsdp", axis=1, tiled=True),
        lax.all_gather(self_out, "fsdp", axis=1, tiled=True),
        lax.all_gather(cross_out, "fsdp", axis=1, tiled=True),
        lax.all_gather(ffn_up, "fsdp", axis=0, tiled=True),
        lax.all_gather(ffn_down, "fsdp", axis=1, tiled=True),
    )
    batches = tokens.shape[0]
    model_width = tokens.shape[2]
    local_width = proj_query.shape[1]
    head_count = local_width // HEAD_DIM
    factor = HEAD_DIM ** (-0.5)
    ctx_index = lax.axis_index("ctx")
    local_stack = jnp.transpose(proj_self, (1, 0, 2)).reshape(model_width, 3 * local_width)
    steps_onehot = (timesteps[:, None] == lax.iota(jnp.int32, time_table.shape[0])[None, :]).astype(
        jnp.bfloat16
    )
    embedded = jnp.dot(steps_onehot, time_table, preferred_element_type=jnp.float32)
    start_sum = tokens.astype(jnp.float32) + embedded[:, None, :]
    normed_one, unit_one, inverse_one = norm_rows(start_sum, norm_gain[0], norm_bias[0])
    rows_self = spread_rows(normed_one.astype(jnp.bfloat16))
    row_count = rows_self.shape[1]
    head_shape = (batches, row_count, head_count, HEAD_DIM)
    projected = jnp.einsum(
        "scd,kdw->kscw", rows_self, proj_self, preferred_element_type=jnp.float32
    ).astype(jnp.bfloat16)
    queries, key_local, value_local = (projected[0], projected[1], projected[2])
    key_all, value_all = (
        lax.all_gather(key_local, "ctx", axis=1, tiled=True),
        lax.all_gather(value_local, "ctx", axis=1, tiled=True),
    )
    length = key_all.shape[1]
    key_span = min(512, length)
    query_pos = ctx_index * row_count + lax.iota(jnp.int32, row_count)
    keys_four = key_all.reshape(batches, length, head_count, HEAD_DIM)
    values_four = value_all.reshape(batches, length, head_count, HEAD_DIM)
    queries_four = queries.reshape(head_shape)
    attended, log_total = attend_forward(
        queries_four, keys_four, values_four, query_pos, prefix, key_span, factor
    )
    context_one = attended.reshape(batches, row_count, local_width).astype(jnp.bfloat16)
    branch_one = finish_branch(context_one, back_self)
    after_one = start_sum + branch_one
    normed_two, unit_two, inverse_two = norm_rows(after_one, norm_gain[1], norm_bias[1])
    rows_cross = spread_rows(normed_two.astype(jnp.bfloat16))
    cross_queries = jnp.einsum(
        "scd,dw->scw", rows_cross, proj_query, preferred_element_type=jnp.float32
    ).astype(jnp.bfloat16)
    enc_pair = jnp.einsum(
        "sed,kdw->ksew", encoder, proj_pair, preferred_element_type=jnp.float32
    ).astype(jnp.bfloat16)
    enc_count = encoder.shape[1]
    cross_keys = enc_pair[0].reshape(batches, enc_count, head_count, HEAD_DIM)
    cross_values = enc_pair[1].reshape(batches, enc_count, head_count, HEAD_DIM)
    cross_four = cross_queries.reshape(head_shape)
    cross_probs = jax.nn.softmax(
        jnp.einsum("sqhe,skhe->sqhk", cross_four, cross_keys, preferred_element_type=jnp.float32)
        * factor,
        axis=-1,
    )
    cross_low = cross_probs.astype(jnp.bfloat16)
    context_two = (
        jnp.einsum("sqhk,skhe->sqhe", cross_low, cross_values, preferred_element_type=jnp.float32)
        .reshape(batches, row_count, local_width)
        .astype(jnp.bfloat16)
    )
    branch_two = finish_branch(context_two, back_cross)
    after_two = after_one + branch_two
    normed_three, unit_three, inverse_three = norm_rows(after_two, norm_gain[2], norm_bias[2])
    rows_ffn = spread_rows(normed_three.astype(jnp.bfloat16))
    pre_act = jnp.einsum("scd,df->scf", rows_ffn, expand_full, preferred_element_type=jnp.float32)
    activated, slopes = gelu_parts(pre_act)
    hidden_low = activated.astype(jnp.bfloat16)
    branch_three = finish_branch(hidden_low, shrink_full)
    final_sum = after_two + branch_three
    grad_three = spread_grads(cotangent)
    grad_shrink = jnp.einsum(
        "scf,scd->fd", hidden_low, grad_three, preferred_element_type=jnp.float32
    )
    grad_pre = (
        jnp.einsum("scd,fd->scf", grad_three, shrink_full, preferred_element_type=jnp.float32)
        * slopes
    ).astype(jnp.bfloat16)
    grad_expand = jnp.einsum("scd,scf->df", rows_ffn, grad_pre, preferred_element_type=jnp.float32)
    back_three, gain_three, shift_three = norm_back(
        finish_grad(grad_pre, expand_full), unit_three, inverse_three, norm_gain[2]
    )
    grad_after_two = cotangent.astype(jnp.float32) + back_three
    grad_two = spread_grads(grad_after_two.astype(jnp.bfloat16))
    grad_back_cross = jnp.einsum(
        "scw,scd->wd", context_two, grad_two, preferred_element_type=jnp.float32
    )
    grad_context_two = jnp.einsum(
        "scd,wd->scw", grad_two, back_cross, preferred_element_type=jnp.float32
    ).astype(jnp.bfloat16)
    grad_cross_four = grad_context_two.reshape(head_shape)
    grad_cross_probs = jnp.einsum(
        "sqhe,skhe->sqhk", grad_cross_four, cross_values, preferred_element_type=jnp.float32
    )
    grad_cross_scores = (
        cross_probs
        * (grad_cross_probs - jnp.sum(cross_probs * grad_cross_probs, -1, keepdims=True))
    ).astype(jnp.bfloat16)
    grad_cross_q = (
        (
            jnp.einsum(
                "sqhk,skhe->sqhe", grad_cross_scores, cross_keys, preferred_element_type=jnp.float32
            )
            * factor
        )
        .reshape(batches, row_count, local_width)
        .astype(jnp.bfloat16)
    )
    part_keys = (
        jnp.einsum(
            "sqhk,sqhe->skhe", grad_cross_scores, cross_four, preferred_element_type=jnp.float32
        )
        * factor
    ).reshape(batches, enc_count, local_width)
    part_values = jnp.einsum(
        "sqhk,sqhe->skhe", cross_low, grad_cross_four, preferred_element_type=jnp.float32
    ).reshape(batches, enc_count, local_width)
    enc_keys, enc_values = (
        lax.psum_scatter(part_keys, "ctx", scatter_dimension=1, tiled=True),
        lax.psum_scatter(part_values, "ctx", scatter_dimension=1, tiled=True),
    )
    enc_keys = enc_keys.astype(jnp.bfloat16)
    enc_values = enc_values.astype(jnp.bfloat16)
    enc_share = enc_keys.shape[1]
    enc_rows = lax.dynamic_slice_in_dim(encoder, ctx_index * enc_share, enc_share, 1)
    grad_pair = jnp.stack(
        [
            jnp.einsum("sed,sew->dw", enc_rows, enc_keys, preferred_element_type=jnp.float32),
            jnp.einsum("sed,sew->dw", enc_rows, enc_values, preferred_element_type=jnp.float32),
        ]
    )
    encoder_grad = lax.psum_scatter(
        jnp.einsum("sew,dw->sed", enc_keys, proj_pair[0], preferred_element_type=jnp.float32)
        + jnp.einsum("sew,dw->sed", enc_values, proj_pair[1], preferred_element_type=jnp.float32),
        "tp",
        scatter_dimension=1,
        tiled=True,
    )
    grad_query_proj = jnp.einsum(
        "scd,scw->dw", rows_cross, grad_cross_q, preferred_element_type=jnp.float32
    )
    back_two, gain_two, shift_two = norm_back(
        finish_grad(grad_cross_q, proj_query), unit_two, inverse_two, norm_gain[1]
    )
    grad_after_one = grad_after_two + back_two
    grad_one = spread_grads(grad_after_one.astype(jnp.bfloat16))
    grad_back_self = jnp.einsum(
        "scw,scd->wd", context_one, grad_one, preferred_element_type=jnp.float32
    )
    grad_context_one = jnp.einsum(
        "scd,wd->scw", grad_one, back_self, preferred_element_type=jnp.float32
    ).astype(jnp.bfloat16)
    grad_ctx_four = grad_context_one.reshape(head_shape)
    delta_rows = jnp.sum(grad_ctx_four.astype(jnp.float32) * attended, -1)
    grad_query, grad_key_all, grad_value_all = key_sweep(
        queries_four,
        grad_ctx_four,
        log_total,
        delta_rows,
        keys_four,
        values_four,
        query_pos,
        prefix,
        key_span,
        factor,
    )
    own_keys, own_values = (
        lax.psum_scatter(grad_key_all, "ctx", scatter_dimension=0, tiled=True),
        lax.psum_scatter(grad_value_all, "ctx", scatter_dimension=0, tiled=True),
    )
    own_keys = jnp.transpose(own_keys, (1, 0, 2))
    own_values = jnp.transpose(own_values, (1, 0, 2))
    grad_joined = jnp.concatenate(
        [grad_query.reshape(batches, row_count, local_width), own_keys, own_values], -1
    ).astype(jnp.bfloat16)
    grad_proj_self = jnp.transpose(
        jnp.einsum(
            "scd,scw->dw", rows_self, grad_joined, preferred_element_type=jnp.float32
        ).reshape(model_width, 3, local_width),
        (1, 0, 2),
    )
    back_one, gain_one, shift_one = norm_back(
        finish_grad(grad_joined, local_stack), unit_one, inverse_one, norm_gain[0]
    )
    input_grad = grad_after_one + back_one
    shard_grads = (
        lax.psum_scatter(grad_proj_self, "fsdp", scatter_dimension=1, tiled=True),
        lax.psum_scatter(grad_query_proj, "fsdp", scatter_dimension=0, tiled=True),
        lax.psum_scatter(grad_pair, "fsdp", scatter_dimension=1, tiled=True),
        lax.psum_scatter(grad_back_self, "fsdp", scatter_dimension=1, tiled=True),
        lax.psum_scatter(grad_back_cross, "fsdp", scatter_dimension=1, tiled=True),
        lax.psum_scatter(grad_expand, "fsdp", scatter_dimension=0, tiled=True),
        lax.psum_scatter(grad_shrink, "fsdp", scatter_dimension=1, tiled=True),
    )
    full_grads = lax.psum(
        (
            shard_grads[0],
            shard_grads[1],
            shard_grads[2],
            shard_grads[3],
            shard_grads[4],
            shard_grads[5],
            shard_grads[6],
        ),
        "ctx",
    )
    squares = jnp.stack(
        [
            jnp.sum(final_sum * final_sum),
            jnp.sum(branch_one * branch_one),
            jnp.sum(branch_two * branch_two),
            jnp.sum(branch_three * branch_three),
        ]
    )
    gain_grad, bias_grad, square_totals = lax.psum(
        (
            jnp.stack([gain_one, gain_two, gain_three]),
            jnp.stack([shift_one, shift_two, shift_three]),
            squares,
        ),
        ("fsdp", "ctx", "tp"),
    )
    entries = (
        tokens.shape[0]
        * tokens.shape[1]
        * tokens.shape[2]
        * lax.axis_size("fsdp")
        * lax.axis_size("ctx")
        * lax.axis_size("tp")
    )
    norms = jnp.sqrt(square_totals / entries)
    return (
        final_sum,
        input_grad,
        encoder_grad,
        full_grads[0],
        full_grads[1],
        full_grads[2],
        full_grads[3],
        full_grads[4],
        full_grads[5],
        full_grads[6],
        gain_grad,
        bias_grad[:2],
        bias_grad[2],
        norms,
    )


def solution(mesh):
    placed = (
        P("fsdp", ("ctx", "tp"), None),
        P("fsdp"),
        P(),
        P("fsdp"),
        P("fsdp", None, None),
        P(None, "fsdp", "tp"),
        P("fsdp", "tp"),
        P(None, "fsdp", "tp"),
        P("tp", "fsdp"),
        P("tp", "fsdp"),
        P("fsdp", "tp"),
        P("tp", "fsdp"),
        P(),
        P(),
        P("fsdp", ("ctx", "tp"), None),
    )
    return jax.shard_map(
        local,
        mesh=mesh,
        in_specs=placed,
        out_specs=(
            P("fsdp", ("ctx", "tp"), None),
            P("fsdp", ("ctx", "tp"), None),
            P("fsdp", ("ctx", "tp"), None),
            P(None, "fsdp", "tp"),
            P("fsdp", "tp"),
            P(None, "fsdp", "tp"),
            P("tp", "fsdp"),
            P("tp", "fsdp"),
            P("fsdp", "tp"),
            P("tp", "fsdp"),
            P(),
            P(),
            P(),
            P(),
        ),
        check_vma=False,
    )
```

profile of v0, /device:TPU:17, one launch (start us, length us, event | category | flops | bytes accessed | tf_op | source)
XLA Modules:
  0.0 2282.3 jit_solution(16497882935876468019)
XLA Ops:
  23.7 72.8 %all-gather.11.cloned.1.call-done = bf16[2,2048,512]{2,1,0:T(8,128)(2,1)} async-done(((bf16[2,512,512]{2,1,0:T(8,128)(2,1)}), bf16[2,2048,512]{2,1,0:T(8,128)(2,1)}) %all-gather.11.cloned.1.call-update) | async-done | bytes 4194320 | tf_op jit(solution)/shard_map/all_gather | solution.py:43
  113.7 13.3 all-gather.23.cloned.1.call-done
  127.0 174.7 %while.30 = (s32[]{:T(128)}, f32[2,2048,2]{1,2,0:T(2,128)S(1)}, f32[2,2048,2]{1,2,0:T(2,128)S(1)}, f32[2,2048,2,64]{1,3,2,0:T(8,128)}, s32[8]{0:T(128)S(1)}, /*i...) while((s32[]{:T(128)}, f32[2,2048,2]{1,2,0:T(2,128)S(1)}, ...), condition=%wide.region_5.6_spmd.clone, body=%wide.region_2.5_spmd.clone.sunk | while | flops 1124642304 | bytes 83910920 | solution.py:108
  309.0 145.8 %reduce-scatter.19.cloned.1.call-done = f32[2,512,512]{2,1,0:T(8,128)} async-done(((f32[2,2048,512]{2,1,0:T(8,128)}), f32[2,512,512]{2,1,0:T(8,128)}) %reduce-scatter.19.cloned.1.call-update) | async-done | bytes 2097168 | tf_op jit(solution)/shard_map/reduce_scatter | solution.py:51
  483.5 56.4 %all-gather.13.cloned.1.call-done = bf16[2,2048,512]{2,1,0:T(8,128)(2,1)} async-done(((bf16[2,512,512]{2,1,0:T(8,128)(2,1)}), bf16[2,2048,512]{2,1,0:T(8,128)(2,1)}) %all-gather.13.cloned.1.call-update) | async-done | bytes 4194320 | tf_op jit(solution)/shard_map/all_gather | solution.py:43
  558.4 145.4 %reduce-scatter.21.cloned.1.call-done = f32[2,512,512]{2,1,0:T(8,128)} async-done(((f32[2,2048,512]{2,1,0:T(8,128)}), f32[2,512,512]{2,1,0:T(8,128)}) %reduce-scatter.21.cloned.1.call-update) | async-done | bytes 2097168 | tf_op jit(solution)/shard_map/reduce_scatter | solution.py:51
  728.2 61.2 %all-gather.15.cloned.1.call-done = bf16[2,2048,512]{2,1,0:T(8,128)(2,1)} async-done(((bf16[2,512,512]{2,1,0:T(8,128)(2,1)}), bf16[2,2048,512]{2,1,0:T(8,128)(2,1)}) %all-gather.15.cloned.1.call-update) | async-done | bytes 4194320 | tf_op jit(solution)/shard_map/all_gather | solution.py:43
  797.1 73.2 %all-gather.17.cloned.1.call-done = bf16[2,2048,512]{2,1,0:T(8,128)(2,1)} async-done(((bf16[2,512,512]{2,1,0:T(8,128)(2,1)}), bf16[2,2048,512]{2,1,0:T(8,128)(2,1)}) %all-gather.17.cloned.1.call-update) | async-done | bytes 4194320 | tf_op jit(solution)/shard_map/all_gather | solution.py:47
  886.0 145.2 %reduce-scatter.25.cloned.1.call-done = f32[2,512,512]{2,1,0:T(8,128)} async-done(((f32[2,2048,512]{2,1,0:T(8,128)}), f32[2,512,512]{2,1,0:T(8,128)}) %reduce-scatter.25.cloned.1.call-update) | async-done | bytes 2097168 | tf_op jit(solution)/shard_map/reduce_scatter | solution.py:60
  1036.9 79.3 %all-gather.19.cloned.1.call-done = bf16[2,2048,512]{2,1,0:T(8,128)(2,1)} async-done(((bf16[2,512,512]{2,1,0:T(8,128)(2,1)}), bf16[2,2048,512]{2,1,0:T(8,128)(2,1)}) %all-gather.19.cloned.1.call-update) | async-done | bytes 4194320 | tf_op jit(solution)/shard_map/all_gather | solution.py:47
  1144.9 137.2 %reduce-scatter.27.cloned.1.call-done = f32[2,512,512]{2,1,0:T(8,128)} async-done(((f32[2,2048,512]{2,1,0:T(8,128)}), f32[2,512,512]{2,1,0:T(8,128)}) %reduce-scatter.27.cloned.1.call-update) | async-done | bytes 2097168 | tf_op jit(solution)/shard_map/reduce_scatter | solution.py:60
  1285.9 143.7 %reduce-scatter.23.cloned.1.call-done = f32[2,512,512]{2,1,0:T(8,128)} async-done(((f32[2,2048,512]{2,1,0:T(8,128)}), f32[2,512,512]{2,1,0:T(8,128)}) %reduce-scatter.23.cloned.1.call-update) | async-done | bytes 2097168 | tf_op jit(solution)/shard_map/reduce_scatter | solution.py:51
  1447.9 68.2 %all-gather.21.cloned.1.call-done = bf16[2,2048,512]{2,1,0:T(8,128)(2,1)} async-done(((bf16[2,512,512]{2,1,0:T(8,128)(2,1)}), bf16[2,2048,512]{2,1,0:T(8,128)(2,1)}) %all-gather.21.cloned.1.call-update) | async-done | bytes 4194320 | tf_op jit(solution)/shard_map/all_gather | solution.py:47
  1521.5 292.8 %while.31 = (s32[]{:T(128)}, f32[2,2048,2,64]{1,3,2,0:T(8,128)}, f32[8,512,2,2,64]{1,4,3,2,0:T(8,128)}, f32[8,512,2,2,64]{1,4,3,2,0:T(8,128)}, s32[8]{0:T(128)S(...) while((s32[]{:T(128)}, f32[2,2048,2,64]{1,3,2,0:T(8,128)}, ...), condition=%wide.region_24.25_spmd.clone, body=%wide.region_23.24_spmd.clone.sunk | while | flops 2731150848 | bytes 182313296 | solution.py:181
  1814.3 12.2 copy.115
  1835.4 12.4 copy.114
  1911.4 20.3 reduce-scatter.53.cloned.1.call-done
  1931.6 26.3 %reduce-scatter.49.cloned.1.call-done = f32[128,128]{1,0:T(8,128)} async-done(((f32[128,512]{1,0:T(8,128)}), f32[128,128]{1,0:T(8,128)}) %reduce-scatter.49.cloned.1.call-update) | async-done | bytes 65552 | tf_op jit(solution)/shard_map/reduce_scatter | solution.py:400
  1957.9 27.1 %reduce-scatter.43.cloned.1.call-done = f32[128,128]{1,0:T(8,128)} async-done(((f32[512,128]{1,0:T(8,128)}), f32[128,128]{1,0:T(8,128)}) %reduce-scatter.43.cloned.1.call-update) | async-done | bytes 65552 | tf_op jit(solution)/shard_map/reduce_scatter | solution.py:397
  1985.0 28.0 %reduce-scatter.45.cloned.1.call-done = f32[2,128,128]{2,1,0:T(8,128)} async-done(((f32[2,512,128]{2,1,0:T(8,128)}), f32[2,128,128]{2,1,0:T(8,128)}) %reduce-scatter.45.cloned.1.call-update) | async-done | bytes 131088 | tf_op jit(solution)/shard_map/reduce_scatter | solution.py:398
  2013.0 27.3 %reduce-scatter.47.cloned.1.call-done = f32[128,128]{1,0:T(8,128)} async-done(((f32[128,512]{1,0:T(8,128)}), f32[128,128]{1,0:T(8,128)}) %reduce-scatter.47.cloned.1.call-update) | async-done | bytes 65552 | tf_op jit(solution)/shard_map/reduce_scatter | solution.py:399
  2040.2 29.3 %reduce-scatter.41.cloned.1.call-done = f32[3,128,128]{2,1,0:T(8,128)} async-done(((f32[3,512,128]{2,1,0:T(8,128)}), f32[3,128,128]{2,1,0:T(8,128)}) %reduce-scatter.41.cloned.1.call-update) | async-done | bytes 196624 | tf_op jit(solution)/shard_map/reduce_scatter | solution.py:396
  2069.6 147.6 %reduce-scatter.33.cloned.1.call-done = f32[2,512,512]{2,1,0:T(8,128)} async-done(((f32[2,2048,512]{2,1,0:T(8,128)}), f32[2,512,512]{2,1,0:T(8,128)}) %reduce-scatter.33.cloned.1.call-update) | async-done | bytes 2097168 | tf_op jit(solution)/shard_map/reduce_scatter | solution.py:60
  2220.1 38.8 %all-reduce = (f32[3,512]{1,0:T(4,128)}, f32[3,512]{1,0:T(4,128)S(1)}, f32[4]{0:T(128)S(1)}) all-reduce(f32[3,512]{1,0:T(4,128)S(1)} %pad_maximum_fusion.4, f32[3,512]{1,0:T(4,128)S(1)} %pad_maximum_fusion.5, f32[4]{0:T(128)S(1)} %pad_maximum_fusion.6), channel_id=1, replica_groups=mesh['fsdp'=4,'ctx'=2,'tp'=4] {'fsdp','ctx','tp'}, use_global_device_ids=true, to_apply=%region_50.51 | all-reduce | flops 3076 | bytes 24608 | tf_op jit(solution)/shard_map/psum | solution.py:424
  (548 shorter events, 722.9 us)
Async XLA Ops:
  7.2 89.2 %all-gather.11.cloned.1.call-start = ((), (), s32[]{:S(2)}) async-start(), calls=%async_computation.18 | async-start | bytes 5242880 | tf_op jit(solution)/shard_map/all_gather | solution.py:43
  15.9 97.7 %all-gather.25.cloned.1.call-start = ((), (), s32[]{:S(2)}) async-start(), calls=%async_computation.43 | async-start | bytes 3145728 | tf_op jit(solution)/shard_map/all_gather | solution.py:234
  102.9 351.9 %reduce-scatter.19.cloned.1.call-start = ((), (), s32[]{:S(2)}) async-start(), calls=%async_computation.19 | async-start | bytes 10485760 | tf_op jit(solution)/shard_map/reduce_scatter | solution.py:51
  309.0 230.8 %all-gather.13.cloned.1.call-start = ((), (), s32[]{:S(2)}) async-start(), calls=%async_computation.20 | async-start | bytes 5242880 | tf_op jit(solution)/shard_map/all_gather | solution.py:43
  460.5 243.3 %reduce-scatter.21.cloned.1.call-start = ((), (), s32[]{:S(2)}) async-start(), calls=%async_computation.21 | async-start | bytes 10485760 | tf_op jit(solution)/shard_map/reduce_scatter | solution.py:51
  558.3 231.1 %all-gather.15.cloned.1.call-start = ((), (), s32[]{:S(2)}) async-start(), calls=%async_computation.22 | async-start | bytes 5242880 | tf_op jit(solution)/shard_map/all_gather | solution.py:43
  710.0 160.3 %all-gather.17.cloned.1.call-start = ((), (), s32[]{:S(2)}) async-start(), calls=%async_computation.24 | async-start | bytes 5242880 | tf_op jit(solution)/shard_map/all_gather | solution.py:47
  710.8 320.4 %reduce-scatter.25.cloned.1.call-start = ((), (), s32[]{:S(2)}) async-start(), calls=%async_computation.25 | async-start | bytes 10485760 | tf_op jit(solution)/shard_map/reduce_scatter | solution.py:60
  885.7 230.5 %all-gather.19.cloned.1.call-start = ((), (), s32[]{:S(2)}) async-start(), calls=%async_computation.26 | async-start | bytes 5242880 | tf_op jit(solution)/shard_map/all_gather | solution.py:47
  1036.9 245.2 %reduce-scatter.27.cloned.1.call-start = ((), (), s32[]{:S(2)}) async-start(), calls=%async_computation.27 | async-start | bytes 10485760 | tf_op jit(solution)/shard_map/reduce_scatter | solution.py:60
  1136.7 292.9 %reduce-scatter.23.cloned.1.call-start = ((), (), s32[]{:S(2)}) async-start(), calls=%async_computation.23 | async-start | bytes 10485760 | tf_op jit(solution)/shard_map/reduce_scatter | solution.py:51
  1144.9 371.3 %all-gather.21.cloned.1.call-start = ((), (), s32[]{:S(2)}) async-start(), calls=%async_computation.28 | async-start | bytes 5242880 | tf_op jit(solution)/shard_map/all_gather | solution.py:47
  1436.8 443.1 %reduce-scatter.37.cloned.1.call-start = ((), (), s32[]{:S(2)}) async-start(), calls=%async_computation.33 | async-start | bytes 393216 | tf_op jit(solution)/shard_map/reduce_scatter | solution.py:329
  1442.9 438.1 %reduce-scatter.35.cloned.1.call-start = ((), (), s32[]{:S(2)}) async-start(), calls=%async_computation.32 | async-start | bytes 393216 | tf_op jit(solution)/shard_map/reduce_scatter | solution.py:328
  1447.8 442.4 %reduce-scatter.31.cloned.1.call-start = ((), (), s32[]{:S(2)}) async-start(), calls=%async_computation.30 | async-start | bytes 6291456 | tf_op jit(solution)/shard_map/reduce_scatter | solution.py:378
  1863.6 68.0 %reduce-scatter.53.cloned.1.call-start = ((), (), s32[]{:S(2)}) async-start(), calls=%async_computation.41 | async-start | bytes 1310720 | tf_op jit(solution)/shard_map/reduce_scatter | solution.py:402
  1871.7 86.2 %reduce-scatter.49.cloned.1.call-start = ((), (), s32[]{:S(2)}) async-start(), calls=%async_computation.39 | async-start | bytes 327680 | tf_op jit(solution)/shard_map/reduce_scatter | solution.py:400
  1875.5 109.5 %reduce-scatter.43.cloned.1.call-start = ((), (), s32[]{:S(2)}) async-start(), calls=%async_computation.36 | async-start | bytes 327680 | tf_op jit(solution)/shard_map/reduce_scatter | solution.py:397
  1879.8 133.2 %reduce-scatter.45.cloned.1.call-start = ((), (), s32[]{:S(2)}) async-start(), calls=%async_computation.37 | async-start | bytes 655360 | tf_op jit(solution)/shard_map/reduce_scatter | solution.py:398
  1883.1 157.2 %reduce-scatter.47.cloned.1.call-start = ((), (), s32[]{:S(2)}) async-start(), calls=%async_computation.38 | async-start | bytes 327680 | tf_op jit(solution)/shard_map/reduce_scatter | solution.py:399
  1890.0 179.6 %reduce-scatter.41.cloned.1.call-start = ((), (), s32[]{:S(2)}) async-start(), calls=%async_computation.35 | async-start | bytes 983040 | tf_op jit(solution)/shard_map/reduce_scatter | solution.py:396
  1899.4 317.8 %reduce-scatter.33.cloned.1.call-start = ((), (), s32[]{:S(2)}) async-start(), calls=%async_computation.31 | async-start | bytes 10485760 | tf_op jit(solution)/shard_map/reduce_scatter | solution.py:60
  1906.5 357.8 %reduce-scatter.39.cloned.1.call-start = ((), (), s32[]{:S(2)}) async-start(), calls=%async_computation.34 | async-start | bytes 655360 | tf_op jit(solution)/shard_map/reduce_scatter | solution.py:341
  1908.7 355.6 %all-reduce.4.cloned.1.call-start = ((), (), s32[]{:S(2)}) async-start(), calls=%async_computation.44 | async-start | bytes 2097152 | tf_op jit(solution)/shard_map/psum | solution.py:404
  (102 other events, 4883.5 us)
Sparse Core Ops, SparseCore 0:
  16.1 80.3 all-gather.10
  115.2 11.7 all-gather.22
  309.1 145.6 reduce-scatter.18
  460.6 79.1 all-gather.12
  558.4 145.2 reduce-scatter.20
  710.1 79.1 all-gather.14
  791.0 79.2 all-gather.16
  885.9 145.2 reduce-scatter.24
  1037.0 79.1 all-gather.18
  1136.8 145.2 reduce-scatter.26
  1284.3 145.1 reduce-scatter.22
  1436.9 79.1 all-gather.20
  1835.5 12.7 reduce-scatter.30
  1856.9 12.7 reduce-scatter.28
  1872.5 28.2 reduce-scatter.50
  1903.9 27.7 reduce-scatter.52
  1934.2 23.6 reduce-scatter.48
  1960.9 24.0 reduce-scatter.42
  1987.8 25.1 reduce-scatter.44
  2016.5 23.6 reduce-scatter.46
  2043.0 26.5 reduce-scatter.40
  2071.9 145.2 reduce-scatter.32
  2219.9 18.3 reduce-scatter.38
  2241.0 22.3 all-reduce.3
  (3 shorter events, 28.4 us)
where the time goes:
time: 2290 us; the launch traced here: 2280 us
  waiting for transfers between devices  1450 us (63%)
  matrix products  421 us (18%)
  local copies, waits for them, and re-layouts  140 us (6%)
  other arithmetic  126 us (6%)
  blocking collectives  91.3 us (4%)
  loops' own time  33.1 us (1%)
    reduce_scatter x3, waiting for transfers between devices, finish_branch(): lax.psum_scatter(jnp.einsum('scw,wd->scd', local_in, local_weight, prefer...  435 us
    reduce_scatter x3, waiting for transfers between devices, finish_grad(): lax.psum_scatter(jnp.einsum('scw,dw->scd', local_grad, local_weight, pref...  430 us
    all_gather x3, waiting for transfers between devices, spread_grads(): return lax.all_gather(grad_rows, 'tp', axis=1, tiled=True)  221 us
    all_gather x3, waiting for transfers between devices, spread_rows(): return lax.all_gather(rows, 'tp', axis=1, tiled=True)  190 us
    dot_general x8, matrix products, attend_block(): jnp.einsum('sqhe,skhe->sqhk', grad_out, value_block, preferred_element_ty...  79.6 us
    dot_general x16, matrix products, block_scores(): jnp.einsum('sqhe,skhe->sqhk', queries, key_block, preferred_element_type=...  67.6 us
    while x104, local copies, waits for them, and re-layouts  56.5 us
    dot_general x8, matrix products, attend_advance(): jnp.einsum('sqhk,skhe->sqhe', weights.astype(jnp.bfloat16), value_block,...  50.7 us
  transfers between devices with their start and end apart: 27, of which 20 were waited for; matrix products, arithmetic and copies ran while one was open for 16% of the time, Pallas kernels for 0%

commit v1 on v0

--- a/solution.py
+++ b/solution.py
@@ -1,8 +1,11 @@
+import functools
 import math
 
 import jax
 import jax.numpy as jnp
 from jax import lax
+from jax.experimental import pallas as pl
+from jax.experimental.pallas import tpu as pltpu
 from jax.sharding import PartitionSpec as P
 
 HEAD_DIM = 64
@@ -12,6 +15,7 @@
 NEG = -1e30
 ROOT_HALF = 1.0 / math.sqrt(2.0)
 INV_ROOT_TWO_PI = 1.0 / math.sqrt(2.0 * math.pi)
+VMEM_LIMIT = 56 * 2**20
 
 
 def norm_rows(hidden, scaling, offsets):
@@ -456,6 +460,579 @@
     )
 
 
+def dot_of(left, right, left_dim, right_dim):
+    return lax.dot_general(
+        left, right, (((left_dim,), (right_dim,)), ((), ())), preferred_element_type=jnp.float32
+    )
+
+
+def bounds(prefix, start, query_span, key_span):
+    whole = jnp.maximum(prefix, start + 1) // key_span
+    every = (jnp.maximum(prefix, start + query_span) + key_span - 1) // key_span
+    return whole, every
+
+
+def hide(scores, limit, offset):
+    return jnp.where(lax.broadcasted_iota(jnp.int32, scores.shape, 0) < limit - offset, scores, NEG)
+
+
+def forward_kernel(scalars, weight_ref, *refs, span, chunk, slots, group):
+    chunk_refs, refs = refs[:slots], refs[slots:]
+    qkv_ref, wide_ref, log_ref = refs[:3]
+    out_refs, refs = refs[3 : 3 + group], refs[3 + group :]
+    queries_ref, keys_ref, values_ref, low_ref = refs
+    step = pl.program_id(0)
+    prefix, me = scalars[0], scalars[1]
+    factor = HEAD_DIM**-0.5
+
+    @pl.when(step == 0)
+    def project():
+        values_ref[HEAD_DIM:, :] = jnp.ones_like(values_ref[HEAD_DIM:, :])
+        for slot in range(slots):
+            place = scalars[2 + slot]
+
+            @pl.when(place >= 0)
+            def one_chunk(slot=slot, place=place):
+                rows = chunk_refs[slot][...]
+                joined = dot_of(weight_ref[...], rows, 1, 1).astype(jnp.bfloat16)
+                here = pl.ds(pl.multiple_of(place * chunk, chunk), chunk)
+                scaled = joined[:HEAD_DIM, :] * jnp.bfloat16(factor)
+                queries_ref[:, here] = scaled
+                values_ref[:HEAD_DIM, here] = joined[2 * HEAD_DIM :, :]
+                keys_ref[here, :] = dot_of(
+                    rows, weight_ref[HEAD_DIM : 2 * HEAD_DIM, :], 1, 1
+                ).astype(jnp.bfloat16)
+                qkv_ref[:HEAD_DIM, here] = scaled
+                qkv_ref[HEAD_DIM:, here] = joined[HEAD_DIM:, :]
+
+    start = pl.multiple_of(step * span, span)
+    queries = queries_ref[:, pl.ds(start, span)]
+    limit = jnp.maximum(prefix, start + 1 + lax.broadcasted_iota(jnp.int32, (1, span), 1))
+    whole, every = bounds(prefix, start, span, span)
+
+    def advance(block, carry, masked):
+        highest, total = carry
+        offset = pl.multiple_of(block * span, span)
+        scores = dot_of(keys_ref[pl.ds(offset, span), :], queries, 1, 0)
+        if masked:
+            scores = hide(scores, limit, offset)
+        higher = jnp.maximum(highest, jnp.max(scores, axis=0, keepdims=True))
+        weights = jnp.exp(scores - higher).astype(jnp.bfloat16)
+        fading = jnp.exp(highest - higher)
+        total = total * fading + dot_of(values_ref[:, pl.ds(offset, span)], weights, 1, 0)
+        return higher, total
+
+    carry = (
+        jnp.full((1, span), NEG, jnp.float32),
+        jnp.zeros((values_ref.shape[0], span), jnp.float32),
+    )
+    carry = lax.fori_loop(0, whole, lambda j, c: advance(j, c, False), carry)
+    highest, total = lax.fori_loop(whole, every, lambda j, c: advance(j, c, True), carry)
+    weight_sum = total[HEAD_DIM : HEAD_DIM + 1, :]
+    attended = total[:HEAD_DIM, :] / weight_sum
+    wide_ref[...] = attended
+    log_ref[...] = highest + jnp.log(weight_sum)
+    low = attended.astype(jnp.bfloat16)
+    for part in range(span // chunk):
+        low_ref[(step * (span // chunk) + part) ^ me] = low[:, part * chunk : (part + 1) * chunk]
+
+    @pl.when(step == pl.num_programs(0) - 1)
+    def finish():
+        for slot in range(group):
+            out_refs[slot][...] = low_ref[slot]
+
+
+def forward_attention(scalars, weight, chunks, length, span, group):
+    slots = len(chunks)
+    chunk = chunks[0].shape[0]
+    whole = lambda *shape: pl.BlockSpec(shape, lambda i, s: (0,) * len(shape))
+    bf16, f32 = jnp.bfloat16, jnp.float32
+    struct = jax.ShapeDtypeStruct
+    outs = pl.pallas_call(
+        functools.partial(forward_kernel, span=span, chunk=chunk, slots=slots, group=group),
+        grid_spec=pltpu.PrefetchScalarGridSpec(
+            num_scalar_prefetch=1,
+            grid=(length // span,),
+            in_specs=[whole(*weight.shape)] + [whole(*c.shape) for c in chunks],
+            out_specs=[
+                whole(3 * HEAD_DIM, length),
+                pl.BlockSpec((HEAD_DIM, span), lambda i, s: (0, i)),
+                pl.BlockSpec((1, span), lambda i, s: (0, i)),
+            ]
+            + [whole(HEAD_DIM, chunk)] * group,
+            scratch_shapes=[
+                pltpu.VMEM((HEAD_DIM, length), bf16),
+                pltpu.VMEM((length, HEAD_DIM), bf16),
+                pltpu.VMEM((HEAD_DIM + 16, length), bf16),
+                pltpu.VMEM((group, HEAD_DIM, chunk), bf16),
+            ],
+        ),
+        out_shape=[
+            struct((3 * HEAD_DIM, length), bf16),
+            struct((HEAD_DIM, length), f32),
+            struct((1, length), f32),
+        ]
+        + [struct((HEAD_DIM, chunk), bf16)] * group,
+        compiler_params=pltpu.CompilerParams(vmem_limit_bytes=VMEM_LIMIT),
+        cost_estimate=pl.CostEstimate(
+            flops=20_000_000_000, bytes_accessed=10_000_000, transcendentals=10_000_000
+        ),
+        name="attention_forward",
+    )(scalars, weight, *chunks)
+    return outs[0], outs[1], outs[2], outs[3:]
+
+
+def backward_kernel(scalars, qkv_ref, wide_ref, log_ref, *refs, span, chunk, group):
+    grad_refs, refs = refs[:group], refs[group:]
+    out_refs, refs = refs[:group], refs[group:]
+    (
+        queries_ref,
+        keys_ref,
+        values_ref,
+        gradt_ref,
+        grad_ref,
+        delta_ref,
+        grad_keys_ref,
+        grad_values_ref,
+        low_ref,
+    ) = refs
+    step = pl.program_id(0)
+    prefix, me = scalars[0], scalars[1]
+    factor = HEAD_DIM**-0.5
+    length = qkv_ref.shape[1]
+
+    @pl.when(step == 0)
+    def prepare():
+        for slot in range(group):
+            here = pl.ds(pl.multiple_of((me ^ slot) * chunk, chunk), chunk)
+            gradt_ref[:, here] = grad_refs[slot][...]
+            grad_ref[here, :] = grad_refs[slot][...].T
+        delta_ref[...] = jnp.sum(
+            gradt_ref[...].astype(jnp.float32) * wide_ref[...], axis=0, keepdims=True
+        )
+        queries_ref[...] = qkv_ref[:HEAD_DIM, :].T
+        keys_ref[...] = qkv_ref[HEAD_DIM : 2 * HEAD_DIM, :].T
+        values_ref[...] = qkv_ref[2 * HEAD_DIM :, :].T
+        grad_keys_ref[...] = jnp.zeros_like(grad_keys_ref)
+        grad_values_ref[...] = jnp.zeros_like(grad_values_ref)
+
+    start = pl.multiple_of(step * span, span)
+    here = pl.ds(start, span)
+    queries_t, queries = qkv_ref[:HEAD_DIM, here], queries_ref[here, :]
+    grads_t, grads = gradt_ref[:, here], grad_ref[here, :]
+    logs, deltas = log_ref[:, here], delta_ref[:, here]
+    limit = jnp.maximum(prefix, start + 1 + lax.broadcasted_iota(jnp.int32, (1, span), 1))
+    whole, every = bounds(prefix, start, span, span)
+
+    def advance(block, grad_queries, masked):
+        there = pl.ds(pl.multiple_of(block * span, span), span)
+        scores = dot_of(keys_ref[there, :], queries_t, 1, 0)
+        if masked:
+            scores = hide(scores, limit, block * span)
+        probs = jnp.exp(scores - logs)
+        grad_probs = dot_of(values_ref[there, :], grads_t, 1, 0)
+        grad_scores = (probs * (grad_probs - deltas)).astype(jnp.bfloat16)
+        grad_values_ref[there, :] += dot_of(probs.astype(jnp.bfloat16), grads, 1, 0)
+        grad_keys_ref[there, :] += dot_of(grad_scores, queries, 1, 0)
+        return grad_queries + dot_of(
+            qkv_ref[HEAD_DIM : 2 * HEAD_DIM, there], grad_scores, 1, 0
+        )
+
+    grad_queries = jnp.zeros((HEAD_DIM, span), jnp.float32)
+    grad_queries = lax.fori_loop(0, whole, lambda j, c: advance(j, c, False), grad_queries)
+    grad_queries = lax.fori_loop(whole, every, lambda j, c: advance(j, c, True), grad_queries)
+    low = (grad_queries * factor).astype(jnp.bfloat16)
+    for part in range(span // chunk):
+        low_ref[(step * (span // chunk) + part) ^ me, :HEAD_DIM, :] = low[
+            :, part * chunk : (part + 1) * chunk
+        ]
+
+    @pl.when(step == pl.num_programs(0) - 1)
+    def finish():
+        for place in range(length // chunk):
+            rows = pl.ds(place * chunk, chunk)
+            low_ref[place ^ me, HEAD_DIM : 2 * HEAD_DIM, :] = grad_keys_ref[rows, :].T.astype(
+                jnp.bfloat16
+            )
+            low_ref[place ^ me, 2 * HEAD_DIM :, :] = grad_values_ref[rows, :].T.astype(jnp.bfloat16)
+        for slot in range(group):
+            out_refs[slot][...] = low_ref[slot]
+
+
+def backward_attention(scalars, qkv, wide, logs, grads, span):
+    group = len(grads)
+    length = qkv.shape[1]
+    chunk = grads[0].shape[1]
+    whole = lambda *shape: pl.BlockSpec(shape, lambda i, s: (0,) * len(shape))
+    bf16, f32 = jnp.bfloat16, jnp.float32
+    return pl.pallas_call(
+        functools.partial(backward_kernel, span=span, chunk=chunk, group=group),
+        grid_spec=pltpu.PrefetchScalarGridSpec(
+            num_scalar_prefetch=1,
+            grid=(length // span,),
+            in_specs=[whole(*qkv.shape), whole(*wide.shape), whole(*logs.shape)]
+            + [whole(*g.shape) for g in grads],
+            out_specs=[whole(3 * HEAD_DIM, chunk)] * group,
+            scratch_shapes=[
+                pltpu.VMEM((length, HEAD_DIM), bf16),
+                pltpu.VMEM((length, HEAD_DIM), bf16),
+                pltpu.VMEM((length, HEAD_DIM), bf16),
+                pltpu.VMEM((HEAD_DIM, length), bf16),
+                pltpu.VMEM((length, HEAD_DIM), bf16),
+                pltpu.VMEM((1, length), f32),
+                pltpu.VMEM((length, HEAD_DIM), f32),
+                pltpu.VMEM((length, HEAD_DIM), f32),
+                pltpu.VMEM((group, 3 * HEAD_DIM, chunk), bf16),
+            ],
+        ),
+        out_shape=[jax.ShapeDtypeStruct((3 * HEAD_DIM, chunk), bf16)] * group,
+        compiler_params=pltpu.CompilerParams(vmem_limit_bytes=VMEM_LIMIT),
+        cost_estimate=pl.CostEstimate(
+            flops=40_000_000_000, bytes_accessed=10_000_000, transcendentals=10_000_000
+        ),
+        name="attention_backward",
+    )(scalars, qkv, wide, logs, *grads)
+
+
+def swap_cores(value):
+    return lax.ppermute(value, "ctx", [(0, 1), (1, 0)])
+
+
+def trade(parts):
+    group = len(parts)
+    return [parts[0]] + [
+        lax.ppermute(parts[k], ("ctx", "tp"), [(i, i ^ k) for i in range(group)])
+        for k in range(1, group)
+    ]
+
+
+def gather_rows(rows):
+    up = lax.ppermute(rows, "tp", [(0, 1), (1, 2), (2, 3)])
+    down = lax.ppermute(rows, "tp", [(1, 0), (2, 1), (3, 2)])
+    up_two = lax.ppermute(up, "tp", [(1, 2), (2, 3)])
+    down_two = lax.ppermute(down, "tp", [(2, 1), (1, 0)])
+    far = lax.ppermute(rows, "tp", [(0, 3), (3, 0)])
+    mine = [rows, up, down, up_two, down_two, far]
+    return mine + [swap_cores(piece) for piece in mine]
+
+
+def slot_places(ctx_index, tp_index):
+    offsets = [0, -1, 1, -2, 2]
+    places = []
+    for core in (ctx_index, 1 - ctx_index):
+        for offset in offsets:
+            chip = tp_index + offset
+            places.append(jnp.where((chip >= 0) & (chip < 4), core * 4 + chip, -1))
+        places.append(jnp.where((tp_index == 0) | (tp_index == 3), core * 4 + 3 - tp_index, -1))
+    return places
+
+
+def norm_back_rows(upstream, unit_rows, inverse, scaling):
+    scaled = upstream * scaling
+    result = inverse * (
+        scaled
+        - jnp.mean(scaled, -1, keepdims=True)
+        - unit_rows * jnp.mean(scaled * unit_rows, -1, keepdims=True)
+    )
+    return result, jnp.sum(upstream * unit_rows, 0), jnp.sum(upstream, 0)
+
+
+def low(value):
+    return value.astype(jnp.bfloat16)
+
+
+def head_parts(value):
+    return value.reshape(value.shape[0], -1, HEAD_DIM)
+
+
+def local_heads(
+    tokens,
+    timesteps,
+    time_table,
+    prefix,
+    encoder,
+    self_qkv,
+    cross_q,
+    cross_kv,
+    self_out,
+    cross_out,
+    ffn_up,
+    ffn_down,
+    norm_gain,
+    norm_bias,
+    cotangent,
+):
+    batches, chunk, width = tokens.shape
+    group = 8
+    length = group * chunk
+    enc_count = encoder.shape[1]
+    factor = HEAD_DIM ** (-0.5)
+    ctx_index, tp_index = lax.axis_index("ctx"), lax.axis_index("tp")
+    me = ctx_index * 4 + tp_index
+    span = 1024
+    piece = width // 4
+    blocks = jnp.concatenate(
+        [
+            self_qkv,
+            cross_q[None],
+            cross_kv,
+            self_out[None],
+            cross_out[None],
+            jnp.transpose(ffn_up.reshape(piece, 4, piece), (1, 0, 2)),
+            ffn_down.reshape(4, piece, piece),
+        ]
+    )
+    count = blocks.shape[0]
+    half = piece // 2
+    own_half = lax.dynamic_slice_in_dim(blocks, ctx_index * half, half, 1)
+    gathered = lax.all_gather(own_half, ("fsdp", "tp"), axis=0, tiled=False)
+    mine = lax.dynamic_slice_in_dim(self_qkv, ctx_index * HEAD_DIM, HEAD_DIM, 2)
+    mine = jnp.transpose(mine, (0, 2, 1)).reshape(3 * HEAD_DIM, piece)
+    columns = [mine] + [
+        lax.ppermute(mine, "fsdp", [(i, i ^ k) for i in range(4)]) for k in range(1, 4)
+    ]
+    fsdp_index = lax.axis_index("fsdp")
+    columns = jnp.stack(columns)
+    head_weight = jnp.concatenate(
+        [lax.dynamic_index_in_dim(columns, fsdp_index ^ f, 0, False) for f in range(4)], 1
+    )
+    steps_onehot = (timesteps[:, None] == lax.iota(jnp.int32, time_table.shape[0])[None, :]).astype(
+        jnp.bfloat16
+    )
+    embedded = jnp.dot(steps_onehot, time_table, preferred_element_type=jnp.float32)
+    places = slot_places(ctx_index, tp_index)
+    start_sums, units_one, kept, arrived = [], [], [], []
+    for s in range(batches):
+        start_sum = tokens[s].astype(jnp.float32) + embedded[s][None, :]
+        normed, unit, inverse = norm_rows(start_sum, norm_gain[0], norm_bias[0])
+        start_sums.append(start_sum)
+        units_one.append((unit, inverse))
+        chunks = gather_rows(low(normed))
+        scalars = jnp.stack([prefix[s], me] + places).astype(jnp.int32)
+        qkv, wide, logs, outs = forward_attention(
+            scalars, head_weight, chunks, length, span, group
+        )
+        kept.append((chunks, scalars, qkv, wide, logs))
+        arrived.append(trade(outs))
+    other = swap_cores(gathered)
+    first = jnp.where(ctx_index == 0, gathered, other)
+    second = jnp.where(ctx_index == 0, other, gathered)
+    whole = jnp.concatenate([first, second], 2).reshape(4, 4, count, piece, piece)
+    square = lambda b: jnp.transpose(whole[:, :, b], (0, 2, 1, 3)).reshape(width, width)
+    flipped = lambda b: jnp.transpose(whole[:, :, b], (1, 2, 0, 3)).reshape(width, width)
+    full_qkv = [square(b) for b in range(3)]
+    full_q, full_k, full_v = square(3), square(4), square(5)
+    full_out, full_cross = flipped(6), flipped(7)
+    full_up = jnp.transpose(whole[:, :, 8:12], (0, 3, 1, 2, 4)).reshape(width, 4 * width)
+    full_down = jnp.transpose(whole[:, :, 12:16], (1, 2, 3, 0, 4)).reshape(4 * width, width)
+    slot_heads = [((me ^ k) % 4) * 2 + (me ^ k) // 4 for k in range(group)]
+    out_heads = full_out.reshape(group, HEAD_DIM, width)
+    out_slots = jnp.concatenate(
+        [lax.dynamic_index_in_dim(out_heads, h, 0, False) for h in slot_heads]
+    )
+    qkv_heads = jnp.stack(full_qkv).reshape(3, width, group, HEAD_DIM)
+    qkv_heads = jnp.transpose(qkv_heads, (2, 0, 3, 1))
+    qkv_slots = jnp.concatenate(
+        [lax.dynamic_index_in_dim(qkv_heads, h, 0, False) for h in slot_heads]
+    ).reshape(group * 3 * HEAD_DIM, width)
+
+    results, sums, returns, early = [], [], [], []
+    for s in range(batches):
+        context_t = jnp.concatenate(arrived[s])
+        branch_one = dot_of(context_t, out_slots, 0, 0)
+        after_one = start_sums[s] + branch_one
+        normed_two, unit_two, inverse_two = norm_rows(after_one, norm_gain[1], norm_bias[1])
+        normed_two = low(normed_two)
+        cross_queries = low(dot_of(normed_two, full_q, 1, 0))
+        cross_keys = low(dot_of(encoder[s], full_k, 1, 0))
+        cross_values = low(dot_of(encoder[s], full_v, 1, 0))
+        queries, keys, values = (
+            head_parts(cross_queries),
+            head_parts(cross_keys),
+            head_parts(cross_values),
+        )
+        probs = jax.nn.softmax(
+            jnp.einsum("qhe,khe->hqk", queries, keys, preferred_element_type=jnp.float32) * factor,
+            axis=-1,
+        )
+        probs_low = low(probs)
+        context_two = low(
+            jnp.einsum("hqk,khe->qhe", probs_low, values, preferred_element_type=jnp.float32)
+        ).reshape(chunk, width)
+        branch_two = dot_of(context_two, full_cross, 1, 0)
+        after_two = after_one + branch_two
+        normed_three, unit_three, inverse_three = norm_rows(after_two, norm_gain[2], norm_bias[2])
+        normed_three = low(normed_three)
+        activated, slopes = gelu_parts(dot_of(normed_three, full_up, 1, 0))
+        hidden = low(activated)
+        branch_three = dot_of(hidden, full_down, 1, 0)
+        final_sum = after_two + branch_three
+        squares = jnp.stack(
+            [jnp.sum(v * v) for v in (final_sum, branch_one, branch_two, branch_three)]
+        )
+        grad_three = cotangent[s]
+        grad_pre = low(dot_of(grad_three, full_down, 1, 1) * slopes)
+        back_three, gain_three, shift_three = norm_back_rows(
+            dot_of(grad_pre, full_up, 1, 1), unit_three, inverse_three, norm_gain[2]
+        )
+        grad_after_two = grad_three.astype(jnp.float32) + back_three
+        grad_two = low(grad_after_two)
+        grad_context = low(dot_of(grad_two, full_cross, 1, 1))
+        grad_heads = head_parts(grad_context)
+        grad_probs = jnp.einsum(
+            "qhe,khe->hqk", grad_heads, values, preferred_element_type=jnp.float32
+        )
+        grad_scores = low(
+            probs * (grad_probs - jnp.sum(probs * grad_probs, -1, keepdims=True))
+        )
+        grad_cross_q = low(
+            jnp.einsum("hqk,khe->qhe", grad_scores, keys, preferred_element_type=jnp.float32)
+            * factor
+        ).reshape(chunk, width)
+        part_keys = (
+            jnp.einsum("hqk,qhe->khe", grad_scores, queries, preferred_element_type=jnp.float32)
+            * factor
+        ).reshape(enc_count, width)
+        part_values = jnp.einsum(
+            "hqk,qhe->khe", probs_low, grad_heads, preferred_element_type=jnp.float32
+        ).reshape(enc_count, width)
+        back_two, gain_two, shift_two = norm_back_rows(
+            dot_of(grad_cross_q, full_q, 1, 1), unit_two, inverse_two, norm_gain[1]
+        )
+        grad_after_one = grad_after_two + back_two
+        grad_one = low(grad_after_one)
+        grad_context_t = low(dot_of(out_slots, grad_one, 1, 1))
+        returns.append(
+            trade([grad_context_t[k * HEAD_DIM : (k + 1) * HEAD_DIM] for k in range(group)])
+        )
+        results.append((final_sum, grad_after_one))
+        sums.append((squares, gain_two, shift_two, gain_three, shift_three))
+        early.append(
+            (
+                dot_of(normed_two, grad_cross_q, 0, 0),
+                dot_of(context_t, grad_one, 1, 0),
+                dot_of(context_two, grad_two, 0, 0),
+                dot_of(normed_three, grad_pre, 0, 0),
+                dot_of(hidden, grad_three, 0, 0),
+                low(jnp.concatenate([part_keys, part_values], 1)),
+            )
+        )
+    share = enc_count // group
+    parts = jnp.stack([e[5] for e in early]).reshape(batches, group, share, 2 * width)
+    parts = [lax.dynamic_index_in_dim(parts, me ^ k, 1, False) for k in range(group)]
+    enc_grads = low(sum(p.astype(jnp.float32) for p in trade(parts)))
+    enc_rows = lax.dynamic_slice_in_dim(encoder, me * share, share, 1)
+    enc_rows = enc_rows.reshape(batches * share, width)
+    enc_flat = enc_grads.reshape(batches * share, 2 * width)
+    encoder_grad = (
+        dot_of(enc_flat[:, :width], full_k, 1, 1) + dot_of(enc_flat[:, width:], full_v, 1, 1)
+    ).reshape(batches, share, width)
+    grad_pair = dot_of(enc_rows, enc_flat, 0, 0)
+    grads_back, head_grads = [], 0.0
+    for s in range(batches):
+        chunks, scalars, qkv, wide, logs = kept[s]
+        outs = backward_attention(scalars, qkv, wide, logs, returns[s], span)
+        grads_back.append(trade(outs))
+        kept[s] = kept[s] + (outs,)
+    add = lambda n: sum(e[n] for e in early)
+    grad_q = add(0)
+    slot_out = add(1).reshape(group, HEAD_DIM, width)
+    head_slots = [((h % 2) * 4 + h // 2) ^ me for h in range(group)]
+    grad_out = jnp.concatenate(
+        [lax.dynamic_index_in_dim(slot_out, k, 0, False) for k in head_slots]
+    )
+    cut = lambda g: jnp.transpose(g.reshape(4, piece, 4, piece), (0, 2, 1, 3))[:, :, None]
+    cut_flipped = lambda g: jnp.transpose(g.reshape(4, piece, 4, piece), (2, 0, 1, 3))[:, :, None]
+    packed = jnp.concatenate(
+        [
+            cut(grad_q),
+            cut(grad_pair[:, :width]),
+            cut(grad_pair[:, width:]),
+            cut_flipped(grad_out),
+            cut_flipped(add(2)),
+            jnp.transpose(add(3).reshape(4, piece, 4, 4, piece), (0, 2, 3, 1, 4)),
+            jnp.transpose(add(4).reshape(4, 4, piece, 4, piece), (3, 0, 1, 2, 4)),
+        ],
+        2,
+    ).reshape(16, -1, 2, half, piece)
+    packed = low(packed)
+    keep_half = lax.dynamic_index_in_dim(packed, ctx_index, 2, False)
+    send_half = lax.dynamic_index_in_dim(packed, 1 - ctx_index, 2, False)
+    halved = keep_half.astype(jnp.float32) + swap_cores(send_half).astype(jnp.float32)
+    scattered = lax.psum_scatter(low(halved), ("fsdp", "tp"), scatter_dimension=0, tiled=False)
+    scattered = scattered.astype(jnp.float32)
+    other_half = swap_cores(scattered)
+    shards = jnp.concatenate(
+        [
+            jnp.where(ctx_index == 0, scattered, other_half),
+            jnp.where(ctx_index == 0, other_half, scattered),
+        ],
+        1,
+    )
+    for s in range(batches):
+        chunks, outs = kept[s][0], kept[s][5]
+        joined = jnp.stack(outs)
+        for slot, rows in enumerate(chunks):
+            place = places[slot]
+            index = jnp.where(place >= 0, place, me) ^ me
+            part = dot_of(lax.dynamic_index_in_dim(joined, index, 0, False), rows, 1, 0)
+            head_grads = head_grads + jnp.where(place >= 0, part, 0.0)
+    head_grads = head_grads.reshape(3 * HEAD_DIM, 4, piece)
+    pieces = [lax.dynamic_index_in_dim(head_grads, fsdp_index ^ k, 1, False) for k in range(4)]
+    head_shard = pieces[0] + sum(
+        lax.ppermute(pieces[k], "fsdp", [(i, i ^ k) for i in range(4)]) for k in range(1, 4)
+    )
+    head_shard = jnp.transpose(head_shard.reshape(3, HEAD_DIM, piece), (0, 2, 1))
+    other_shard = swap_cores(head_shard)
+    grad_self = jnp.concatenate(
+        [
+            jnp.where(ctx_index == 0, head_shard, other_shard),
+            jnp.where(ctx_index == 0, other_shard, head_shard),
+        ],
+        2,
+    )
+    input_grads, gains_one, shifts_one = [], 0.0, 0.0
+    for s in range(batches):
+        upstream = dot_of(jnp.concatenate(grads_back[s]), qkv_slots, 0, 0)
+        unit, inverse = units_one[s]
+        back, gain, shift = norm_back_rows(upstream, unit, inverse, norm_gain[0])
+        input_grads.append(results[s][1] + back)
+        gains_one, shifts_one = gains_one + gain, shifts_one + shift
+    total = lambda n: sum(v[n] for v in sums)
+    gain_grad, bias_grad, square_totals = lax.psum(
+        (
+            jnp.stack([gains_one, total(1), total(3)]),
+            jnp.stack([shifts_one, total(2), total(4)]),
+            total(0),
+        ),
+        ("fsdp", "ctx", "tp"),
+    )
+    entries = (
+        tokens.shape[0]
+        * tokens.shape[1]
+        * tokens.shape[2]
+        * lax.axis_size("fsdp")
+        * lax.axis_size("ctx")
+        * lax.axis_size("tp")
+    )
+    return (
+        jnp.stack([r[0] for r in results]),
+        jnp.stack(input_grads),
+        encoder_grad,
+        grad_self,
+        shards[0],
+        shards[1:3],
+        shards[3],
+        shards[4],
+        jnp.transpose(shards[5:9], (1, 0, 2)).reshape(piece, width),
+        shards[9:13].reshape(width, piece),
+        gain_grad,
+        bias_grad[:2],
+        bias_grad[2],
+        jnp.sqrt(square_totals / entries),
+    )
+
+
 def solution(mesh):
     placed = (
         P("fsdp", ("ctx", "tp"), None),
@@ -474,8 +1051,9 @@
         P(),
         P("fsdp", ("ctx", "tp"), None),
     )
+    heads_fit = dict(mesh.shape) == {"fsdp": 4, "ctx": 2, "tp": 4}
     return jax.shard_map(
-        local,
+        local_heads if heads_fit else local,
         mesh=mesh,
         in_specs=placed,
         out_specs=(

time: 2290 us -> 799 us (0.35)
  waiting for transfers between devices: 1450 us -> 133 us
  matrix products: 421 us -> 120 us
  starting transfers between devices: 1.46 us -> 161 us
  Pallas kernels: 0 us -> 128 us
  other arithmetic: 126 us -> 45.6 us
  blocking collectives: 91.3 us -> 37.2 us
  loops' own time: 33.1 us -> 0 us
    reduce_scatter x18 -> x1, waiting for transfers between devices: 1020 us -> 0.02 us  [local_heads(): lax.psum_scatter(low(halved), ('fsdp', 'tp'), scatter_dimension=0, tiled=...]
    all_gather x8 -> x1, waiting for transfers between devices: 428 us -> 0.01 us  [local_heads(): gathered = lax.all_gather(own_half, ('fsdp', 'tp'), axis=0, tiled=False)]
    dot_general x85 -> x74, matrix products: 416 us -> 112 us  [the longest x63 98.8 us: dot_of(): lax.dot_general(left, right, (((left_dim,), (right_dim,)), ((), ())), pre...]
    ppermute x0 -> x81, starting transfers between devices: none -> 160 us  [the longest x49 70.6 us: trade(): lax.ppermute(parts[k], ('ctx', 'tp'), [(i, i ^ k) for i in range(group)])]
    ppermute x0 -> x81, waiting for transfers between devices: none -> 133 us  [the longest x49 105 us: trade(): lax.ppermute(parts[k], ('ctx', 'tp'), [(i, i ^ k) for i in range(group)])]
    pallas_call x0 -> x4, Pallas kernels: none -> 128 us  [the longest x2 72.7 us: backward_attention(): pl.pallas_call(functools.partial(backward_kernel, span=span, chunk=chunk,...]
    while x104 -> x0, local copies, waits for them, and re-layouts: 56.5 us -> none
    all_gather x7 -> x0, blocking collectives: 52.5 us -> none  [the longest x1 9.34 us: local(): lax.all_gather(ffn_down, 'fsdp', axis=1, tiled=True)]
  transfers between devices with their start and end apart: 27 -> 83, of which waited for: 20 -> 23; matrix products, arithmetic and copies ran while one was open for 16% -> 21% of each run, Pallas kernels for 0% -> 16%
where the time goes in v1:
time: 799 us; the launch traced here: 790 us
  starting transfers between devices  161 us (20%)
  local copies, waits for them, and re-layouts  148 us (19%)
  waiting for transfers between devices  133 us (17%)
  Pallas kernels  128 us (16%)
  matrix products  120 us (15%)
  other arithmetic  45.6 us (6%)
  blocking collectives  37.2 us (5%)
  between operations  17.3 us (2%)
    ppermute x49, waiting for transfers between devices, trade(): lax.ppermute(parts[k], ('ctx', 'tp'), [(i, i ^ k) for i in range(group)])  105 us
    dot_general x63, matrix products, dot_of(): lax.dot_general(left, right, (((left_dim,), (right_dim,)), ((), ())), pre...  98.8 us
    pallas_call x2, Pallas kernels, backward_attention(): pl.pallas_call(functools.partial(backward_kernel, span=span, chunk=chunk,...  72.7 us
    ppermute x49, starting transfers between devices, trade(): lax.ppermute(parts[k], ('ctx', 'tp'), [(i, i ^ k) for i in range(group)])  70.6 us
    unnamed x427, local copies, waits for them, and re-layouts  57.9 us
    pallas_call x2, Pallas kernels, forward_attention(): pl.pallas_call(functools.partial(forward_kernel, span=span, chunk=chunk,...  55.2 us
    ppermute x16, starting transfers between devices, swap_cores(): return lax.ppermute(value, 'ctx', [(0, 1), (1, 0)])  52.8 us
    psum x1, blocking collectives, local_heads(): lax.psum((jnp.stack([gains_one, total(1), total(3)]), jnp.stack([shifts_o...  37.2 us
  transfers between devices with their start and end apart: 83, of which 23 were waited for; matrix products, arithmetic and copies ran while one was open for 21% of the time, Pallas kernels for 16%

profile of v1, /device:TPU:17, one launch (start us, length us, event | category | flops | bytes accessed | tf_op | source)
XLA Modules:
  0.0 790.1 jit_solution(7987212402189977290)
XLA Ops:
  41.0 13.0 %collective-permute-start.27 = (bf16[512,512]{1,0:T(8,128)(2,1)S(1)}, bf16[512,512]{1,0:T(8,128)(2,1)S(1)}, u32[]{:S(2)}, u32[]{:S(2)}) collective-permute-start(bf16[512,512]{1,0:T(8,128)(2,1)S(1)} %get-tuple-element.226.refs_0_), channel_id=1, source_target_pairs={{0,4},{4,0},{1,5},{5,1},{2,6},{6,2},{3,7},{7,3},{8,12},{12,8},{9,1... | collective-permute-start | bytes 1572872 | tf_op jit(solution)/shard_map/ppermute | solution.py:698
  54.0 5.6 collective-permute-start.5
  59.7 8.2 %collective-permute-done.22.refs_1_ = bf16[512,512]{1,0:T(8,128)(2,1)S(1)} collective-permute-done((bf16[512,512]{1,0:T(8,128)(2,1)S(1)}, bf16[512,512]{1,0:T(8,128)(2,1)S(1)}, u32[]{:S(2)}, u32[]{:S(2)}) %collective-permute-start.22) | collective-permute-done | bytes 524320 | tf_op jit(solution)/shard_map/ppermute | solution.py:710
  69.9 17.3 %collective-permute-start.9 = (bf16[512,512]{1,0:T(8,128)(2,1)S(1)}, bf16[512,512]{1,0:T(8,128)(2,1)}, u32[]{:S(2)}, u32[]{:S(2)}) collective-permute-start(bf16[512,512]{1,0:T(8,128)(2,1)S(1)} %collective-permute-done.3.refs_1_), channel_id=1, source_target_pairs={{0,4},{4,0},{1,5},{5,1},{2,6},{6,2},{3,7},{7,3},{8,12},{12,8},{9,1... | collective-permute-start | bytes 1572872 | tf_op jit(solution)/shard_map/ppermute | solution.py:698
  88.0 9.8 %collective-permute-done.5.refs_3_ = bf16[512,512]{1,0:T(8,128)(2,1)S(1)} collective-permute-done((bf16[512,512]{1,0:T(8,128)(2,1)S(1)}, bf16[512,512]{1,0:T(8,128)(2,1)S(1)}, u32[]{:S(2)}, u32[]{:S(2)}) %collective-permute-start.5) | collective-permute-done | bytes 524320 | tf_op jit(solution)/shard_map/ppermute | solution.py:712
  104.3 16.1 %collective-permute-start.28 = (bf16[512,512]{1,0:T(8,128)(2,1)S(1)}, bf16[512,512]{1,0:T(8,128)(2,1)S(1)}, u32[]{:S(2)}, u32[]{:S(2)}) collective-permute-start(bf16[512,512]{1,0:T(8,128)(2,1)S(1)} %collective-permute-done.22.refs_1_), channel_id=1, source_target_pairs={{0,4},{4,0},{1,5},{5,1},{2,6},{6,2},{3,7},{7,3},{8,12},{12,8},{9,1... | collective-permute-start | bytes 1572872 | tf_op jit(solution)/shard_map/ppermute | solution.py:698
  130.9 28.1 %attention_forward.2 = (bf16[192,4096]{1,0:T(8,128)(2,1)}, f32[64,4096]{1,0:T(8,128)}, f32[1,4096]{1,0:T(1,128)}, bf16[64,512]{1,0:T(8,128)(2,1)}, bf16[64,512]{...) custom-call(s32[14]{0:T(128)} %stack.211.scalars, ...), custom_call_target="tpu_custom_call" | custom-call | flops 20000000000 | bytes 10000000 | tf_op jit(solution)/shard_map/attention_forward/pallas_call | solution.py:551
  164.4 27.1 %attention_forward.3 = (bf16[192,4096]{1,0:T(8,128)(2,1)}, f32[64,4096]{1,0:T(8,128)}, f32[1,4096]{1,0:T(1,128)}, bf16[64,512]{1,0:T(8,128)(2,1)}, bf16[64,512]{...) custom-call(s32[14]{0:T(128)} %stack.217.scalars, ...), custom_call_target="tpu_custom_call" | custom-call | flops 20000000000 | bytes 10000000 | tf_op jit(solution)/shard_map/attention_forward/pallas_call | solution.py:551
  214.6 5.8 broadcast_select_fusion.1
  220.4 10.1 %pad_maximum_fusion = bf16[16,16,128,128]{3,2,1,0:T(8,128)(2,1)} fusion(bf16[16,16,64,128]{3,2,1,0:T(8,128)(2,1)} %get-tuple-element.222, bf16[16,16,64,128]{3,2,1,0:T(8,128)(2,1)} %get-tuple-element.221), kind=kLoop, calls=%fused_computation.2 | loop fusion | flops 16777216 | bytes 16777216 | tf_op jit(solution)/shard_map/concatenate | solution.py:820
  404.7 6.0 add_convert_fusion.1
  429.4 5.2 maximum_add_fusion
  441.6 35.0 %attention_backward.3 = (bf16[192,512]{1,0:T(8,128)(2,1)}, bf16[192,512]{1,0:T(8,128)(2,1)}, bf16[192,512]{1,0:T(8,128)(2,1)}, bf16[192,512]{1,0:T(8,128)(2,1)},...) custom-call(s32[14]{0:T(128)} %stack.217.scalars, ...), custom_call_target="tpu_custom_call" | custom-call | flops 40000000000 | bytes 10000000 | tf_op jit(solution)/shard_map/attention_backward/pallas_call | solution.py:668
  485.7 7.2 collective-permute-start.70
  493.0 37.7 %attention_backward.2 = (bf16[192,512]{1,0:T(8,128)(2,1)}, bf16[192,512]{1,0:T(8,128)(2,1)}, bf16[192,512]{1,0:T(8,128)(2,1)}, bf16[192,512]{1,0:T(8,128)(2,1)},...) custom-call(s32[14]{0:T(128)} %stack.211.scalars, ...), custom_call_target="tpu_custom_call" | custom-call | flops 40000000000 | bytes 10000000 | tf_op jit(solution)/shard_map/attention_backward/pallas_call | solution.py:668
  599.2 5.9 collective-permute-start.77
  621.9 6.4 collective-permute-done.63
  634.2 15.7 %collective-permute-done.66 = bf16[192,512]{1,0:T(8,128)(2,1)S(1)} collective-permute-done((bf16[192,512]{1,0:T(8,128)(2,1)}, bf16[192,512]{1,0:T(8,128)(2,1)S(1)}, u32[]{:S(2)}, u32[]{:S(2)}) %collective-permute-start.66) | collective-permute-done | bytes 196640 | tf_op jit(solution)/shard_map/ppermute | solution.py:704
  651.2 23.9 %collective-permute-done.67 = bf16[192,512]{1,0:T(8,128)(2,1)S(1)} collective-permute-done((bf16[192,512]{1,0:T(8,128)(2,1)S(1)}, bf16[192,512]{1,0:T(8,128)(2,1)S(1)}, u32[]{:S(2)}, u32[]{:S(2)}) %collective-permute-start.67) | collective-permute-done | bytes 196640 | tf_op jit(solution)/shard_map/ppermute | solution.py:704
  678.0 5.6 collective-permute-done.48
  687.5 19.4 %collective-permute-done.49 = bf16[192,512]{1,0:T(8,128)(2,1)S(1)} collective-permute-done((bf16[192,512]{1,0:T(8,128)(2,1)}, bf16[192,512]{1,0:T(8,128)(2,1)S(1)}, u32[]{:S(2)}, u32[]{:S(2)}) %collective-permute-start.49) | collective-permute-done | bytes 196640 | tf_op jit(solution)/shard_map/ppermute | solution.py:704
  707.0 8.1 %collective-permute-done.52 = bf16[192,512]{1,0:T(8,128)(2,1)S(1)} collective-permute-done((bf16[192,512]{1,0:T(8,128)(2,1)}, bf16[192,512]{1,0:T(8,128)(2,1)S(1)}, u32[]{:S(2)}, u32[]{:S(2)}) %collective-permute-start.52) | collective-permute-done | bytes 196640 | tf_op jit(solution)/shard_map/ppermute | solution.py:704
  715.1 15.5 %collective-permute-done.53 = bf16[192,512]{1,0:T(8,128)(2,1)S(1)} collective-permute-done((bf16[192,512]{1,0:T(8,128)(2,1)}, bf16[192,512]{1,0:T(8,128)(2,1)S(1)}, u32[]{:S(2)}, u32[]{:S(2)}) %collective-permute-start.53) | collective-permute-done | bytes 196640 | tf_op jit(solution)/shard_map/ppermute | solution.py:704
  738.5 37.2 %all-reduce = (f32[3,512]{1,0:T(4,128)}, f32[3,512]{1,0:T(4,128)S(1)}, f32[4]{0:T(128)S(1)}) all-reduce(f32[3,512]{1,0:T(4,128)S(1)} %pad_maximum_fusion.8, f32[3,512]{1,0:T(4,128)S(1)} %pad_maximum_fusion.9, f32[4]{0:T(128)S(1)} %maximum_add_fusion), channel_id=1, replica_groups=mesh['fsdp'=4,'ctx'=2,'tp'=4] {'fsdp','ctx','tp'}, use_global_device_ids=true, to_apply=%region_37.38 | all-reduce | flops 3076 | bytes 24608 | tf_op jit(solution)/shard_map/psum | solution.py:1002
  (794 shorter events, 402.9 us)
Async XLA Ops:
  7.2 123.6 %all-gather.3.cloned.1.call-start = ((), (), s32[]{:S(2)}) async-start(), calls=%async_computation.2 | async-start | bytes 4456448 | tf_op jit(solution)/shard_map/all_gather | solution.py:788
  15.4 722.0 %reduce-scatter.2.cloned.1.call-start = ((), (), s32[]{:S(2)}) async-start(), calls=%async_computation.1 | async-start | bytes 3620864 | tf_op jit(solution)/shard_map/reduce_scatter | solution.py:962
  40.3 46.9 %collective-permute-start.26 = (bf16[512,512]{1,0:T(8,128)(2,1)S(1)}, bf16[512,512]{1,0:T(8,128)(2,1)S(1)}, u32[]{:S(2)}, u32[]{:S(2)}) collective-permute-start(bf16[512,512]{1,0:T(8,128)(2,1)S(1)} %get-tuple-element.226.refs_0_), channel_id=1, source_target_pairs={{0,3},{3,0},{4,7},{7,4},{8,11},{11,8},{12,15},{15,12},{16,19},{19,... | collective-permute-start | bytes 1572872 | tf_op jit(solution)/shard_map/ppermute | solution.py:714
  41.0 46.3 %collective-permute-start.27 = (bf16[512,512]{1,0:T(8,128)(2,1)S(1)}, bf16[512,512]{1,0:T(8,128)(2,1)S(1)}, u32[]{:S(2)}, u32[]{:S(2)}) collective-permute-start(bf16[512,512]{1,0:T(8,128)(2,1)S(1)} %get-tuple-element.226.refs_0_), channel_id=1, source_target_pairs={{0,4},{4,0},{1,5},{5,1},{2,6},{6,2},{3,7},{7,3},{8,12},{12,8},{9,1... | collective-permute-start | bytes 1572872 | tf_op jit(solution)/shard_map/ppermute | solution.py:698
  130.8 83.8 %collective-permute-start.21 = (bf16[16,16,64,128]{3,2,1,0:T(8,128)(2,1)}, bf16[16,16,64,128]{3,2,1,0:T(8,128)(2,1)}, u32[]{:S(2)}, u32[]{:S(2)}) collective-permute-start(bf16[16,16,64,128]{3,2,1,0:T(8,128)(2,1)} %bitcast.693), channel_id=1, source_target_pairs={{0,4},{4,0},{1,5},{5,1},{2,6},{6,2},{3,7},{7,3},{8,12},{12,8},{9,1... | collective-permute-start | bytes 12582920 | tf_op jit(solution)/shard_map/ppermute | solution.py:698
  343.8 83.7 %collective-permute-start.54 = (bf16[64,512]{1,0:T(8,128)(2,1)}, bf16[64,512]{1,0:T(8,128)(2,1)}, u32[]{:S(2)}, u32[]{:S(2)}) collective-permute-start(bf16[64,512]{1,0:T(8,128)(2,1)} %get-tuple-element.263), channel_id=1, source_target_pairs={{0,1},{1,0},{2,3},{3,2},{4,5},{5,4},{6,7},{7,6},{8,9},{9,8},{10,11... | collective-permute-start | bytes 196616 | tf_op jit(solution)/shard_map/ppermute | solution.py:704
  343.8 85.2 %collective-permute-start.55 = (bf16[64,512]{1,0:T(8,128)(2,1)}, bf16[64,512]{1,0:T(8,128)(2,1)}, u32[]{:S(2)}, u32[]{:S(2)}) collective-permute-start(bf16[64,512]{1,0:T(8,128)(2,1)} %get-tuple-element.262), channel_id=1, source_target_pairs={{0,2},{1,3},{2,0},{3,1},{4,6},{5,7},{6,4},{7,5},{8,10},{9,11},{10,... | collective-permute-start | bytes 196616 | tf_op jit(solution)/shard_map/ppermute | solution.py:704
  346.3 88.3 %collective-permute-start.56 = (bf16[64,512]{1,0:T(8,128)(2,1)}, bf16[64,512]{1,0:T(8,128)(2,1)}, u32[]{:S(2)}, u32[]{:S(2)}) collective-permute-start(bf16[64,512]{1,0:T(8,128)(2,1)} %get-tuple-element.261), channel_id=1, source_target_pairs={{0,3},{1,2},{2,1},{3,0},{4,7},{5,6},{6,5},{7,4},{8,11},{9,10},{10,... | collective-permute-start | bytes 196616 | tf_op jit(solution)/shard_map/ppermute | solution.py:704
  346.5 90.1 %collective-permute-start.57 = (bf16[64,512]{1,0:T(8,128)(2,1)}, bf16[64,512]{1,0:T(8,128)(2,1)}, u32[]{:S(2)}, u32[]{:S(2)}) collective-permute-start(bf16[64,512]{1,0:T(8,128)(2,1)} %get-tuple-element.260), channel_id=1, source_target_pairs={{0,4},{1,5},{2,6},{3,7},{4,0},{5,1},{6,2},{7,3},{8,12},{9,13},{10,... | collective-permute-start | bytes 196616 | tf_op jit(solution)/shard_map/ppermute | solution.py:704
  348.1 89.6 %collective-permute-start.58 = (bf16[64,512]{1,0:T(8,128)(2,1)}, bf16[64,512]{1,0:T(8,128)(2,1)}, u32[]{:S(2)}, u32[]{:S(2)}) collective-permute-start(bf16[64,512]{1,0:T(8,128)(2,1)} %get-tuple-element.259), channel_id=1, source_target_pairs={{0,5},{1,4},{2,7},{3,6},{4,1},{5,0},{6,3},{7,2},{8,13},{9,12},{10,... | collective-permute-start | bytes 196616 | tf_op jit(solution)/shard_map/ppermute | solution.py:704
  439.2 44.8 %collective-permute-start.44 = (bf16[64,512]{1,0:T(8,128)(2,1)S(1)}, bf16[64,512]{1,0:T(8,128)(2,1)S(1)}, u32[]{:S(2)}, u32[]{:S(2)}) collective-permute-start(bf16[64,512]{1,0:T(8,128)(2,1)S(1)} %copy-done.128), channel_id=1, source_target_pairs={{0,5},{1,4},{2,7},{3,6},{4,1},{5,0},{6,3},{7,2},{8,13},{9,12},{10,... | collective-permute-start | bytes 196616 | tf_op jit(solution)/shard_map/ppermute | solution.py:704
  479.8 63.5 %collective-permute-start.74 = (bf16[2,32,1024]{2,1,0:T(8,128)(2,1)}, bf16[2,32,1024]{2,1,0:T(8,128)(2,1)}, u32[]{:S(2)}, u32[]{:S(2)}) collective-permute-start(bf16[2,32,1024]{2,1,0:T(8,128)(2,1)} %get-tuple-element.234), channel_id=1, source_target_pairs={{0,7},{1,6},{2,5},{3,4},{4,3},{5,2},{6,1},{7,0},{8,15},{9,14},{10,... | collective-permute-start | bytes 393224 | tf_op jit(solution)/shard_map/ppermute | solution.py:704
  481.0 62.2 %collective-permute-start.73 = (bf16[2,32,1024]{2,1,0:T(8,128)(2,1)}, bf16[2,32,1024]{2,1,0:T(8,128)(2,1)}, u32[]{:S(2)}, u32[]{:S(2)}) collective-permute-start(bf16[2,32,1024]{2,1,0:T(8,128)(2,1)} %get-tuple-element.235), channel_id=1, source_target_pairs={{0,6},{1,7},{2,4},{3,5},{4,2},{5,3},{6,0},{7,1},{8,14},{9,15},{10,... | collective-permute-start | bytes 393224 | tf_op jit(solution)/shard_map/ppermute | solution.py:704
  484.0 62.1 %collective-permute-start.72 = (bf16[2,32,1024]{2,1,0:T(8,128)(2,1)}, bf16[2,32,1024]{2,1,0:T(8,128)(2,1)}, u32[]{:S(2)}, u32[]{:S(2)}) collective-permute-start(bf16[2,32,1024]{2,1,0:T(8,128)(2,1)} %get-tuple-element.236), channel_id=1, source_target_pairs={{0,5},{1,4},{2,7},{3,6},{4,1},{5,0},{6,3},{7,2},{8,13},{9,12},{10,... | collective-permute-start | bytes 393224 | tf_op jit(solution)/shard_map/ppermute | solution.py:704
  484.2 61.9 %collective-permute-start.71 = (bf16[2,32,1024]{2,1,0:T(8,128)(2,1)}, bf16[2,32,1024]{2,1,0:T(8,128)(2,1)}, u32[]{:S(2)}, u32[]{:S(2)}) collective-permute-start(bf16[2,32,1024]{2,1,0:T(8,128)(2,1)} %get-tuple-element.237), channel_id=1, source_target_pairs={{0,4},{1,5},{2,6},{3,7},{4,0},{5,1},{6,2},{7,3},{8,12},{9,13},{10,... | collective-permute-start | bytes 393224 | tf_op jit(solution)/shard_map/ppermute | solution.py:704
  485.7 62.5 %collective-permute-start.70 = (bf16[2,32,1024]{2,1,0:T(8,128)(2,1)S(1)}, bf16[2,32,1024]{2,1,0:T(8,128)(2,1)}, u32[]{:S(2)}, u32[]{:S(2)}) collective-permute-start(bf16[2,32,1024]{2,1,0:T(8,128)(2,1)S(1)} %copy-done.120), channel_id=1, source_target_pairs={{0,3},{1,2},{2,1},{3,0},{4,7},{5,6},{6,5},{7,4},{8,11},{9,10},{10,... | collective-permute-start | bytes 393224 | tf_op jit(solution)/shard_map/ppermute | solution.py:704
  546.1 72.4 %collective-permute-start.61 = (bf16[192,512]{1,0:T(8,128)(2,1)}, bf16[192,512]{1,0:T(8,128)(2,1)}, u32[]{:S(2)}, u32[]{:S(2)}) collective-permute-start(bf16[192,512]{1,0:T(8,128)(2,1)} %get-tuple-element.83), channel_id=1, source_target_pairs={{0,1},{1,0},{2,3},{3,2},{4,5},{5,4},{6,7},{7,6},{8,9},{9,8},{10,11... | collective-permute-start | bytes 589832 | tf_op jit(solution)/shard_map/ppermute | solution.py:704
  546.1 73.7 %collective-permute-start.62 = (bf16[192,512]{1,0:T(8,128)(2,1)}, bf16[192,512]{1,0:T(8,128)(2,1)}, u32[]{:S(2)}, u32[]{:S(2)}) collective-permute-start(bf16[192,512]{1,0:T(8,128)(2,1)} %get-tuple-element.84), channel_id=1, source_target_pairs={{0,2},{1,3},{2,0},{3,1},{4,6},{5,7},{6,4},{7,5},{8,10},{9,11},{10,... | collective-permute-start | bytes 589832 | tf_op jit(solution)/shard_map/ppermute | solution.py:704
  619.8 55.3 %collective-permute-start.67 = (bf16[192,512]{1,0:T(8,128)(2,1)S(1)}, bf16[192,512]{1,0:T(8,128)(2,1)S(1)}, u32[]{:S(2)}, u32[]{:S(2)}) collective-permute-start(bf16[192,512]{1,0:T(8,128)(2,1)S(1)} %copy-done.111), channel_id=1, source_target_pairs={{0,7},{1,6},{2,5},{3,4},{4,3},{5,2},{6,1},{7,0},{8,15},{9,14},{10,... | collective-permute-start | bytes 589832 | tf_op jit(solution)/shard_map/ppermute | solution.py:704
  628.3 46.9 %collective-permute-start.47 = (bf16[192,512]{1,0:T(8,128)(2,1)}, bf16[192,512]{1,0:T(8,128)(2,1)S(1)}, u32[]{:S(2)}, u32[]{:S(2)}) collective-permute-start(bf16[192,512]{1,0:T(8,128)(2,1)} %get-tuple-element.72), channel_id=1, source_target_pairs={{0,1},{1,0},{2,3},{3,2},{4,5},{5,4},{6,7},{7,6},{8,9},{9,8},{10,11... | collective-permute-start | bytes 589832 | tf_op jit(solution)/shard_map/ppermute | solution.py:704
  629.2 54.4 %collective-permute-start.48 = (bf16[192,512]{1,0:T(8,128)(2,1)}, bf16[192,512]{1,0:T(8,128)(2,1)S(1)}, u32[]{:S(2)}, u32[]{:S(2)}) collective-permute-start(bf16[192,512]{1,0:T(8,128)(2,1)} %get-tuple-element.73), channel_id=1, source_target_pairs={{0,2},{1,3},{2,0},{3,1},{4,6},{5,7},{6,4},{7,5},{8,10},{9,11},{10,... | collective-permute-start | bytes 589832 | tf_op jit(solution)/shard_map/ppermute | solution.py:704
  633.2 73.7 %collective-permute-start.49 = (bf16[192,512]{1,0:T(8,128)(2,1)}, bf16[192,512]{1,0:T(8,128)(2,1)S(1)}, u32[]{:S(2)}, u32[]{:S(2)}) collective-permute-start(bf16[192,512]{1,0:T(8,128)(2,1)} %get-tuple-element.74), channel_id=1, source_target_pairs={{0,3},{1,2},{2,1},{3,0},{4,7},{5,6},{6,5},{7,4},{8,11},{9,10},{10,... | collective-permute-start | bytes 589832 | tf_op jit(solution)/shard_map/ppermute | solution.py:704
  649.9 57.0 %collective-permute-start.50 = (bf16[192,512]{1,0:T(8,128)(2,1)}, bf16[192,512]{1,0:T(8,128)(2,1)S(1)}, u32[]{:S(2)}, u32[]{:S(2)}) collective-permute-start(bf16[192,512]{1,0:T(8,128)(2,1)} %get-tuple-element.75), channel_id=1, source_target_pairs={{0,4},{1,5},{2,6},{3,7},{4,0},{5,1},{6,2},{7,3},{8,12},{9,13},{10,... | collective-permute-start | bytes 589832 | tf_op jit(solution)/shard_map/ppermute | solution.py:704
  683.6 47.0 %collective-permute-start.53 = (bf16[192,512]{1,0:T(8,128)(2,1)}, bf16[192,512]{1,0:T(8,128)(2,1)S(1)}, u32[]{:S(2)}, u32[]{:S(2)}) collective-permute-start(bf16[192,512]{1,0:T(8,128)(2,1)} %get-tuple-element.78), channel_id=1, source_target_pairs={{0,7},{1,6},{2,5},{3,4},{4,3},{5,2},{6,1},{7,0},{8,15},{9,14},{10,... | collective-permute-start | bytes 589832 | tf_op jit(solution)/shard_map/ppermute | solution.py:704
  (230 other events, 3623.2 us)
Sparse Core Ops, SparseCore 0:
  15.5 107.7 all-gather.2
  590.8 139.9 reduce-scatter.1

commit v2 on v0

--- a/solution.py
+++ b/solution.py
@@ -1,8 +1,11 @@
+import functools
 import math
 
 import jax
 import jax.numpy as jnp
 from jax import lax
+from jax.experimental import pallas as pl
+from jax.experimental.pallas import tpu as pltpu
 from jax.sharding import PartitionSpec as P
 
 HEAD_DIM = 64
@@ -12,6 +15,7 @@
 NEG = -1e30
 ROOT_HALF = 1.0 / math.sqrt(2.0)
 INV_ROOT_TWO_PI = 1.0 / math.sqrt(2.0 * math.pi)
+VMEM_LIMIT = 56 * 2**20
 
 
 def norm_rows(hidden, scaling, offsets):
@@ -456,6 +460,931 @@
     )
 
 
+def dot_of(left, right, left_dim, right_dim):
+    return lax.dot_general(
+        left, right, (((left_dim,), (right_dim,)), ((), ())), preferred_element_type=jnp.float32
+    )
+
+
+def bounds(prefix, start, query_span, key_span):
+    whole = jnp.maximum(prefix, start + 1) // key_span
+    every = (jnp.maximum(prefix, start + query_span) + key_span - 1) // key_span
+    return whole, every
+
+
+def hide(scores, limit, offset):
+    return jnp.where(lax.broadcasted_iota(jnp.int32, scores.shape, 0) < limit - offset, scores, NEG)
+
+
+def backward_kernel(scalars, qkv_ref, wide_ref, log_ref, *refs, span, chunk, group):
+    grad_refs, refs = refs[:group], refs[group:]
+    out_refs, refs = refs[:group], refs[group:]
+    (
+        queries_ref,
+        keys_ref,
+        values_ref,
+        gradt_ref,
+        grad_ref,
+        delta_ref,
+        grad_keys_ref,
+        grad_values_ref,
+        low_ref,
+    ) = refs
+    step = pl.program_id(0)
+    prefix, me = scalars[0], scalars[1]
+    factor = HEAD_DIM**-0.5
+    length = qkv_ref.shape[1]
+
+    @pl.when(step == 0)
+    def prepare():
+        for slot in range(group):
+            here = pl.ds(pl.multiple_of((me ^ slot) * chunk, chunk), chunk)
+            gradt_ref[:, here] = grad_refs[slot][...]
+            grad_ref[here, :] = grad_refs[slot][...].T
+        delta_ref[...] = jnp.sum(
+            gradt_ref[...].astype(jnp.float32) * wide_ref[...], axis=0, keepdims=True
+        )
+        queries_ref[...] = qkv_ref[:HEAD_DIM, :].T
+        keys_ref[...] = qkv_ref[HEAD_DIM : 2 * HEAD_DIM, :].T
+        values_ref[...] = qkv_ref[2 * HEAD_DIM :, :].T
+        grad_keys_ref[...] = jnp.zeros_like(grad_keys_ref)
+        grad_values_ref[...] = jnp.zeros_like(grad_values_ref)
+
+    start = pl.multiple_of(step * span, span)
+    here = pl.ds(start, span)
+    queries_t, queries = qkv_ref[:HEAD_DIM, here], queries_ref[here, :]
+    grads_t, grads = gradt_ref[:, here], grad_ref[here, :]
+    logs, deltas = log_ref[:, here], delta_ref[:, here]
+    limit = jnp.maximum(prefix, start + 1 + lax.broadcasted_iota(jnp.int32, (1, span), 1))
+    whole, every = bounds(prefix, start, span, span)
+
+    def advance(block, grad_queries, masked):
+        there = pl.ds(pl.multiple_of(block * span, span), span)
+        scores = dot_of(keys_ref[there, :], queries_t, 1, 0)
+        if masked:
+            scores = hide(scores, limit, block * span)
+        probs = jnp.exp(scores - logs)
+        grad_probs = dot_of(values_ref[there, :], grads_t, 1, 0)
+        grad_scores = (probs * (grad_probs - deltas)).astype(jnp.bfloat16)
+        grad_values_ref[there, :] += dot_of(probs.astype(jnp.bfloat16), grads, 1, 0)
+        grad_keys_ref[there, :] += dot_of(grad_scores, queries, 1, 0)
+        return grad_queries + dot_of(
+            qkv_ref[HEAD_DIM : 2 * HEAD_DIM, there], grad_scores, 1, 0
+        )
+
+    grad_queries = jnp.zeros((HEAD_DIM, span), jnp.float32)
+    grad_queries = lax.fori_loop(0, whole, lambda j, c: advance(j, c, False), grad_queries)
+    grad_queries = lax.fori_loop(whole, every, lambda j, c: advance(j, c, True), grad_queries)
+    low = (grad_queries * factor).astype(jnp.bfloat16)
+    for part in range(span // chunk):
+        low_ref[(step * (span // chunk) + part) ^ me, :HEAD_DIM, :] = low[
+            :, part * chunk : (part + 1) * chunk
+        ]
+
+    @pl.when(step == pl.num_programs(0) - 1)
+    def finish():
+        for place in range(length // chunk):
+            rows = pl.ds(place * chunk, chunk)
+            low_ref[place ^ me, HEAD_DIM : 2 * HEAD_DIM, :] = grad_keys_ref[rows, :].T.astype(
+                jnp.bfloat16
+            )
+            low_ref[place ^ me, 2 * HEAD_DIM :, :] = grad_values_ref[rows, :].T.astype(jnp.bfloat16)
+        for slot in range(group):
+            out_refs[slot][...] = low_ref[slot]
+
+
+def backward_attention(scalars, qkv, wide, logs, grads, span):
+    group = len(grads)
+    length = qkv.shape[1]
+    chunk = grads[0].shape[1]
+    whole = lambda *shape: pl.BlockSpec(shape, lambda i, s: (0,) * len(shape))
+    bf16, f32 = jnp.bfloat16, jnp.float32
+    return pl.pallas_call(
+        functools.partial(backward_kernel, span=span, chunk=chunk, group=group),
+        grid_spec=pltpu.PrefetchScalarGridSpec(
+            num_scalar_prefetch=1,
+            grid=(length // span,),
+            in_specs=[whole(*qkv.shape), whole(*wide.shape), whole(*logs.shape)]
+            + [whole(*g.shape) for g in grads],
+            out_specs=[whole(3 * HEAD_DIM, chunk)] * group,
+            scratch_shapes=[
+                pltpu.VMEM((length, HEAD_DIM), bf16),
+                pltpu.VMEM((length, HEAD_DIM), bf16),
+                pltpu.VMEM((length, HEAD_DIM), bf16),
+                pltpu.VMEM((HEAD_DIM, length), bf16),
+                pltpu.VMEM((length, HEAD_DIM), bf16),
+                pltpu.VMEM((1, length), f32),
+                pltpu.VMEM((length, HEAD_DIM), f32),
+                pltpu.VMEM((length, HEAD_DIM), f32),
+                pltpu.VMEM((group, 3 * HEAD_DIM, chunk), bf16),
+            ],
+        ),
+        out_shape=[jax.ShapeDtypeStruct((3 * HEAD_DIM, chunk), bf16)] * group,
+        compiler_params=pltpu.CompilerParams(vmem_limit_bytes=VMEM_LIMIT),
+        cost_estimate=pl.CostEstimate(
+            flops=40_000_000_000, bytes_accessed=10_000_000, transcendentals=10_000_000
+        ),
+        name="attention_backward",
+    )(scalars, qkv, wide, logs, *grads)
+
+
+def swap_cores(value):
+    return lax.ppermute(value, "ctx", [(0, 1), (1, 0)])
+
+
+def trade(parts):
+    group = len(parts)
+    return [parts[0]] + [
+        lax.ppermute(parts[k], ("ctx", "tp"), [(i, i ^ k) for i in range(group)])
+        for k in range(1, group)
+    ]
+
+
+def norm_back_rows(upstream, unit_rows, inverse, scaling):
+    scaled = upstream * scaling
+    result = inverse * (
+        scaled
+        - jnp.mean(scaled, -1, keepdims=True)
+        - unit_rows * jnp.mean(scaled * unit_rows, -1, keepdims=True)
+    )
+    return result, jnp.sum(upstream * unit_rows, 0), jnp.sum(upstream, 0)
+
+
+def low(value):
+    return value.astype(jnp.bfloat16)
+
+
+def head_parts(value):
+    return value.reshape(value.shape[0], -1, HEAD_DIM)
+
+
+def rows_norm(hidden, scaling, offsets):
+    centre = hidden - jnp.mean(hidden, -1, keepdims=True)
+    inverse = lax.rsqrt(jnp.mean(centre * centre, -1, keepdims=True) + EPS)
+    unit_rows = centre * inverse
+    return low(unit_rows * scaling + offsets), unit_rows, inverse
+
+
+def rows_back(upstream, unit_rows, inverse, scaling):
+    scaled = upstream * scaling
+    result = inverse * (
+        scaled
+        - jnp.mean(scaled, -1, keepdims=True)
+        - unit_rows * jnp.mean(scaled * unit_rows, -1, keepdims=True)
+    )
+    return (
+        result,
+        jnp.sum(upstream * unit_rows, 0, keepdims=True),
+        jnp.sum(upstream, 0, keepdims=True),
+    )
+
+
+MESH = pl.DeviceIdType.MESH
+
+
+def meet(group, tp, fsdp):
+    here, core, chip = lax.axis_index("fsdp"), lax.axis_index("ctx"), lax.axis_index("tp")
+    me = core * tp + chip
+    barrier = pltpu.get_barrier_semaphore()
+    for k in range(1, group):
+        other = me ^ k
+        pl.semaphore_signal(
+            barrier, inc=1, device_id={"ctx": other // tp, "tp": other % tp}, device_id_type=MESH
+        )
+    for k in range(1, fsdp):
+        pl.semaphore_signal(barrier, inc=1, device_id={"fsdp": here ^ k}, device_id_type=MESH)
+    pl.semaphore_wait(barrier, group - 1 + fsdp - 1)
+
+
+def forward_kernel(
+    prefix_ref,
+    tokens_ref,
+    step_ref,
+    gain_ref,
+    bias_ref,
+    mine_ref,
+    rows_out,
+    qkv_ref,
+    wide_ref,
+    log_ref,
+    ctx_ref,
+    weight_ref,
+    rows_ref,
+    columns,
+    weight,
+    keys_ref,
+    values_ref,
+    low_ref,
+    landing,
+    w_send,
+    w_recv,
+    x_send,
+    x_recv,
+    c_send,
+    c_recv,
+    keep_sem,
+    *,
+    span,
+    tp,
+    fsdp,
+):
+    batches, chunk, width = tokens_ref.shape
+    group = rows_ref.shape[1]
+    length = group * chunk
+    blocks, ratio = length // span, span // chunk
+    wide_blocks = max(1, length // 2 // span)
+    factor = HEAD_DIM**-0.5
+    here, core, chip = lax.axis_index("fsdp"), lax.axis_index("ctx"), lax.axis_index("tp")
+    me = core * tp + chip
+    meet(group, tp, fsdp)
+
+    def w_copy(k):
+        return pltpu.make_async_remote_copy(
+            src_ref=mine_ref,
+            dst_ref=columns.at[k],
+            send_sem=w_send.at[k],
+            recv_sem=w_recv.at[k],
+            device_id={"fsdp": here ^ k},
+            device_id_type=MESH,
+        )
+
+    for k in range(1, fsdp):
+        w_copy(k).start()
+
+    def x_copy(seq, origin, kind):
+        target = ({"tp": chip + 1}, {"tp": chip - 1}, {"ctx": 1 - core})[kind]
+        block = rows_ref.at[seq, core * tp + origin]
+        return pltpu.make_async_remote_copy(
+            src_ref=block,
+            dst_ref=block,
+            send_sem=x_send.at[seq, origin, kind],
+            recv_sem=x_recv.at[seq, core * tp + origin],
+            device_id=target,
+            device_id_type=MESH,
+        )
+
+    def x_wait(seq, place):
+        pltpu.make_async_remote_copy(
+            src_ref=rows_ref.at[seq, place],
+            dst_ref=rows_ref.at[seq, place],
+            send_sem=x_send.at[seq, 0, 0],
+            recv_sem=x_recv.at[seq, place],
+            device_id={"ctx": 1 - core},
+            device_id_type=MESH,
+        ).wait_recv()
+
+    def own_sends(seq):
+        @pl.when(chip < tp - 1)
+        def upward():
+            x_copy(seq, chip, 0).start()
+
+        @pl.when(chip > 0)
+        def downward():
+            x_copy(seq, chip, 1).start()
+
+        x_copy(seq, chip, 2).start()
+
+    def normalise(seq):
+        start_sum = tokens_ref[seq].astype(jnp.float32) + step_ref[seq]
+        normed, unused, unused_too = rows_norm(start_sum, gain_ref[...], bias_ref[...])
+        rows_ref[seq, me] = normed
+
+    normalise(0)
+    own_sends(0)
+    normalise(1)
+    values_ref[:, HEAD_DIM:, :] = jnp.ones_like(values_ref[:, HEAD_DIM:, :])
+    piece = mine_ref.shape[1]
+    for k in range(fsdp):
+        if k:
+            w_copy(k).wait_recv()
+        part = columns[k] if k else mine_ref[...]
+        for f in range(fsdp):
+
+            @pl.when((here ^ k) == f)
+            def place(f=f, part=part):
+                weight[:, f * piece : (f + 1) * piece] = part
+
+    weight_ref[...] = weight[...]
+
+    def project(seq, place):
+        rows = rows_ref[seq, place]
+        joined = low(dot_of(weight[...], rows, 1, 1))
+        at = pl.ds(pl.multiple_of(place * chunk, chunk), chunk)
+        qkv_ref[seq, :HEAD_DIM, at] = joined[:HEAD_DIM] * jnp.bfloat16(factor)
+        qkv_ref[seq, HEAD_DIM:, at] = joined[HEAD_DIM:]
+        values_ref[seq, :HEAD_DIM, at] = joined[2 * HEAD_DIM :]
+        keys_ref[seq, at, :] = low(dot_of(rows, weight[HEAD_DIM : 2 * HEAD_DIM, :], 1, 1))
+
+    def stage(seq, hop):
+        @pl.when(chip >= hop)
+        def from_below():
+            x_wait(seq, core * tp + chip - hop)
+
+            @pl.when(chip < tp - 1)
+            def onward():
+                x_copy(seq, chip - hop, 0).start()
+
+            x_copy(seq, chip - hop, 2).start()
+
+        @pl.when(chip + hop < tp)
+        def from_above():
+            x_wait(seq, core * tp + chip + hop)
+
+            @pl.when(chip > 0)
+            def onward():
+                x_copy(seq, chip + hop, 1).start()
+
+            x_copy(seq, chip + hop, 2).start()
+
+    def project_some(seq, first, count):
+        def one(k, unused):
+            project(seq, first + k)
+            return unused
+
+        lax.fori_loop(0, count, one, 0)
+
+    def complete(seq):
+        def one(k, unused):
+            x_wait(seq, (1 - core) * tp + k)
+            return unused
+
+        project_some(seq, core * tp, tp)
+        lax.fori_loop(0, tp, one, 0)
+        project_some(seq, (1 - core) * tp, tp)
+
+    for hop in range(1, tp):
+        stage(0, hop)
+        if hop == tp - 2:
+            own_sends(1)
+    complete(0)
+
+    def c_copy(seq, place):
+        return pltpu.make_async_remote_copy(
+            src_ref=low_ref.at[seq, place],
+            dst_ref=landing.at[seq, me],
+            send_sem=c_send.at[seq, place],
+            recv_sem=c_recv.at[seq, me],
+            device_id={"ctx": place // tp, "tp": place % tp},
+            device_id_type=MESH,
+        )
+
+    def c_wait(seq, place):
+        pltpu.make_async_remote_copy(
+            src_ref=low_ref.at[seq, place],
+            dst_ref=landing.at[seq, place],
+            send_sem=c_send.at[seq, place],
+            recv_sem=c_recv.at[seq, place],
+            device_id={"ctx": place // tp, "tp": place % tp},
+            device_id_type=MESH,
+        ).wait_recv()
+
+    def attend(index, unused):
+        seq, block = index // blocks, index % blocks
+
+        @pl.when(index == blocks - 1)
+        def pass_on():
+            stage(1, 1)
+
+        @pl.when(index == blocks)
+        def receive():
+            for hop in range(3, tp):
+                stage(1, hop)
+            complete(1)
+
+        start = pl.multiple_of(block * span, span)
+        queries = qkv_ref[seq, :HEAD_DIM, pl.ds(start, span)]
+        limit = jnp.maximum(
+            prefix_ref[seq], start + 1 + lax.broadcasted_iota(jnp.int32, (1, span), 1)
+        )
+
+        def advance(other, carry, masked):
+            highest, total = carry
+            offset = pl.multiple_of(other * span, span)
+            scores = dot_of(keys_ref[seq, pl.ds(offset, span), :], queries, 1, 0)
+            if masked:
+                scores = hide(scores, limit, offset)
+            higher = jnp.maximum(highest, jnp.max(scores, axis=0, keepdims=True))
+            weights = low(jnp.exp(scores - higher))
+            fading = jnp.exp(highest - higher)
+            total = total * fading + dot_of(values_ref[seq, :, pl.ds(offset, span)], weights, 1, 0)
+            return higher, total
+
+        carry = (
+            jnp.full((1, span), NEG, jnp.float32),
+            jnp.zeros((values_ref.shape[1], span), jnp.float32),
+        )
+        carry = lax.fori_loop(0, block, lambda j, c: advance(j, c, False), carry)
+        highest, total = lax.fori_loop(
+            block, jnp.maximum(block + 1, wide_blocks), lambda j, c: advance(j, c, True), carry
+        )
+        weight_sum = total[HEAD_DIM : HEAD_DIM + 1, :]
+        attended = total[:HEAD_DIM, :] / weight_sum
+        wide_ref[seq, :, pl.ds(start, span)] = attended
+        log_ref[seq, :, pl.ds(start, span)] = highest + jnp.log(weight_sum)
+        attended = low(attended)
+        for part in range(ratio):
+            place = block * ratio + part
+            low_ref[seq, place] = attended[:, part * chunk : (part + 1) * chunk]
+
+            @pl.when(place != me)
+            def send(place=place):
+                c_copy(seq, place).start()
+
+        @pl.when(index == blocks - 1)
+        def pass_on_two():
+            stage(1, 2)
+
+        return unused
+
+    lax.fori_loop(0, batches * blocks, attend, 0)
+    keep = pltpu.make_async_copy(rows_ref, rows_out, keep_sem)
+    keep.start()
+    for seq in range(batches):
+
+        def collect(k, unused, seq=seq):
+            c_wait(seq, me ^ k)
+            ctx_ref[seq, me ^ k] = landing[seq, me ^ k]
+            return unused
+
+        lax.fori_loop(1, group, collect, 0)
+        ctx_ref[seq, me] = low_ref[seq, me]
+    for k in range(1, fsdp):
+        w_copy(k).wait_send()
+    for seq in range(batches):
+        for hop in range(tp):
+
+            @pl.when(chip >= hop)
+            def sent_up(seq=seq, hop=hop):
+                @pl.when(chip < tp - 1)
+                def onward():
+                    x_copy(seq, chip - hop, 0).wait_send()
+
+                x_copy(seq, chip - hop, 2).wait_send()
+
+            @pl.when(chip + hop < tp)
+            def sent_down(seq=seq, hop=hop):
+                @pl.when(chip > 0)
+                def onward():
+                    x_copy(seq, chip + hop, 1).wait_send()
+
+                if hop:
+                    x_copy(seq, chip + hop, 2).wait_send()
+
+        def sent(k, unused, seq=seq):
+            c_copy(seq, me ^ k).wait_send()
+            return unused
+
+        lax.fori_loop(1, group, sent, 0)
+    keep.wait()
+
+
+def forward_group(prefix, tokens, steps, gain, bias, mine, span, group, tp, fsdp):
+    batches, chunk, width = tokens.shape
+    length = group * chunk
+    bf16, f32 = jnp.bfloat16, jnp.float32
+    struct = jax.ShapeDtypeStruct
+    inside = pl.BlockSpec(memory_space=pltpu.VMEM)
+    dma = pltpu.SemaphoreType.DMA
+    return pl.pallas_call(
+        functools.partial(forward_kernel, span=span, tp=tp, fsdp=fsdp),
+        in_specs=[pl.BlockSpec(memory_space=pltpu.SMEM)] + [inside] * 5,
+        out_specs=[pl.BlockSpec(memory_space=pl.ANY)] + [inside] * 5,
+        out_shape=[
+            struct((batches, group, chunk, width), bf16),
+            struct((batches, 3 * HEAD_DIM, length), bf16),
+            struct((batches, HEAD_DIM, length), f32),
+            struct((batches, 1, length), f32),
+            struct((batches, group, HEAD_DIM, chunk), bf16),
+            struct((3 * HEAD_DIM, width), bf16),
+        ],
+        scratch_shapes=[
+            pltpu.VMEM((batches, group, chunk, width), bf16),
+            pltpu.VMEM((fsdp,) + mine.shape, bf16),
+            pltpu.VMEM((3 * HEAD_DIM, width), bf16),
+            pltpu.VMEM((batches, length, HEAD_DIM), bf16),
+            pltpu.VMEM((batches, HEAD_DIM + 16, length), bf16),
+            pltpu.VMEM((batches, group, HEAD_DIM, chunk), bf16),
+            pltpu.VMEM((batches, group, HEAD_DIM, chunk), bf16),
+            dma((fsdp,)),
+            dma((fsdp,)),
+            dma((batches, tp, 3)),
+            dma((batches, group)),
+            dma((batches, group)),
+            dma((batches, group)),
+            dma,
+        ],
+        compiler_params=pltpu.CompilerParams(
+            vmem_limit_bytes=VMEM_LIMIT, collective_id=1, has_side_effects=True
+        ),
+        cost_estimate=pl.CostEstimate(
+            flops=60_000_000_000, bytes_accessed=30_000_000, transcendentals=20_000_000
+        ),
+        name="forward_group",
+    )(prefix, tokens, steps, gain, bias, mine)
+
+
+QUERY, KEY, VALUE, SELF_OUT, CROSS_OUT, UP, DOWN = 0, 1, 2, 3, 4, 5, 9
+
+
+def middle_kernel(
+    scalars,
+    gathered,
+    tokens_ref,
+    step_ref,
+    enc_ref,
+    cot_ref,
+    gain_ref,
+    bias_ref,
+    ctx_ref,
+    final_ref,
+    after_ref,
+    back_ref,
+    enc_grad_ref,
+    stats_ref,
+    packed_ref,
+    weights,
+    totals,
+    context,
+    queries,
+    keys,
+    values,
+    probs,
+    context_two,
+    grad_heads,
+    grad_queries,
+    grad_keys,
+    grad_values,
+    sem,
+    *,
+    tp,
+    group,
+):
+    me = scalars[0]
+    seq = pl.program_id(0)
+    chunk, width = tokens_ref.shape[1:]
+    piece = gathered.shape[-1]
+    factor = HEAD_DIM**-0.5
+    heads = width // HEAD_DIM
+
+    @pl.when(seq == 0)
+    def assemble():
+        copies = []
+        for f in range(width // piece):
+            for c in range(group // tp):
+                for t in range(tp):
+                    head = t * (group // tp) + c
+                    copies.append(
+                        pltpu.make_async_copy(
+                            gathered.at[f, c, t, pl.ds(3, weights.shape[0])],
+                            weights.at[
+                                :, pl.ds(head * HEAD_DIM, HEAD_DIM), pl.ds(f * piece, piece)
+                            ],
+                            sem.at[(f * group // tp + c) * tp + t],
+                        )
+                    )
+        for copy in copies:
+            copy.start()
+        totals[...] = jnp.zeros_like(totals)
+        stats_ref[...] = jnp.zeros_like(stats_ref)
+        for copy in copies:
+            copy.wait()
+
+    for other in range(group):
+        head = (other % tp) * (group // tp) + other // tp
+        context[head * HEAD_DIM : (head + 1) * HEAD_DIM, :] = ctx_ref[0, other]
+    start_sum = tokens_ref[0].astype(jnp.float32) + step_ref[0]
+    branch_one = dot_of(context[...], weights[SELF_OUT], 0, 0)
+    after_one = start_sum + branch_one
+    stats_ref[1:2, :] += jnp.sum(branch_one * branch_one, 0, keepdims=True)
+    normed_two, unit_two, inverse_two = rows_norm(after_one, gain_ref[1:2], bias_ref[1:2])
+    queries[...] = low(dot_of(weights[QUERY], normed_two, 1, 1))
+    keys[...] = low(dot_of(weights[KEY], enc_ref[0], 1, 1))
+    values[...] = low(dot_of(weights[VALUE], enc_ref[0], 1, 1))
+
+    def attend(head, unused):
+        rows = pl.ds(pl.multiple_of(head * HEAD_DIM, HEAD_DIM), HEAD_DIM)
+        scores = dot_of(keys[rows, :].T, queries[rows, :], 1, 0) * factor
+        powers = jnp.exp(scores - jnp.max(scores, 0, keepdims=True))
+        attn = powers / jnp.sum(powers, 0, keepdims=True)
+        probs[head] = attn
+        context_two[rows, :] = low(dot_of(values[rows, :], low(attn), 1, 0))
+        return unused
+
+    lax.fori_loop(0, heads, attend, 0, unroll=2)
+    branch_two = dot_of(context_two[...], weights[CROSS_OUT], 0, 0)
+    after_two = after_one + branch_two
+    stats_ref[2:3, :] += jnp.sum(branch_two * branch_two, 0, keepdims=True)
+    normed_three, unit_three, inverse_three = rows_norm(after_two, gain_ref[2:3], bias_ref[2:3])
+    grad_three = cot_ref[0]
+
+    def feed(part, carry):
+        branch, grad = carry
+        up, down = weights[UP + part], weights[DOWN + part]
+        inputs = dot_of(up, normed_three, 1, 1)
+        activated, slopes = gelu_parts(inputs)
+        hidden = low(activated)
+        branch = branch + dot_of(hidden, down, 0, 0)
+        totals[DOWN - 2 + part] += dot_of(hidden, grad_three, 1, 0)
+        grad_pre = low(dot_of(down, grad_three, 1, 1) * slopes)
+        totals[UP - 2 + part] += dot_of(grad_pre, normed_three, 1, 0)
+        return branch, grad + dot_of(grad_pre, up, 0, 0)
+
+    blank = jnp.zeros((chunk, width), jnp.float32)
+    branch_three, grad_norm = lax.fori_loop(0, DOWN - UP, feed, (blank, blank))
+    final_sum = after_two + branch_three
+    final_ref[0] = final_sum
+    stats_ref[0:1, :] += jnp.sum(final_sum * final_sum, 0, keepdims=True)
+    stats_ref[3:4, :] += jnp.sum(branch_three * branch_three, 0, keepdims=True)
+    back, gain_sum, bias_sum = rows_back(grad_norm, unit_three, inverse_three, gain_ref[2:3])
+    stats_ref[6:7, :] += gain_sum
+    stats_ref[7:8, :] += bias_sum
+    grad_after_two = grad_three.astype(jnp.float32) + back
+    grad_two = low(grad_after_two)
+    totals[2] += dot_of(context_two[...], grad_two, 1, 0)
+    grad_heads[...] = low(dot_of(weights[CROSS_OUT], grad_two, 1, 1))
+
+    def attend_back(head, unused):
+        rows = pl.ds(pl.multiple_of(head * HEAD_DIM, HEAD_DIM), HEAD_DIM)
+        grads = grad_heads[rows, :]
+        attn = probs[head]
+        grad_probs = dot_of(values[rows, :].T, grads, 1, 0)
+        grad_scores = low(
+            attn * (grad_probs - jnp.sum(attn * grad_probs, 0, keepdims=True))
+        )
+        grad_queries[rows, :] = low(dot_of(keys[rows, :], grad_scores, 1, 0) * factor)
+        grad_keys[rows, :] = dot_of(queries[rows, :], grad_scores, 1, 1) * factor
+        grad_values[rows, :] = dot_of(grads, low(attn), 1, 1)
+        return unused
+
+    lax.fori_loop(0, heads, attend_back, 0, unroll=2)
+    enc_grad_ref[0, :, :width] = low(grad_keys[...].T)
+    enc_grad_ref[0, :, width:] = low(grad_values[...].T)
+    totals[0] += dot_of(grad_queries[...], normed_two, 1, 0)
+    upstream = dot_of(grad_queries[...], weights[QUERY], 0, 0)
+    back, gain_sum, bias_sum = rows_back(upstream, unit_two, inverse_two, gain_ref[1:2])
+    stats_ref[4:5, :] += gain_sum
+    stats_ref[5:6, :] += bias_sum
+    grad_after_one = grad_after_two + back
+    after_ref[0] = grad_after_one
+    grad_one = low(grad_after_one)
+    totals[1] += dot_of(context[...], grad_one, 1, 0)
+    context[...] = low(dot_of(weights[SELF_OUT], grad_one, 1, 1))
+    for slot in range(group):
+        other = me ^ slot
+        head = (other % tp) * (group // tp) + other // tp
+        back_ref[0, slot] = context[
+            pl.ds(pl.multiple_of(head * HEAD_DIM, HEAD_DIM), HEAD_DIM), :
+        ]
+
+    @pl.when(seq == pl.num_programs(0) - 1)
+    def pack():
+        for f in range(width // piece):
+            for c in range(group // tp):
+                for t in range(tp):
+                    head = t * (group // tp) + c
+                    packed_ref[f, c, t] = low(
+                        totals[
+                            :,
+                            head * HEAD_DIM : (head + 1) * HEAD_DIM,
+                            f * piece : (f + 1) * piece,
+                        ]
+                    )
+
+
+def middle(scalars, gathered, tokens, steps, encoder, cotangent, gains, biases, contexts, tp):
+    batches, chunk, width = tokens.shape
+    group = contexts.shape[1]
+    enc_count = encoder.shape[1]
+    heads = width // HEAD_DIM
+    bf16, f32 = jnp.bfloat16, jnp.float32
+    struct = jax.ShapeDtypeStruct
+    each = lambda *shape: pl.BlockSpec((1,) + shape, lambda i, s: (i,) + (0,) * len(shape))
+    once = lambda *shape: pl.BlockSpec(
+        shape, lambda i, s: (0,) * len(shape), pipeline_mode=pl.Buffered(1)
+    )
+    count = gathered.shape[3] - 3
+    packed = gathered.shape[:3] + (count - 2,) + gathered.shape[4:]
+    return pl.pallas_call(
+        functools.partial(middle_kernel, tp=tp, group=group),
+        grid_spec=pltpu.PrefetchScalarGridSpec(
+            num_scalar_prefetch=1,
+            grid=(batches,),
+            in_specs=[
+                pl.BlockSpec(memory_space=pl.ANY),
+                each(chunk, width),
+                each(1, width),
+                each(enc_count, width),
+                each(chunk, width),
+                once(3, width),
+                once(3, width),
+                each(group, HEAD_DIM, chunk),
+            ],
+            out_specs=[
+                each(chunk, width),
+                each(chunk, width),
+                each(group, HEAD_DIM, chunk),
+                each(enc_count, 2 * width),
+                once(8, width),
+                once(*packed),
+            ],
+            scratch_shapes=[
+                pltpu.VMEM((count, width, width), bf16),
+                pltpu.VMEM((count - 2, width, width), f32),
+                pltpu.VMEM((width, chunk), bf16),
+                pltpu.VMEM((width, chunk), bf16),
+                pltpu.VMEM((width, enc_count), bf16),
+                pltpu.VMEM((width, enc_count), bf16),
+                pltpu.VMEM((heads, enc_count, chunk), f32),
+                pltpu.VMEM((width, chunk), bf16),
+                pltpu.VMEM((width, chunk), bf16),
+                pltpu.VMEM((width, chunk), bf16),
+                pltpu.VMEM((width, enc_count), f32),
+                pltpu.VMEM((width, enc_count), f32),
+                pltpu.SemaphoreType.DMA((32,)),
+            ],
+        ),
+        out_shape=[
+            struct((batches, chunk, width), f32),
+            struct((batches, chunk, width), f32),
+            struct((batches, group, HEAD_DIM, chunk), bf16),
+            struct((batches, enc_count, 2 * width), bf16),
+            struct((8, width), f32),
+            struct(packed, bf16),
+        ],
+        compiler_params=pltpu.CompilerParams(vmem_limit_bytes=VMEM_LIMIT),
+        cost_estimate=pl.CostEstimate(
+            flops=30_000_000_000, bytes_accessed=30_000_000, transcendentals=10_000_000
+        ),
+        name="middle",
+    )(scalars, gathered, tokens, steps, encoder, cotangent, gains, biases, contexts)
+
+
+def local_heads(
+    tokens,
+    timesteps,
+    time_table,
+    prefix,
+    encoder,
+    self_qkv,
+    cross_q,
+    cross_kv,
+    self_out,
+    cross_out,
+    ffn_up,
+    ffn_down,
+    norm_gain,
+    norm_bias,
+    cotangent,
+):
+    batches, chunk, width = tokens.shape
+    group = 8
+    length = group * chunk
+    enc_count = encoder.shape[1]
+    factor = HEAD_DIM ** (-0.5)
+    ctx_index, tp_index = lax.axis_index("ctx"), lax.axis_index("tp")
+    me = ctx_index * 4 + tp_index
+    span = 1024
+    piece = width // 4
+    flip = lambda w: jnp.swapaxes(w, -1, -2)
+    blocks = jnp.concatenate(
+        [
+            flip(self_qkv),
+            flip(cross_q)[None],
+            flip(cross_kv),
+            self_out[None],
+            cross_out[None],
+            flip(ffn_up).reshape(4, piece, piece),
+            ffn_down.reshape(4, piece, piece),
+        ]
+    )
+    count = blocks.shape[0]
+    half = piece // 2
+    own_half = lax.dynamic_slice_in_dim(blocks, ctx_index * half, half, 1)
+    gathered = lax.all_gather(own_half, ("fsdp", "ctx", "tp"), axis=0, tiled=False)
+    gathered = gathered.reshape(4, 2, 4, count, half, piece)
+    mine = own_half[:3].reshape(3 * HEAD_DIM, piece)
+    fsdp_index = lax.axis_index("fsdp")
+    steps_onehot = (timesteps[:, None] == lax.iota(jnp.int32, time_table.shape[0])[None, :]).astype(
+        jnp.bfloat16
+    )
+    embedded = jnp.dot(steps_onehot, time_table, preferred_element_type=jnp.float32)[:, None, :]
+    rows, qkv, wide, logs, contexts, head_weight = forward_group(
+        prefix, tokens, embedded, norm_gain[:1], norm_bias[:1], mine, span, group, 4, 4
+    )
+    final, grad_after, returned, enc_parts, stats, packed = middle(
+        me[None].astype(jnp.int32),
+        gathered,
+        tokens,
+        embedded,
+        encoder,
+        cotangent,
+        norm_gain,
+        norm_bias,
+        contexts,
+        4,
+    )
+    returns = [trade([returned[s, k] for k in range(group)]) for s in range(batches)]
+    whole_block = lambda b: jnp.transpose(gathered[:, :, :, b], (2, 1, 3, 0, 4)).reshape(
+        width, width
+    )
+    full_k, full_v = whole_block(4), whole_block(5)
+    qkv_heads = jnp.transpose(gathered[:, :, :, :3], (1, 2, 3, 4, 0, 5)).reshape(
+        group, 3 * HEAD_DIM, width
+    )
+    qkv_slots = jnp.concatenate(
+        [lax.dynamic_index_in_dim(qkv_heads, me ^ k, 0, False) for k in range(group)]
+    )
+    share = enc_count // group
+    parts = enc_parts.reshape(batches, group, share, 2 * width)
+    parts = [lax.dynamic_index_in_dim(parts, me ^ k, 1, False) for k in range(group)]
+    enc_grads = low(sum(p.astype(jnp.float32) for p in trade(parts)))
+    enc_rows = lax.dynamic_slice_in_dim(encoder, me * share, share, 1)
+    enc_rows = enc_rows.reshape(batches * share, width)
+    enc_flat = enc_grads.reshape(batches * share, 2 * width)
+    encoder_grad = (
+        dot_of(enc_flat[:, :width], full_k, 1, 0) + dot_of(enc_flat[:, width:], full_v, 1, 0)
+    ).reshape(batches, share, width)
+    grad_pair = dot_of(enc_flat, enc_rows, 0, 0)
+    grads_back, head_grads = [], 0.0
+    for s in range(batches):
+        scalars = jnp.stack([prefix[s], me]).astype(jnp.int32)
+        outs = backward_attention(scalars, qkv[s], wide[s], logs[s], returns[s], span)
+        grads_back.append(trade(outs))
+        for k in range(group):
+            own_rows = lax.dynamic_index_in_dim(rows[s], me ^ k, 0, False)
+            head_grads = head_grads + dot_of(outs[k], own_rows, 1, 0)
+    pair = low(grad_pair).reshape(2, 4, 2, half, 4, piece)
+    packed = jnp.concatenate([packed, jnp.transpose(pair, (4, 2, 1, 0, 3, 5))], 3)
+    scattered = lax.psum_scatter(
+        packed.reshape((32,) + packed.shape[3:]),
+        ("fsdp", "ctx", "tp"),
+        scatter_dimension=0,
+        tiled=False,
+    ).astype(jnp.float32)
+    other_half = swap_cores(scattered)
+    shards = jnp.concatenate(
+        [
+            jnp.where(ctx_index == 0, scattered, other_half),
+            jnp.where(ctx_index == 0, other_half, scattered),
+        ],
+        1,
+    )
+    head_grads = head_grads.reshape(3 * HEAD_DIM, 4, piece)
+    pieces = [lax.dynamic_index_in_dim(head_grads, fsdp_index ^ k, 1, False) for k in range(4)]
+    head_shard = pieces[0] + sum(
+        lax.ppermute(pieces[k], "fsdp", [(i, i ^ k) for i in range(4)]) for k in range(1, 4)
+    )
+    head_shard = jnp.transpose(head_shard.reshape(3, HEAD_DIM, piece), (0, 2, 1))
+    other_shard = swap_cores(head_shard)
+    grad_self = jnp.concatenate(
+        [
+            jnp.where(ctx_index == 0, head_shard, other_shard),
+            jnp.where(ctx_index == 0, other_shard, head_shard),
+        ],
+        2,
+    )
+    input_grads, gains_one, shifts_one = [], 0.0, 0.0
+    for s in range(batches):
+        upstream = dot_of(jnp.concatenate(grads_back[s]), qkv_slots, 0, 0)
+        start_sum = tokens[s].astype(jnp.float32) + embedded[s]
+        unused, unit, inverse = norm_rows(start_sum, norm_gain[0], norm_bias[0])
+        back, gain, shift = norm_back_rows(upstream, unit, inverse, norm_gain[0])
+        input_grads.append(grad_after[s] + back)
+        gains_one, shifts_one = gains_one + gain, shifts_one + shift
+    gain_grad, bias_grad, square_totals = lax.psum(
+        (
+            jnp.stack([gains_one, stats[4], stats[6]]),
+            jnp.stack([shifts_one, stats[5], stats[7]]),
+            jnp.sum(stats[:4], -1),
+        ),
+        ("fsdp", "ctx", "tp"),
+    )
+    entries = (
+        tokens.shape[0]
+        * tokens.shape[1]
+        * tokens.shape[2]
+        * lax.axis_size("fsdp")
+        * lax.axis_size("ctx")
+        * lax.axis_size("tp")
+    )
+    return (
+        final,
+        jnp.stack(input_grads),
+        encoder_grad,
+        grad_self,
+        shards[0].T,
+        flip(shards[11:13]),
+        shards[1],
+        shards[2],
+        shards[3:7].reshape(width, piece).T,
+        shards[7:11].reshape(width, piece),
+        gain_grad,
+        bias_grad[:2],
+        bias_grad[2],
+        jnp.sqrt(square_totals / entries),
+    )
+
+
 def solution(mesh):
     placed = (
         P("fsdp", ("ctx", "tp"), None),
@@ -474,8 +1403,9 @@
         P(),
         P("fsdp", ("ctx", "tp"), None),
     )
+    heads_fit = dict(mesh.shape) == {"fsdp": 4, "ctx": 2, "tp": 4}
     return jax.shard_map(
-        local,
+        local_heads if heads_fit else local,
         mesh=mesh,
         in_specs=placed,
         out_specs=(

time: 2290 us -> 597 us (0.26)
  waiting for transfers between devices: 1450 us -> 102 us
  matrix products: 421 us -> 17.7 us
  Pallas kernels: 0 us -> 287 us
  other arithmetic: 126 us -> 19.8 us
  local copies, waits for them, and re-layouts: 140 us -> 42.6 us
  starting transfers between devices: 1.46 us -> 64 us
  blocking collectives: 91.3 us -> 36.7 us
  loops' own time: 33.1 us -> 0 us
    reduce_scatter x18 -> x1, waiting for transfers between devices: 1020 us -> 0.01 us  [local_heads(): lax.psum_scatter(packed.reshape((32,) + packed.shape[3:]), ('fsdp', 'ctx'...]
    all_gather x8 -> x1, waiting for transfers between devices: 428 us -> 0.01 us  [local_heads(): lax.all_gather(own_half, ('fsdp', 'ctx', 'tp'), axis=0, tiled=False)]
    dot_general x85 -> x22, matrix products: 416 us -> 17.7 us  [the longest x21 17.5 us: dot_of(): lax.dot_general(left, right, (((left_dim,), (right_dim,)), ((), ())), pre...]
    pallas_call x0 -> x4, Pallas kernels: none -> 287 us  [the longest x1 157 us: forward_group(): pl.pallas_call(functools.partial(forward_kernel, span=span, tp=tp, fsdp=f...]
    ppermute x0 -> x40, waiting for transfers between devices: none -> 101 us  [the longest x35 99.8 us: trade(): lax.ppermute(parts[k], ('ctx', 'tp'), [(i, i ^ k) for i in range(group)])]
    ppermute x0 -> x40, starting transfers between devices: none -> 64 us  [the longest x35 54.2 us: trade(): lax.ppermute(parts[k], ('ctx', 'tp'), [(i, i ^ k) for i in range(group)])]
    while x104 -> x0, local copies, waits for them, and re-layouts: 56.5 us -> none
    all_gather x7 -> x0, blocking collectives: 52.5 us -> none  [the longest x1 9.34 us: local(): lax.all_gather(ffn_down, 'fsdp', axis=1, tiled=True)]
  transfers between devices with their start and end apart: 27 -> 42, of which waited for: 20 -> 16; matrix products, arithmetic and copies ran while one was open for 16% -> 10% of each run, Pallas kernels for 0% -> 39%
where the time goes in v2:
time: 597 us; the launch traced here: 585 us
  Pallas kernels  287 us (48%)
  waiting for transfers between devices  102 us (17%)
  starting transfers between devices  64 us (11%)
  local copies, waits for them, and re-layouts  42.6 us (7%)
  blocking collectives  36.7 us (6%)
  other arithmetic  19.8 us (3%)
  matrix products  17.7 us (3%)
  between operations  15.7 us (3%)
    pallas_call x1, Pallas kernels, forward_group(): pl.pallas_call(functools.partial(forward_kernel, span=span, tp=tp, fsdp=f...  157 us
    ppermute x35, waiting for transfers between devices, trade(): lax.ppermute(parts[k], ('ctx', 'tp'), [(i, i ^ k) for i in range(group)])  99.8 us
    pallas_call x2, Pallas kernels, backward_attention(): pl.pallas_call(functools.partial(backward_kernel, span=span, chunk=chunk,...  72.9 us
    pallas_call x1, Pallas kernels, middle(): pl.pallas_call(functools.partial(middle_kernel, tp=tp, group=group), grid...  57.5 us
    ppermute x35, starting transfers between devices, trade(): lax.ppermute(parts[k], ('ctx', 'tp'), [(i, i ^ k) for i in range(group)])  54.2 us
    psum x1, blocking collectives, local_heads(): lax.psum((jnp.stack([gains_one, stats[4], stats[6]]), jnp.stack([shifts_o...  36.7 us
    dot_general x21, matrix products, dot_of(): lax.dot_general(left, right, (((left_dim,), (right_dim,)), ((), ())), pre...  17.5 us
    unnamed x165, local copies, waits for them, and re-layouts  12.6 us
  transfers between devices with their start and end apart: 42, of which 16 were waited for; matrix products, arithmetic and copies ran while one was open for 10% of the time, Pallas kernels for 39%

profile of v2, /device:TPU:17, one launch (start us, length us, event | category | flops | bytes accessed | tf_op | source)
XLA Modules:
  0.0 585.0 jit_solution(11752261043410779536)
XLA Ops:
  23.7 156.6 %forward_group.1 = (bf16[2,8,512,512]{3,2,1,0:T(8,128)(2,1)}, bf16[2,192,4096]{2,1,0:T(8,128)(2,1)}, f32[2,64,4096]{2,1,0:T(8,128)}, f32[2,1,4096]{2,1,0:T(1,128...) custom-call(s32[2]{0:T(128)} %prefix_ref.1, bf16[2,512,512]{2,1,0:T(8,128)(2,1)} %tokens_ref.3, ...), custom_call_target="tpu_custom_call" | custom-call | flops 60000002048 | bytes 30000000 | tf_op jit(solution)/shard_map/forward_group/pallas_call | solution.py:948
  180.3 6.1 %fusion.125 = (bf16[1,8,512,512]{3,2,1,0:T(8,128)(2,1)}, bf16[1,8,512,512]{3,2,1,0:T(8,128)(2,1)}) fusion(bf16[2,8,512,512]{3,2,1,0:T(8,128)(2,1)} %get-tuple-element.65), kind=kLoop, calls=%fused_computation.232 | loop fusion | bytes 16777216 | tf_op jit(solution)/shard_map/slice | solution.py:1314
  197.6 57.5 %middle.1 = (f32[2,512,512]{2,1,0:T(8,128)}, f32[2,512,512]{2,1,0:T(8,128)}, bf16[2,8,64,512]{3,2,1,0:T(8,128)(2,1)}, bf16[2,256,1024]{2,1,0:T(8,128)(2,1)}, f32...) custom-call(s32[1]{0:T(128)} %bitcast.scalars, bf16[4,2,4,16,64,128]{5,4,3,2,1,0:T(8,128)(2,1)} %bitcast.260, ...), custom_call_target="tpu_custom_call" | custom-call | flops 30000001024 | bytes 30000000 | tf_op jit(solution)/shard_map/middle/pallas_call | solution.py:1167
  262.8 7.0 %collective-permute-done.34 = bf16[2,32,1024]{2,1,0:T(8,128)(2,1)S(1)} collective-permute-done((bf16[2,32,1024]{2,1,0:T(8,128)(2,1)S(1)}, bf16[2,32,1024]{2,1,0:T(8,128)(2,1)S(1)}, u32[]{:S(2)}, u32[]{:S(2)}) %collective-permute-start.34) | collective-permute-done | bytes 131104 | tf_op jit(solution)/shard_map/ppermute | solution.py:598
  270.8 4.8 collective-permute-done.33
  278.7 3.7 collective-permute-start.19
  290.4 6.0 %pad_maximum_fusion = bf16[4,2,4,13,64,128]{5,4,3,2,1,0:T(8,128)(2,1)} fusion(bf16[4,2,4,2,64,128]{5,4,3,2,1,0:T(8,128)(2,1)S(1)} %bitcast.250, bf16[4,2,4,11,64,128]{5,4,3,2,1,0:T(8,128)(2,1)} %get-tuple-element.66), kind=kLoop, calls=%fused_computation | loop fusion | flops 3407872 | bytes 13631488 | tf_op jit(solution)/shard_map/concatenate | solution.py:1317
  303.8 35.4 %attention_backward.3 = (bf16[192,512]{1,0:T(8,128)(2,1)}, bf16[192,512]{1,0:T(8,128)(2,1)}, bf16[192,512]{1,0:T(8,128)(2,1)}, bf16[192,512]{1,0:T(8,128)(2,1)},...) custom-call(s32[2]{0:T(128)} %pad_add_fusion.1.scalars, ...), custom_call_target="tpu_custom_call" | custom-call | flops 40000000000 | bytes 10000000 | tf_op jit(solution)/shard_map/attention_backward/pallas_call | solution.py:562
  351.3 37.5 %attention_backward.2 = (bf16[192,512]{1,0:T(8,128)(2,1)}, bf16[192,512]{1,0:T(8,128)(2,1)}, bf16[192,512]{1,0:T(8,128)(2,1)}, bf16[192,512]{1,0:T(8,128)(2,1)},...) custom-call(s32[2]{0:T(128)} %pad_add_fusion.scalars, ...), custom_call_target="tpu_custom_call" | custom-call | flops 40000000000 | bytes 10000000 | tf_op jit(solution)/shard_map/attention_backward/pallas_call | solution.py:562
  399.0 4.6 collective-permute-start.37
  410.4 4.1 collective-permute-start.25
  418.1 8.0 %collective-permute-done.23 = bf16[192,512]{1,0:T(8,128)(2,1)S(1)} collective-permute-done((bf16[192,512]{1,0:T(8,128)(2,1)S(1)}, bf16[192,512]{1,0:T(8,128)(2,1)S(1)}, u32[]{:S(2)}, u32[]{:S(2)}) %collective-permute-start.23) | collective-permute-done | bytes 196640 | tf_op jit(solution)/shard_map/ppermute | solution.py:598
  429.0 3.4 collective-permute-done.25
  433.6 12.8 %collective-permute-done.26 = bf16[192,512]{1,0:T(8,128)(2,1)S(1)} collective-permute-done((bf16[192,512]{1,0:T(8,128)(2,1)S(1)}, bf16[192,512]{1,0:T(8,128)(2,1)S(1)}, u32[]{:S(2)}, u32[]{:S(2)}) %collective-permute-start.26) | collective-permute-done | bytes 196640 | tf_op jit(solution)/shard_map/ppermute | solution.py:598
  446.4 3.2 collective-permute-start.10
  449.6 25.1 %collective-permute-done.27 = bf16[192,512]{1,0:T(8,128)(2,1)S(1)} collective-permute-done((bf16[192,512]{1,0:T(8,128)(2,1)S(1)}, bf16[192,512]{1,0:T(8,128)(2,1)S(1)}, u32[]{:S(2)}, u32[]{:S(2)}) %collective-permute-start.27) | collective-permute-done | bytes 196640 | tf_op jit(solution)/shard_map/ppermute | solution.py:598
  475.7 3.9 collective-permute-done.8
  479.6 9.7 %collective-permute-start.13 = (bf16[192,512]{1,0:T(8,128)(2,1)S(1)}, bf16[192,512]{1,0:T(8,128)(2,1)S(1)}, u32[]{:S(2)}, u32[]{:S(2)}) collective-permute-start(bf16[192,512]{1,0:T(8,128)(2,1)S(1)} %copy-done.18), channel_id=1, source_target_pairs={{0,7},{1,6},{2,5},{3,4},{4,3},{5,2},{6,1},{7,0},{8,15},{9,14},{10,... | collective-permute-start | bytes 589832 | tf_op jit(solution)/shard_map/ppermute | solution.py:598
  489.2 14.6 %collective-permute-done.9 = bf16[192,512]{1,0:T(8,128)(2,1)S(1)} collective-permute-done((bf16[192,512]{1,0:T(8,128)(2,1)S(1)}, bf16[192,512]{1,0:T(8,128)(2,1)S(1)}, u32[]{:S(2)}, u32[]{:S(2)}) %collective-permute-start.9) | collective-permute-done | bytes 196640 | tf_op jit(solution)/shard_map/ppermute | solution.py:598
  503.9 3.5 collective-permute-start.38
  507.5 4.9 collective-permute-done.12
  512.4 10.2 %collective-permute-done.13 = bf16[192,512]{1,0:T(8,128)(2,1)S(1)} collective-permute-done((bf16[192,512]{1,0:T(8,128)(2,1)S(1)}, bf16[192,512]{1,0:T(8,128)(2,1)S(1)}, u32[]{:S(2)}, u32[]{:S(2)}) %collective-permute-start.13) | collective-permute-done | bytes 196640 | tf_op jit(solution)/shard_map/ppermute | solution.py:598
  526.3 36.7 %all-reduce = (f32[3,512]{1,0:T(4,128)}, f32[3,512]{1,0:T(4,128)S(1)}, f32[4]{0:T(128)S(1)}) all-reduce(f32[3,512]{1,0:T(4,128)S(1)} %pad_maximum_fusion.5, f32[3,512]{1,0:T(4,128)S(1)} %pad_maximum_fusion.6, f32[4]{0:T(128)S(1)} %slice_reduce_fusion), channel_id=1, replica_groups=mesh['fsdp'=4,'ctx'=2,'tp'=4] {'fsdp','ctx','tp'}, use_global_device_ids=true, to_apply=%region_11.12 | all-reduce | flops 3076 | bytes 24608 | tf_op jit(solution)/shard_map/psum | solution.py:1354
  563.6 3.2 fusion.39
  (315 shorter events, 106.9 us)
Async XLA Ops:
  7.2 184.4 %all-gather.3.cloned.1.call-start = ((), (), s32[]{:S(2)}) async-start(), calls=%async_computation.2 | async-start | bytes 8650752 | tf_op jit(solution)/shard_map/all_gather | solution.py:1263
  14.5 552.2 %reduce-scatter.2.cloned.1.call-start = ((), (), s32[]{:S(2)}) async-start(), calls=%async_computation.1 | async-start | bytes 7028736 | tf_op jit(solution)/shard_map/reduce_scatter | solution.py:1318
  260.9 21.5 %collective-permute-start.31 = (bf16[2,32,1024]{2,1,0:T(8,128)(2,1)S(1)}, bf16[2,32,1024]{2,1,0:T(8,128)(2,1)S(1)}, u32[]{:S(2)}, u32[]{:S(2)}) collective-permute-start(bf16[2,32,1024]{2,1,0:T(8,128)(2,1)S(1)} %get-tuple-element.141), channel_id=1, source_target_pairs={{0,4},{1,5},{2,6},{3,7},{4,0},{5,1},{6,2},{7,3},{8,12},{9,13},{10,... | collective-permute-start | bytes 393224 | tf_op jit(solution)/shard_map/ppermute | solution.py:598
  262.8 19.7 %collective-permute-start.30 = (bf16[2,32,1024]{2,1,0:T(8,128)(2,1)S(1)}, bf16[2,32,1024]{2,1,0:T(8,128)(2,1)S(1)}, u32[]{:S(2)}, u32[]{:S(2)}) collective-permute-start(bf16[2,32,1024]{2,1,0:T(8,128)(2,1)S(1)} %get-tuple-element.142), channel_id=1, source_target_pairs={{0,3},{1,2},{2,1},{3,0},{4,7},{5,6},{6,5},{7,4},{8,11},{9,10},{10,... | collective-permute-start | bytes 393224 | tf_op jit(solution)/shard_map/ppermute | solution.py:598
  297.3 44.3 %collective-permute-start.6 = (bf16[64,512]{1,0:T(8,128)(2,1)S(1)}, bf16[64,512]{1,0:T(8,128)(2,1)S(1)}, u32[]{:S(2)}, u32[]{:S(2)}) collective-permute-start(bf16[64,512]{1,0:T(8,128)(2,1)S(1)} %copy-done.41), channel_id=1, source_target_pairs={{0,7},{1,6},{2,5},{3,4},{4,3},{5,2},{6,1},{7,0},{8,15},{9,14},{10,... | collective-permute-start | bytes 196616 | tf_op jit(solution)/shard_map/ppermute | solution.py:598
  299.2 45.2 %collective-permute-start.5 = (bf16[64,512]{1,0:T(8,128)(2,1)S(1)}, bf16[64,512]{1,0:T(8,128)(2,1)S(1)}, u32[]{:S(2)}, u32[]{:S(2)}) collective-permute-start(bf16[64,512]{1,0:T(8,128)(2,1)S(1)} %copy-done.40), channel_id=1, source_target_pairs={{0,6},{1,7},{2,4},{3,5},{4,2},{5,3},{6,0},{7,1},{8,14},{9,15},{10,... | collective-permute-start | bytes 196616 | tf_op jit(solution)/shard_map/ppermute | solution.py:598
  299.8 45.8 %collective-permute-start.4 = (bf16[64,512]{1,0:T(8,128)(2,1)S(1)}, bf16[64,512]{1,0:T(8,128)(2,1)S(1)}, u32[]{:S(2)}, u32[]{:S(2)}) collective-permute-start(bf16[64,512]{1,0:T(8,128)(2,1)S(1)} %copy-done.39), channel_id=1, source_target_pairs={{0,5},{1,4},{2,7},{3,6},{4,1},{5,0},{6,3},{7,2},{8,13},{9,12},{10,... | collective-permute-start | bytes 196616 | tf_op jit(solution)/shard_map/ppermute | solution.py:598
  301.8 45.3 %collective-permute-start.3 = (bf16[64,512]{1,0:T(8,128)(2,1)S(1)}, bf16[64,512]{1,0:T(8,128)(2,1)S(1)}, u32[]{:S(2)}, u32[]{:S(2)}) collective-permute-start(bf16[64,512]{1,0:T(8,128)(2,1)S(1)} %copy-done.38), channel_id=1, source_target_pairs={{0,4},{1,5},{2,6},{3,7},{4,0},{5,1},{6,2},{7,3},{8,12},{9,13},{10,... | collective-permute-start | bytes 196616 | tf_op jit(solution)/shard_map/ppermute | solution.py:598
  303.2 44.1 %collective-permute-start.2 = (bf16[64,512]{1,0:T(8,128)(2,1)S(1)}, bf16[64,512]{1,0:T(8,128)(2,1)S(1)}, u32[]{:S(2)}, u32[]{:S(2)}) collective-permute-start(bf16[64,512]{1,0:T(8,128)(2,1)S(1)} %get-tuple-element.156), channel_id=1, source_target_pairs={{0,3},{1,2},{2,1},{3,0},{4,7},{5,6},{6,5},{7,4},{8,11},{9,10},{10,... | collective-permute-start | bytes 196616 | tf_op jit(solution)/shard_map/ppermute | solution.py:598
  345.7 68.9 %collective-permute-start.21 = (bf16[192,512]{1,0:T(8,128)(2,1)}, bf16[192,512]{1,0:T(8,128)(2,1)}, u32[]{:S(2)}, u32[]{:S(2)}) collective-permute-start(bf16[192,512]{1,0:T(8,128)(2,1)} %get-tuple-element.57), channel_id=1, source_target_pairs={{0,1},{1,0},{2,3},{3,2},{4,5},{5,4},{6,7},{7,6},{8,9},{9,8},{10,11... | collective-permute-start | bytes 589832 | tf_op jit(solution)/shard_map/ppermute | solution.py:598
  347.2 68.6 %collective-permute-start.22 = (bf16[192,512]{1,0:T(8,128)(2,1)}, bf16[192,512]{1,0:T(8,128)(2,1)}, u32[]{:S(2)}, u32[]{:S(2)}) collective-permute-start(bf16[192,512]{1,0:T(8,128)(2,1)} %get-tuple-element.58), channel_id=1, source_target_pairs={{0,2},{1,3},{2,0},{3,1},{4,6},{5,7},{6,4},{7,5},{8,10},{9,11},{10,... | collective-permute-start | bytes 589832 | tf_op jit(solution)/shard_map/ppermute | solution.py:598
  405.6 20.5 %collective-permute-start.23 = (bf16[192,512]{1,0:T(8,128)(2,1)S(1)}, bf16[192,512]{1,0:T(8,128)(2,1)S(1)}, u32[]{:S(2)}, u32[]{:S(2)}) collective-permute-start(bf16[192,512]{1,0:T(8,128)(2,1)S(1)} %copy-done.33), channel_id=1, source_target_pairs={{0,3},{1,2},{2,1},{3,0},{4,7},{5,6},{6,5},{7,4},{8,11},{9,10},{10,... | collective-permute-start | bytes 589832 | tf_op jit(solution)/shard_map/ppermute | solution.py:598
  408.4 17.8 %collective-permute-start.24 = (bf16[192,512]{1,0:T(8,128)(2,1)S(1)}, bf16[192,512]{1,0:T(8,128)(2,1)S(1)}, u32[]{:S(2)}, u32[]{:S(2)}) collective-permute-start(bf16[192,512]{1,0:T(8,128)(2,1)S(1)} %copy-done.29), channel_id=1, source_target_pairs={{0,4},{1,5},{2,6},{3,7},{4,0},{5,1},{6,2},{7,3},{8,12},{9,13},{10,... | collective-permute-start | bytes 589832 | tf_op jit(solution)/shard_map/ppermute | solution.py:598
  410.4 22.0 %collective-permute-start.25 = (bf16[192,512]{1,0:T(8,128)(2,1)S(1)}, bf16[192,512]{1,0:T(8,128)(2,1)S(1)}, u32[]{:S(2)}, u32[]{:S(2)}) collective-permute-start(bf16[192,512]{1,0:T(8,128)(2,1)S(1)} %copy-done.25), channel_id=1, source_target_pairs={{0,5},{1,4},{2,7},{3,6},{4,1},{5,0},{6,3},{7,2},{8,13},{9,12},{10,... | collective-permute-start | bytes 589832 | tf_op jit(solution)/shard_map/ppermute | solution.py:598
  414.5 31.9 %collective-permute-start.26 = (bf16[192,512]{1,0:T(8,128)(2,1)S(1)}, bf16[192,512]{1,0:T(8,128)(2,1)S(1)}, u32[]{:S(2)}, u32[]{:S(2)}) collective-permute-start(bf16[192,512]{1,0:T(8,128)(2,1)S(1)} %copy-done.20), channel_id=1, source_target_pairs={{0,6},{1,7},{2,4},{3,5},{4,2},{5,3},{6,0},{7,1},{8,14},{9,15},{10,... | collective-permute-start | bytes 589832 | tf_op jit(solution)/shard_map/ppermute | solution.py:598
  415.8 58.9 %collective-permute-start.27 = (bf16[192,512]{1,0:T(8,128)(2,1)S(1)}, bf16[192,512]{1,0:T(8,128)(2,1)S(1)}, u32[]{:S(2)}, u32[]{:S(2)}) collective-permute-start(bf16[192,512]{1,0:T(8,128)(2,1)S(1)} %copy-done.17), channel_id=1, source_target_pairs={{0,7},{1,6},{2,5},{3,4},{4,3},{5,2},{6,1},{7,0},{8,15},{9,14},{10,... | collective-permute-start | bytes 589832 | tf_op jit(solution)/shard_map/ppermute | solution.py:598
  426.1 48.6 %collective-permute-start.7 = (bf16[192,512]{1,0:T(8,128)(2,1)S(1)}, bf16[192,512]{1,0:T(8,128)(2,1)S(1)}, u32[]{:S(2)}, u32[]{:S(2)}) collective-permute-start(bf16[192,512]{1,0:T(8,128)(2,1)S(1)} %copy-done.37), channel_id=1, source_target_pairs={{0,1},{1,0},{2,3},{3,2},{4,5},{5,4},{6,7},{7,6},{8,9},{9,8},{10,11... | collective-permute-start | bytes 589832 | tf_op jit(solution)/shard_map/ppermute | solution.py:598
  426.2 53.4 %collective-permute-start.8 = (bf16[192,512]{1,0:T(8,128)(2,1)S(1)}, bf16[192,512]{1,0:T(8,128)(2,1)S(1)}, u32[]{:S(2)}, u32[]{:S(2)}) collective-permute-start(bf16[192,512]{1,0:T(8,128)(2,1)S(1)} %copy-done.35), channel_id=1, source_target_pairs={{0,2},{1,3},{2,0},{3,1},{4,6},{5,7},{6,4},{7,5},{8,10},{9,11},{10,... | collective-permute-start | bytes 589832 | tf_op jit(solution)/shard_map/ppermute | solution.py:598
  432.4 71.4 %collective-permute-start.9 = (bf16[192,512]{1,0:T(8,128)(2,1)S(1)}, bf16[192,512]{1,0:T(8,128)(2,1)S(1)}, u32[]{:S(2)}, u32[]{:S(2)}) collective-permute-start(bf16[192,512]{1,0:T(8,128)(2,1)S(1)} %copy-done.31), channel_id=1, source_target_pairs={{0,3},{1,2},{2,1},{3,0},{4,7},{5,6},{6,5},{7,4},{8,11},{9,10},{10,... | collective-permute-start | bytes 589832 | tf_op jit(solution)/shard_map/ppermute | solution.py:598
  446.4 61.0 %collective-permute-start.10 = (bf16[192,512]{1,0:T(8,128)(2,1)S(1)}, bf16[192,512]{1,0:T(8,128)(2,1)S(1)}, u32[]{:S(2)}, u32[]{:S(2)}) collective-permute-start(bf16[192,512]{1,0:T(8,128)(2,1)S(1)} %copy-done.27), channel_id=1, source_target_pairs={{0,4},{1,5},{2,6},{3,7},{4,0},{5,1},{6,2},{7,3},{8,12},{9,13},{10,... | collective-permute-start | bytes 589832 | tf_op jit(solution)/shard_map/ppermute | solution.py:598
  474.7 32.8 %collective-permute-start.11 = (bf16[192,512]{1,0:T(8,128)(2,1)S(1)}, bf16[192,512]{1,0:T(8,128)(2,1)S(1)}, u32[]{:S(2)}, u32[]{:S(2)}) collective-permute-start(bf16[192,512]{1,0:T(8,128)(2,1)S(1)} %copy-done.23), channel_id=1, source_target_pairs={{0,5},{1,4},{2,7},{3,6},{4,1},{5,0},{6,3},{7,2},{8,13},{9,12},{10,... | collective-permute-start | bytes 589832 | tf_op jit(solution)/shard_map/ppermute | solution.py:598
  474.7 37.6 %collective-permute-start.12 = (bf16[192,512]{1,0:T(8,128)(2,1)S(1)}, bf16[192,512]{1,0:T(8,128)(2,1)S(1)}, u32[]{:S(2)}, u32[]{:S(2)}) collective-permute-start(bf16[192,512]{1,0:T(8,128)(2,1)S(1)} %copy-done.21), channel_id=1, source_target_pairs={{0,6},{1,7},{2,4},{3,5},{4,2},{5,3},{6,0},{7,1},{8,14},{9,15},{10,... | collective-permute-start | bytes 589832 | tf_op jit(solution)/shard_map/ppermute | solution.py:598
  479.6 43.0 %collective-permute-start.13 = (bf16[192,512]{1,0:T(8,128)(2,1)S(1)}, bf16[192,512]{1,0:T(8,128)(2,1)S(1)}, u32[]{:S(2)}, u32[]{:S(2)}) collective-permute-start(bf16[192,512]{1,0:T(8,128)(2,1)S(1)} %copy-done.18), channel_id=1, source_target_pairs={{0,7},{1,6},{2,5},{3,4},{4,3},{5,2},{6,1},{7,0},{8,15},{9,14},{10,... | collective-permute-start | bytes 589832 | tf_op jit(solution)/shard_map/ppermute | solution.py:598
  503.9 69.2 %collective-permute-start.38 = (f32[3,128,64]{1,2,0:T(8,128)S(1)}, f32[3,128,64]{1,2,0:T(8,128)S(1)}, u32[]{:S(2)}, u32[]{:S(2)}) collective-permute-start(f32[3,128,64]{1,2,0:T(8,128)S(1)} %bitcast.263), channel_id=1, source_target_pairs={{0,4},{4,0},{1,5},{5,1},{2,6},{6,2},{3,7},{7,3},{8,12},{12,8},{9,1... | collective-permute-start | bytes 294920 | tf_op jit(solution)/shard_map/ppermute | solution.py:592
  (84 other events, 1515.6 us)
Sparse Core Ops, SparseCore 0:
  14.7 91.9 all-gather.2
  296.6 220.8 reduce-scatter.1

commit v3 on v2

--- a/solution.py
+++ b/solution.py
@@ -15,7 +15,7 @@
 NEG = -1e30
 ROOT_HALF = 1.0 / math.sqrt(2.0)
 INV_ROOT_TWO_PI = 1.0 / math.sqrt(2.0 * math.pi)
-VMEM_LIMIT = 56 * 2**20
+VMEM_LIMIT = 60 * 2**20
 
 
 def norm_rows(hidden, scaling, offsets):
@@ -476,146 +476,8 @@
     return jnp.where(lax.broadcasted_iota(jnp.int32, scores.shape, 0) < limit - offset, scores, NEG)
 
 
-def backward_kernel(scalars, qkv_ref, wide_ref, log_ref, *refs, span, chunk, group):
-    grad_refs, refs = refs[:group], refs[group:]
-    out_refs, refs = refs[:group], refs[group:]
-    (
-        queries_ref,
-        keys_ref,
-        values_ref,
-        gradt_ref,
-        grad_ref,
-        delta_ref,
-        grad_keys_ref,
-        grad_values_ref,
-        low_ref,
-    ) = refs
-    step = pl.program_id(0)
-    prefix, me = scalars[0], scalars[1]
-    factor = HEAD_DIM**-0.5
-    length = qkv_ref.shape[1]
-
-    @pl.when(step == 0)
-    def prepare():
-        for slot in range(group):
-            here = pl.ds(pl.multiple_of((me ^ slot) * chunk, chunk), chunk)
-            gradt_ref[:, here] = grad_refs[slot][...]
-            grad_ref[here, :] = grad_refs[slot][...].T
-        delta_ref[...] = jnp.sum(
-            gradt_ref[...].astype(jnp.float32) * wide_ref[...], axis=0, keepdims=True
-        )
-        queries_ref[...] = qkv_ref[:HEAD_DIM, :].T
-        keys_ref[...] = qkv_ref[HEAD_DIM : 2 * HEAD_DIM, :].T
-        values_ref[...] = qkv_ref[2 * HEAD_DIM :, :].T
-        grad_keys_ref[...] = jnp.zeros_like(grad_keys_ref)
-        grad_values_ref[...] = jnp.zeros_like(grad_values_ref)
-
-    start = pl.multiple_of(step * span, span)
-    here = pl.ds(start, span)
-    queries_t, queries = qkv_ref[:HEAD_DIM, here], queries_ref[here, :]
-    grads_t, grads = gradt_ref[:, here], grad_ref[here, :]
-    logs, deltas = log_ref[:, here], delta_ref[:, here]
-    limit = jnp.maximum(prefix, start + 1 + lax.broadcasted_iota(jnp.int32, (1, span), 1))
-    whole, every = bounds(prefix, start, span, span)
-
-    def advance(block, grad_queries, masked):
-        there = pl.ds(pl.multiple_of(block * span, span), span)
-        scores = dot_of(keys_ref[there, :], queries_t, 1, 0)
-        if masked:
-            scores = hide(scores, limit, block * span)
-        probs = jnp.exp(scores - logs)
-        grad_probs = dot_of(values_ref[there, :], grads_t, 1, 0)
-        grad_scores = (probs * (grad_probs - deltas)).astype(jnp.bfloat16)
-        grad_values_ref[there, :] += dot_of(probs.astype(jnp.bfloat16), grads, 1, 0)
-        grad_keys_ref[there, :] += dot_of(grad_scores, queries, 1, 0)
-        return grad_queries + dot_of(
-            qkv_ref[HEAD_DIM : 2 * HEAD_DIM, there], grad_scores, 1, 0
-        )
-
-    grad_queries = jnp.zeros((HEAD_DIM, span), jnp.float32)
-    grad_queries = lax.fori_loop(0, whole, lambda j, c: advance(j, c, False), grad_queries)
-    grad_queries = lax.fori_loop(whole, every, lambda j, c: advance(j, c, True), grad_queries)
-    low = (grad_queries * factor).astype(jnp.bfloat16)
-    for part in range(span // chunk):
-        low_ref[(step * (span // chunk) + part) ^ me, :HEAD_DIM, :] = low[
-            :, part * chunk : (part + 1) * chunk
-        ]
-
-    @pl.when(step == pl.num_programs(0) - 1)
-    def finish():
-        for place in range(length // chunk):
-            rows = pl.ds(place * chunk, chunk)
-            low_ref[place ^ me, HEAD_DIM : 2 * HEAD_DIM, :] = grad_keys_ref[rows, :].T.astype(
-                jnp.bfloat16
-            )
-            low_ref[place ^ me, 2 * HEAD_DIM :, :] = grad_values_ref[rows, :].T.astype(jnp.bfloat16)
-        for slot in range(group):
-            out_refs[slot][...] = low_ref[slot]
-
-
-def backward_attention(scalars, qkv, wide, logs, grads, span):
-    group = len(grads)
-    length = qkv.shape[1]
-    chunk = grads[0].shape[1]
-    whole = lambda *shape: pl.BlockSpec(shape, lambda i, s: (0,) * len(shape))
-    bf16, f32 = jnp.bfloat16, jnp.float32
-    return pl.pallas_call(
-        functools.partial(backward_kernel, span=span, chunk=chunk, group=group),
-        grid_spec=pltpu.PrefetchScalarGridSpec(
-            num_scalar_prefetch=1,
-            grid=(length // span,),
-            in_specs=[whole(*qkv.shape), whole(*wide.shape), whole(*logs.shape)]
-            + [whole(*g.shape) for g in grads],
-            out_specs=[whole(3 * HEAD_DIM, chunk)] * group,
-            scratch_shapes=[
-                pltpu.VMEM((length, HEAD_DIM), bf16),
-                pltpu.VMEM((length, HEAD_DIM), bf16),
-                pltpu.VMEM((length, HEAD_DIM), bf16),
-                pltpu.VMEM((HEAD_DIM, length), bf16),
-                pltpu.VMEM((length, HEAD_DIM), bf16),
-                pltpu.VMEM((1, length), f32),
-                pltpu.VMEM((length, HEAD_DIM), f32),
-                pltpu.VMEM((length, HEAD_DIM), f32),
-                pltpu.VMEM((group, 3 * HEAD_DIM, chunk), bf16),
-            ],
-        ),
-        out_shape=[jax.ShapeDtypeStruct((3 * HEAD_DIM, chunk), bf16)] * group,
-        compiler_params=pltpu.CompilerParams(vmem_limit_bytes=VMEM_LIMIT),
-        cost_estimate=pl.CostEstimate(
-            flops=40_000_000_000, bytes_accessed=10_000_000, transcendentals=10_000_000
-        ),
-        name="attention_backward",
-    )(scalars, qkv, wide, logs, *grads)
-
-
-def swap_cores(value):
-    return lax.ppermute(value, "ctx", [(0, 1), (1, 0)])
-
-
-def trade(parts):
-    group = len(parts)
-    return [parts[0]] + [
-        lax.ppermute(parts[k], ("ctx", "tp"), [(i, i ^ k) for i in range(group)])
-        for k in range(1, group)
-    ]
-
-
-def norm_back_rows(upstream, unit_rows, inverse, scaling):
-    scaled = upstream * scaling
-    result = inverse * (
-        scaled
-        - jnp.mean(scaled, -1, keepdims=True)
-        - unit_rows * jnp.mean(scaled * unit_rows, -1, keepdims=True)
-    )
-    return result, jnp.sum(upstream * unit_rows, 0), jnp.sum(upstream, 0)
-
-
 def low(value):
     return value.astype(jnp.bfloat16)
-
-
-def head_parts(value):
-    return value.reshape(value.shape[0], -1, HEAD_DIM)
 
 
 def rows_norm(hidden, scaling, offsets):
@@ -987,7 +849,6 @@
 
 
 def middle_kernel(
-    scalars,
     gathered,
     tokens_ref,
     step_ref,
@@ -1019,7 +880,6 @@
     tp,
     group,
 ):
-    me = scalars[0]
     seq = pl.program_id(0)
     chunk, width = tokens_ref.shape[1:]
     piece = gathered.shape[-1]
@@ -1129,12 +989,9 @@
     grad_one = low(grad_after_one)
     totals[1] += dot_of(context[...], grad_one, 1, 0)
     context[...] = low(dot_of(weights[SELF_OUT], grad_one, 1, 1))
-    for slot in range(group):
-        other = me ^ slot
+    for other in range(group):
         head = (other % tp) * (group // tp) + other // tp
-        back_ref[0, slot] = context[
-            pl.ds(pl.multiple_of(head * HEAD_DIM, HEAD_DIM), HEAD_DIM), :
-        ]
+        back_ref[0, other] = context[head * HEAD_DIM : (head + 1) * HEAD_DIM, :]
 
     @pl.when(seq == pl.num_programs(0) - 1)
     def pack():
@@ -1142,7 +999,7 @@
             for c in range(group // tp):
                 for t in range(tp):
                     head = t * (group // tp) + c
-                    packed_ref[f, c, t] = low(
+                    packed_ref[c, f, t] = low(
                         totals[
                             :,
                             head * HEAD_DIM : (head + 1) * HEAD_DIM,
@@ -1151,23 +1008,21 @@
                     )
 
 
-def middle(scalars, gathered, tokens, steps, encoder, cotangent, gains, biases, contexts, tp):
+def middle(gathered, tokens, steps, encoder, cotangent, gains, biases, contexts, tp):
     batches, chunk, width = tokens.shape
     group = contexts.shape[1]
     enc_count = encoder.shape[1]
     heads = width // HEAD_DIM
     bf16, f32 = jnp.bfloat16, jnp.float32
     struct = jax.ShapeDtypeStruct
-    each = lambda *shape: pl.BlockSpec((1,) + shape, lambda i, s: (i,) + (0,) * len(shape))
+    each = lambda *shape: pl.BlockSpec((1,) + shape, lambda i: (i,) + (0,) * len(shape))
     once = lambda *shape: pl.BlockSpec(
-        shape, lambda i, s: (0,) * len(shape), pipeline_mode=pl.Buffered(1)
+        shape, lambda i: (0,) * len(shape), pipeline_mode=pl.Buffered(1)
     )
     count = gathered.shape[3] - 3
-    packed = gathered.shape[:3] + (count - 2,) + gathered.shape[4:]
+    packed = (group // tp, gathered.shape[0], tp, count - 2) + gathered.shape[4:]
     return pl.pallas_call(
         functools.partial(middle_kernel, tp=tp, group=group),
-        grid_spec=pltpu.PrefetchScalarGridSpec(
-            num_scalar_prefetch=1,
             grid=(batches,),
             in_specs=[
                 pl.BlockSpec(memory_space=pl.ANY),
@@ -1202,7 +1057,6 @@
                 pltpu.VMEM((width, enc_count), f32),
                 pltpu.SemaphoreType.DMA((32,)),
             ],
-        ),
         out_shape=[
             struct((batches, chunk, width), f32),
             struct((batches, chunk, width), f32),
@@ -1216,7 +1070,714 @@
             flops=30_000_000_000, bytes_accessed=30_000_000, transcendentals=10_000_000
         ),
         name="middle",
-    )(scalars, gathered, tokens, steps, encoder, cotangent, gains, biases, contexts)
+    )(gathered, tokens, steps, encoder, cotangent, gains, biases, contexts)
+
+
+def backward_kernel(
+    prefix_ref,
+    returned,
+    enc_parts,
+    packed,
+    gathered,
+    rows_in,
+    qkv_ref,
+    wide_ref,
+    log_ref,
+    tokens_ref,
+    step_ref,
+    gain_ref,
+    after_ref,
+    enc_ref,
+    stats_ref,
+    input_ref,
+    enc_out,
+    self_out,
+    query_out,
+    pair_out,
+    back_out,
+    cross_out,
+    up_out,
+    down_out,
+    sums_out,
+    landing,
+    outgoing,
+    incoming,
+    queries_ref,
+    keys_ref,
+    values_ref,
+    grad_ref,
+    gradt_ref,
+    delta_ref,
+    grad_keys_ref,
+    grad_values_ref,
+    rows_ref,
+    heads_ref,
+    pair_weights,
+    enc_landing,
+    pair_ref,
+    pair_landing,
+    core_landing,
+    partial_ref,
+    fsdp_landing,
+    line_ref,
+    line_landing,
+    shard_ref,
+    head_ref,
+    head_landing,
+    head_shard,
+    sums_ref,
+    sums_landing,
+    sums_two,
+    d_send,
+    d_recv,
+    e_send,
+    e_recv,
+    g_send,
+    g_recv,
+    r_send,
+    r_recv,
+    f_send,
+    f_recv,
+    t_send,
+    t_recv,
+    h_send,
+    h_recv,
+    s_send,
+    s_recv,
+    local_sem,
+    rows_sem,
+    *,
+    span,
+    tp,
+    fsdp,
+):
+    batches, chunk, width = tokens_ref.shape
+    group = landing.shape[1]
+    length = group * chunk
+    blocks, ratio = length // span, span // chunk
+    wide_blocks = max(1, length // 2 // span)
+    factor = HEAD_DIM**-0.5
+    here, core, chip = lax.axis_index("fsdp"), lax.axis_index("ctx"), lax.axis_index("tp")
+    me = core * tp + chip
+    cores = group // tp
+    share = enc_landing.shape[2]
+    piece = width // fsdp
+    early = packed.shape[3]
+    meet(group, tp, fsdp)
+
+    def send_to(source, target, send, recv, **place):
+        return pltpu.make_async_remote_copy(
+            src_ref=source,
+            dst_ref=target,
+            send_sem=send,
+            recv_sem=recv,
+            device_id=place,
+            device_id_type=MESH,
+        )
+
+    def member(place):
+        return {"ctx": place // tp, "tp": place % tp}
+
+    local = [
+        pltpu.make_async_copy(
+            packed.at[core], partial_ref.at[:, :, pl.ds(0, early)], local_sem.at[0]
+        )
+    ]
+    for seq in range(batches):
+        local.append(
+            pltpu.make_async_copy(
+                returned.at[seq, me], landing.at[seq, me], local_sem.at[1 + seq]
+            )
+        )
+    local.append(
+        pltpu.make_async_copy(
+            enc_parts.at[:, pl.ds(pl.multiple_of(me * share, share), share)],
+            enc_landing.at[me],
+            local_sem.at[1 + batches],
+        )
+    )
+    first = 2 + batches
+    for f in range(fsdp):
+        for c in range(cores):
+            for t in range(tp):
+                head = t * cores + c
+                number = (f * cores + c) * tp + t
+                local.append(
+                    pltpu.make_async_copy(
+                        gathered.at[f, c, t, pl.ds(0, 3)],
+                        heads_ref.at[c * tp + t, :, :, pl.ds(f * piece, piece)],
+                        local_sem.at[first + 2 * number],
+                    )
+                )
+                local.append(
+                    pltpu.make_async_copy(
+                        gathered.at[f, c, t, pl.ds(3 + KEY, 2)],
+                        pair_weights.at[
+                            :, pl.ds(head * HEAD_DIM, HEAD_DIM), pl.ds(f * piece, piece)
+                        ],
+                        local_sem.at[first + 2 * number + 1],
+                    )
+                )
+
+    def d_copy(seq, place):
+        return send_to(
+            returned.at[seq, place],
+            landing.at[seq, me],
+            d_send.at[seq, place],
+            d_recv.at[seq, me],
+            **member(place),
+        )
+
+    def d_wait(seq, place):
+        send_to(
+            returned.at[seq, place],
+            landing.at[seq, place],
+            d_send.at[seq, place],
+            d_recv.at[seq, place],
+            **member(place),
+        ).wait_recv()
+
+    def e_copy(place):
+        return send_to(
+            enc_parts.at[:, pl.ds(pl.multiple_of(place * share, share), share)],
+            enc_landing.at[me],
+            e_send.at[place],
+            e_recv.at[me],
+            **member(place),
+        )
+
+    def e_wait(place):
+        send_to(
+            enc_landing.at[place],
+            enc_landing.at[place],
+            e_send.at[place],
+            e_recv.at[place],
+            **member(place),
+        ).wait_recv()
+
+    core_copy = send_to(
+        packed.at[1 - core], core_landing, r_send.at[0], r_recv.at[0], ctx=1 - core
+    )
+    pair_copy = send_to(
+        pair_ref.at[1 - core], pair_landing, r_send.at[1], r_recv.at[1], ctx=1 - core
+    )
+    shard_copy = send_to(
+        shard_ref.at[core], shard_ref.at[core], r_send.at[2], r_recv.at[2], ctx=1 - core
+    )
+    shard_wait = send_to(
+        shard_ref.at[1 - core], shard_ref.at[1 - core], r_send.at[2], r_recv.at[2], ctx=1 - core
+    )
+    head_copy = send_to(
+        head_shard.at[core], head_shard.at[core], r_send.at[3], r_recv.at[3], ctx=1 - core
+    )
+    head_wait = send_to(
+        head_shard.at[1 - core], head_shard.at[1 - core], r_send.at[3], r_recv.at[3], ctx=1 - core
+    )
+    f_copies = [
+        send_to(
+            partial_ref.at[here ^ k], fsdp_landing.at[k - 1], f_send.at[k], f_recv.at[k], fsdp=here ^ k
+        )
+        for k in range(1, fsdp)
+    ]
+    t_copies = [
+        send_to(line_ref.at[chip ^ k], line_landing.at[k - 1], t_send.at[k], t_recv.at[k], tp=chip ^ k)
+        for k in range(1, tp)
+    ]
+    h_copies = [
+        send_to(
+            head_ref.at[here ^ k], head_landing.at[k - 1], h_send.at[k], h_recv.at[k], fsdp=here ^ k
+        )
+        for k in range(1, fsdp)
+    ]
+
+    def s_copy(k):
+        return send_to(
+            sums_ref, sums_landing.at[k], s_send.at[k], s_recv.at[k], **member(me ^ k)
+        )
+
+    s_fsdp = [
+        send_to(
+            sums_two, sums_landing.at[group + k], s_send.at[group + k], s_recv.at[group + k], fsdp=here ^ k
+        )
+        for k in range(1, fsdp)
+    ]
+
+    for seq in range(batches):
+        local[1 + seq].start()
+
+    def start_grads(seq):
+        def one(k, unused):
+            d_copy(seq, me ^ k).start()
+            return unused
+
+        lax.fori_loop(1, group, one, 0)
+
+    start_grads(0)
+    core_copy.start()
+    for copy in [local[0]] + local[1 + batches :]:
+        copy.start()
+    start_grads(1)
+
+    def start_enc(k, unused):
+        e_copy(me ^ k).start()
+        return unused
+
+    lax.fori_loop(1, group, start_enc, 0)
+
+    def g_copy(seq, place, part):
+        lines = pl.ds(0, HEAD_DIM) if part == 0 else pl.ds(HEAD_DIM, 2 * HEAD_DIM)
+        return send_to(
+            outgoing.at[seq, place, lines],
+            incoming.at[seq, me, lines],
+            g_send.at[seq, place, part],
+            g_recv.at[seq, me, part],
+            **member(place),
+        )
+
+    def g_wait(seq, place, part):
+        lines = pl.ds(0, HEAD_DIM) if part == 0 else pl.ds(HEAD_DIM, 2 * HEAD_DIM)
+        send_to(
+            outgoing.at[seq, place, lines],
+            incoming.at[seq, place, lines],
+            g_send.at[seq, place, part],
+            g_recv.at[seq, place, part],
+            **member(place),
+        ).wait_recv()
+
+    def prepare(seq):
+        pltpu.make_async_copy(
+            returned.at[seq, me], landing.at[seq, me], local_sem.at[1 + seq]
+        ).wait()
+
+        def arrive(k, unused):
+            d_wait(seq, me ^ k)
+            return unused
+
+        lax.fori_loop(1, group, arrive, 0)
+
+        def lay(place, unused):
+            at = pl.ds(pl.multiple_of(place * chunk, chunk), chunk)
+            grads = landing[seq, place]
+            gradt_ref[:, at] = grads
+            grad_ref[at, :] = grads.T
+            delta_ref[:, at] = jnp.sum(
+                grads.astype(jnp.float32) * wide_ref[seq, :, at], axis=0, keepdims=True
+            )
+            queries_ref[at, :] = qkv_ref[seq, :HEAD_DIM, at].T
+            keys_ref[at, :] = qkv_ref[seq, HEAD_DIM : 2 * HEAD_DIM, at].T
+            values_ref[at, :] = qkv_ref[seq, 2 * HEAD_DIM :, at].T
+            return unused
+
+        lax.fori_loop(0, group, lay, 0)
+        grad_keys_ref[...] = jnp.zeros_like(grad_keys_ref)
+        grad_values_ref[...] = jnp.zeros_like(grad_values_ref)
+
+    def encoder_part():
+        local[1 + batches].wait()
+
+        def arrive(k, unused):
+            e_wait(me ^ k)
+            return unused
+
+        lax.fori_loop(1, group, arrive, 0)
+        total = enc_landing[0].astype(jnp.float32)
+        for place in range(1, group):
+            total = total + enc_landing[place].astype(jnp.float32)
+        for copy in local[first:]:
+            copy.wait()
+        grads = low(total)
+        enc_rows = enc_ref[:, pl.ds(pl.multiple_of(me * share, share), share), :]
+        flat, enc_flat = grads.reshape(batches * share, 2 * width), enc_rows.reshape(
+            batches * share, width
+        )
+        result = dot_of(flat[:, :width], pair_weights[0], 1, 0) + dot_of(
+            flat[:, width:], pair_weights[1], 1, 0
+        )
+        enc_out[...] = result.reshape(batches, share, width)
+        for which in range(2):
+            grad = low(dot_of(flat[:, which * width : (which + 1) * width], enc_flat, 0, 0))
+            for f in range(fsdp):
+                for c in range(cores):
+                    for t in range(tp):
+                        head = t * cores + c
+                        pair_ref[c, f, t, which] = grad[
+                            head * HEAD_DIM : (head + 1) * HEAD_DIM, f * piece : (f + 1) * piece
+                        ]
+        pair_copy.start()
+
+    def sum_cores():
+        local[0].wait()
+        core_copy.wait_recv()
+        pair_copy.wait_recv()
+
+        def one(f, unused):
+            def two(t, unused):
+                partial_ref[f, t, :early] = low(
+                    partial_ref[f, t, :early].astype(jnp.float32)
+                    + core_landing[f, t].astype(jnp.float32)
+                )
+                partial_ref[f, t, early:] = low(
+                    pair_ref[core, f, t].astype(jnp.float32)
+                    + pair_landing[f, t].astype(jnp.float32)
+                )
+                return unused
+
+            return lax.fori_loop(0, tp, two, unused)
+
+        lax.fori_loop(0, fsdp, one, 0)
+        for copy in f_copies:
+            copy.start()
+
+    def sum_fsdp():
+        for copy in f_copies:
+            copy.wait_recv()
+
+        def one(t, unused):
+            total = partial_ref[here, t].astype(jnp.float32)
+            for k in range(fsdp - 1):
+                total = total + fsdp_landing[k, t].astype(jnp.float32)
+            line_ref[t] = low(total)
+            return unused
+
+        lax.fori_loop(0, tp, one, 0)
+        for copy in t_copies:
+            copy.start()
+
+    def sum_line():
+        for copy in t_copies:
+            copy.wait_recv()
+        total = line_ref[chip].astype(jnp.float32)
+        for k in range(tp - 1):
+            total = total + line_landing[k].astype(jnp.float32)
+        shard_ref[core] = total
+        shard_copy.start()
+
+    prepare(0)
+
+    def attend(index, unused):
+        seq, block = index // blocks, blocks - 1 - index % blocks
+
+        @pl.when(index == 2)
+        def encoder_hook():
+            encoder_part()
+
+        @pl.when(index == blocks - 1)
+        def core_hook():
+            sum_cores()
+
+        @pl.when(index == blocks)
+        def next_sequence():
+            prepare(1)
+
+        @pl.when(index == blocks + 1)
+        def fsdp_hook():
+            sum_fsdp()
+
+        @pl.when(index == blocks + 2)
+        def line_hook():
+            sum_line()
+
+        start = pl.multiple_of(block * span, span)
+        at = pl.ds(start, span)
+        queries_t, queries = qkv_ref[seq, :HEAD_DIM, at], queries_ref[at, :]
+        grads_t, grads = gradt_ref[:, at], grad_ref[at, :]
+        logs, deltas = log_ref[seq, :, at], delta_ref[:, at]
+        limit = jnp.maximum(
+            prefix_ref[seq], start + 1 + lax.broadcasted_iota(jnp.int32, (1, span), 1)
+        )
+
+        def advance(other, grad_queries, masked):
+            offset = pl.multiple_of(other * span, span)
+            there = pl.ds(offset, span)
+            scores = dot_of(keys_ref[there, :], queries_t, 1, 0)
+            if masked:
+                scores = hide(scores, limit, offset)
+            probs = jnp.exp(scores - logs)
+            grad_probs = dot_of(values_ref[there, :], grads_t, 1, 0)
+            grad_scores = low(probs * (grad_probs - deltas))
+            grad_values_ref[there, :] += dot_of(low(probs), grads, 1, 0)
+            grad_keys_ref[there, :] += dot_of(grad_scores, queries, 1, 0)
+            return grad_queries + dot_of(
+                qkv_ref[seq, HEAD_DIM : 2 * HEAD_DIM, there], grad_scores, 1, 0
+            )
+
+        grad_queries = jnp.zeros((HEAD_DIM, span), jnp.float32)
+        grad_queries = lax.fori_loop(0, block, lambda j, c: advance(j, c, False), grad_queries)
+        grad_queries = lax.fori_loop(
+            block, jnp.maximum(block + 1, wide_blocks), lambda j, c: advance(j, c, True), grad_queries
+        )
+        done = low(grad_queries * factor)
+        for part in range(ratio):
+            place = block * ratio + part
+            outgoing[seq, place, :HEAD_DIM, :] = done[:, part * chunk : (part + 1) * chunk]
+
+            @pl.when(place != me)
+            def send(place=place):
+                g_copy(seq, place, 0).start()
+
+        lowest = jnp.where(block == 0, 0, block)
+        highest = jnp.where(
+            block == 0, wide_blocks, jnp.where(block >= wide_blocks, block + 1, block)
+        )
+
+        def give(place, unused):
+            at = pl.ds(pl.multiple_of(place * chunk, chunk), chunk)
+            outgoing[seq, place, HEAD_DIM : 2 * HEAD_DIM, :] = low(grad_keys_ref[at, :].T)
+            outgoing[seq, place, 2 * HEAD_DIM :, :] = low(grad_values_ref[at, :].T)
+
+            @pl.when(place != me)
+            def send():
+                g_copy(seq, place, 1).start()
+
+            return unused
+
+        lax.fori_loop(lowest * ratio, highest * ratio, give, 0)
+        return unused
+
+    lax.fori_loop(0, batches * blocks, attend, 0)
+    sums_ref[...] = jnp.zeros_like(sums_ref)
+    sums_ref[:8, :] = stats_ref[...]
+
+    def rows_copy(number):
+        return pltpu.make_async_copy(
+            rows_in.at[number // group, number % group],
+            rows_ref.at[number % rows_ref.shape[0]],
+            rows_sem.at[number % rows_ref.shape[0]],
+        )
+
+    depth = rows_ref.shape[0]
+    for number in range(depth):
+        rows_copy(number).start()
+
+    def weigh(number, total):
+        rows_copy(number).wait()
+        total = total + dot_of(
+            outgoing[number // group, number % group], rows_ref[number % depth], 1, 0
+        )
+
+        @pl.when(number + depth < batches * group)
+        def more():
+            rows_copy(number + depth).start()
+
+        return total
+
+    total = lax.fori_loop(
+        0, batches * group, weigh, jnp.zeros((3 * HEAD_DIM, width), jnp.float32)
+    )
+    for f in range(fsdp):
+        head_ref[f] = total[:, f * piece : (f + 1) * piece]
+    for copy in h_copies:
+        copy.start()
+
+    def finish(seq, unused):
+        def arrive(k, unused):
+            g_wait(seq, me ^ k, 0)
+            g_wait(seq, me ^ k, 1)
+            return unused
+
+        lax.fori_loop(1, group, arrive, 0)
+        incoming[seq, me] = outgoing[seq, me]
+        upstream = dot_of(
+            incoming[seq].reshape(group * 3 * HEAD_DIM, chunk),
+            heads_ref[...].reshape(group * 3 * HEAD_DIM, width),
+            0,
+            0,
+        )
+        start_sum = tokens_ref[seq].astype(jnp.float32) + step_ref[seq]
+        centre = start_sum - jnp.mean(start_sum, -1, keepdims=True)
+        inverse = lax.rsqrt(jnp.mean(centre * centre, -1, keepdims=True) + EPS)
+        back, gain_sum, bias_sum = rows_back(upstream, centre * inverse, inverse, gain_ref[...])
+        input_ref[seq] = after_ref[seq] + back
+        sums_ref[8:9, :] += gain_sum
+        sums_ref[9:10, :] += bias_sum
+        return unused
+
+    lax.fori_loop(0, batches, finish, 0)
+
+    def start_sums(k, unused):
+        s_copy(k).start()
+        return unused
+
+    lax.fori_loop(1, group, start_sums, 0)
+    for copy in h_copies:
+        copy.wait_recv()
+    total = head_ref[here]
+    for k in range(fsdp - 1):
+        total = total + head_landing[k]
+    head_shard[core] = total
+    head_copy.start()
+
+    def arrive_sums(k, total):
+        s_copy(k).wait_recv()
+        return total + sums_landing[k]
+
+    sums_two[...] = lax.fori_loop(1, group, arrive_sums, sums_ref[...])
+    for copy in s_fsdp:
+        copy.start()
+    shard_wait.wait_recv()
+
+    def whole(block):
+        return jnp.concatenate([shard_ref[0, block], shard_ref[1, block]], 0)
+
+    query_out[...] = whole(0).T
+    back_out[...] = whole(1)
+    cross_out[...] = whole(2)
+    for part in range(4):
+        up_out[:, part * piece : (part + 1) * piece] = whole(3 + part).T
+        down_out[part * piece : (part + 1) * piece, :] = whole(7 + part)
+    pair_out[0] = whole(11).T
+    pair_out[1] = whole(12).T
+    head_wait.wait_recv()
+    for which in range(3):
+        lines = slice(which * HEAD_DIM, (which + 1) * HEAD_DIM)
+        self_out[which] = jnp.concatenate([head_shard[0, lines], head_shard[1, lines]], 0).T
+    total = sums_two[...]
+    for k, copy in enumerate(s_fsdp):
+        copy.wait_recv()
+        total = total + sums_landing[group + 1 + k]
+    sums_out[...] = total
+    core_copy.wait_send()
+    pair_copy.wait_send()
+    shard_copy.wait_send()
+    head_copy.wait_send()
+    for copy in f_copies + t_copies + h_copies + s_fsdp:
+        copy.wait_send()
+
+    def sent(k, unused):
+        e_copy(me ^ k).wait_send()
+        s_copy(k).wait_send()
+        for seq in range(batches):
+            d_copy(seq, me ^ k).wait_send()
+            g_copy(seq, me ^ k, 0).wait_send()
+            g_copy(seq, me ^ k, 1).wait_send()
+        return unused
+
+    lax.fori_loop(1, group, sent, 0)
+
+
+def backward_group(
+    prefix,
+    returned,
+    enc_parts,
+    packed,
+    gathered,
+    rows,
+    qkv,
+    wide,
+    logs,
+    tokens,
+    steps,
+    gain,
+    after,
+    encoder,
+    stats,
+    span,
+    tp,
+    fsdp,
+):
+    batches, chunk, width = tokens.shape
+    group = returned.shape[1]
+    length = group * chunk
+    share = encoder.shape[1] // group
+    piece = width // fsdp
+    count = packed.shape[3]
+    tail = packed.shape[4:]
+    bf16, f32 = jnp.bfloat16, jnp.float32
+    struct = jax.ShapeDtypeStruct
+    inside = pl.BlockSpec(memory_space=pltpu.VMEM)
+    outside = pl.BlockSpec(memory_space=pl.ANY)
+    dma = pltpu.SemaphoreType.DMA
+    vmem = pltpu.VMEM
+    parts = group * fsdp
+    return pl.pallas_call(
+        functools.partial(backward_kernel, span=span, tp=tp, fsdp=fsdp),
+        in_specs=[pl.BlockSpec(memory_space=pltpu.SMEM)] + [outside] * 5 + [inside] * 9,
+        out_specs=[inside] * 10,
+        out_shape=[
+            struct((batches, chunk, width), f32),
+            struct((batches, share, width), f32),
+            struct((3, piece, piece), f32),
+            struct((piece, piece), f32),
+            struct((2, piece, piece), f32),
+            struct((piece, piece), f32),
+            struct((piece, piece), f32),
+            struct((piece, width), f32),
+            struct((width, piece), f32),
+            struct((16, width), f32),
+        ],
+        scratch_shapes=[
+            vmem((batches, group, HEAD_DIM, chunk), bf16),
+            vmem((batches, group, 3 * HEAD_DIM, chunk), bf16),
+            vmem((batches, group, 3 * HEAD_DIM, chunk), bf16),
+            vmem((length, HEAD_DIM), bf16),
+            vmem((length, HEAD_DIM), bf16),
+            vmem((length, HEAD_DIM), bf16),
+            vmem((length, HEAD_DIM), bf16),
+            vmem((HEAD_DIM, length), bf16),
+            vmem((1, length), f32),
+            vmem((length, HEAD_DIM), f32),
+            vmem((length, HEAD_DIM), f32),
+            vmem((4, chunk, width), bf16),
+            vmem((group, 3, HEAD_DIM, width), bf16),
+            vmem((2, width, width), bf16),
+            vmem((group, batches, share, 2 * width), bf16),
+            vmem((group // tp, fsdp, tp, 2) + tail, bf16),
+            vmem((fsdp, tp, 2) + tail, bf16),
+            vmem((fsdp, tp, count) + tail, bf16),
+            vmem((fsdp, tp, count + 2) + tail, bf16),
+            vmem((fsdp - 1, tp, count + 2) + tail, bf16),
+            vmem((tp, count + 2) + tail, bf16),
+            vmem((tp - 1, count + 2) + tail, bf16),
+            vmem((2, count + 2) + tail, f32),
+            vmem((fsdp, 3 * HEAD_DIM, piece), f32),
+            vmem((fsdp - 1, 3 * HEAD_DIM, piece), f32),
+            vmem((2, 3 * HEAD_DIM, piece), f32),
+            vmem((16, width), f32),
+            vmem((group + fsdp, 16, width), f32),
+            vmem((16, width), f32),
+            dma((batches, group)),
+            dma((batches, group)),
+            dma((group,)),
+            dma((group,)),
+            dma((batches, group, 2)),
+            dma((batches, group, 2)),
+            dma((4,)),
+            dma((4,)),
+            dma((fsdp,)),
+            dma((fsdp,)),
+            dma((tp,)),
+            dma((tp,)),
+            dma((fsdp,)),
+            dma((fsdp,)),
+            dma((group + fsdp,)),
+            dma((group + fsdp,)),
+            dma((2 + batches + 2 * parts,)),
+            dma((4,)),
+        ],
+        compiler_params=pltpu.CompilerParams(
+            vmem_limit_bytes=VMEM_LIMIT, collective_id=2, has_side_effects=True
+        ),
+        cost_estimate=pl.CostEstimate(
+            flops=100_000_000_000, bytes_accessed=40_000_000, transcendentals=20_000_000
+        ),
+        name="backward_group",
+    )(
+        prefix,
+        returned,
+        enc_parts,
+        packed,
+        gathered,
+        rows,
+        qkv,
+        wide,
+        logs,
+        tokens,
+        steps,
+        gain,
+        after,
+        encoder,
+        stats,
+    )
 
 
 def local_heads(
@@ -1272,7 +1833,6 @@
         prefix, tokens, embedded, norm_gain[:1], norm_bias[:1], mine, span, group, 4, 4
     )
     final, grad_after, returned, enc_parts, stats, packed = middle(
-        me[None].astype(jnp.int32),
         gathered,
         tokens,
         embedded,
@@ -1283,82 +1843,27 @@
         contexts,
         4,
     )
-    returns = [trade([returned[s, k] for k in range(group)]) for s in range(batches)]
-    whole_block = lambda b: jnp.transpose(gathered[:, :, :, b], (2, 1, 3, 0, 4)).reshape(
-        width, width
-    )
-    full_k, full_v = whole_block(4), whole_block(5)
-    qkv_heads = jnp.transpose(gathered[:, :, :, :3], (1, 2, 3, 4, 0, 5)).reshape(
-        group, 3 * HEAD_DIM, width
-    )
-    qkv_slots = jnp.concatenate(
-        [lax.dynamic_index_in_dim(qkv_heads, me ^ k, 0, False) for k in range(group)]
-    )
-    share = enc_count // group
-    parts = enc_parts.reshape(batches, group, share, 2 * width)
-    parts = [lax.dynamic_index_in_dim(parts, me ^ k, 1, False) for k in range(group)]
-    enc_grads = low(sum(p.astype(jnp.float32) for p in trade(parts)))
-    enc_rows = lax.dynamic_slice_in_dim(encoder, me * share, share, 1)
-    enc_rows = enc_rows.reshape(batches * share, width)
-    enc_flat = enc_grads.reshape(batches * share, 2 * width)
-    encoder_grad = (
-        dot_of(enc_flat[:, :width], full_k, 1, 0) + dot_of(enc_flat[:, width:], full_v, 1, 0)
-    ).reshape(batches, share, width)
-    grad_pair = dot_of(enc_flat, enc_rows, 0, 0)
-    grads_back, head_grads = [], 0.0
-    for s in range(batches):
-        scalars = jnp.stack([prefix[s], me]).astype(jnp.int32)
-        outs = backward_attention(scalars, qkv[s], wide[s], logs[s], returns[s], span)
-        grads_back.append(trade(outs))
-        for k in range(group):
-            own_rows = lax.dynamic_index_in_dim(rows[s], me ^ k, 0, False)
-            head_grads = head_grads + dot_of(outs[k], own_rows, 1, 0)
-    pair = low(grad_pair).reshape(2, 4, 2, half, 4, piece)
-    packed = jnp.concatenate([packed, jnp.transpose(pair, (4, 2, 1, 0, 3, 5))], 3)
-    scattered = lax.psum_scatter(
-        packed.reshape((32,) + packed.shape[3:]),
-        ("fsdp", "ctx", "tp"),
-        scatter_dimension=0,
-        tiled=False,
-    ).astype(jnp.float32)
-    other_half = swap_cores(scattered)
-    shards = jnp.concatenate(
-        [
-            jnp.where(ctx_index == 0, scattered, other_half),
-            jnp.where(ctx_index == 0, other_half, scattered),
-        ],
-        1,
-    )
-    head_grads = head_grads.reshape(3 * HEAD_DIM, 4, piece)
-    pieces = [lax.dynamic_index_in_dim(head_grads, fsdp_index ^ k, 1, False) for k in range(4)]
-    head_shard = pieces[0] + sum(
-        lax.ppermute(pieces[k], "fsdp", [(i, i ^ k) for i in range(4)]) for k in range(1, 4)
-    )
-    head_shard = jnp.transpose(head_shard.reshape(3, HEAD_DIM, piece), (0, 2, 1))
-    other_shard = swap_cores(head_shard)
-    grad_self = jnp.concatenate(
-        [
-            jnp.where(ctx_index == 0, head_shard, other_shard),
-            jnp.where(ctx_index == 0, other_shard, head_shard),
-        ],
-        2,
-    )
-    input_grads, gains_one, shifts_one = [], 0.0, 0.0
-    for s in range(batches):
-        upstream = dot_of(jnp.concatenate(grads_back[s]), qkv_slots, 0, 0)
-        start_sum = tokens[s].astype(jnp.float32) + embedded[s]
-        unused, unit, inverse = norm_rows(start_sum, norm_gain[0], norm_bias[0])
-        back, gain, shift = norm_back_rows(upstream, unit, inverse, norm_gain[0])
-        input_grads.append(grad_after[s] + back)
-        gains_one, shifts_one = gains_one + gain, shifts_one + shift
-    gain_grad, bias_grad, square_totals = lax.psum(
-        (
-            jnp.stack([gains_one, stats[4], stats[6]]),
-            jnp.stack([shifts_one, stats[5], stats[7]]),
-            jnp.sum(stats[:4], -1),
-        ),
-        ("fsdp", "ctx", "tp"),
-    )
+    outs = backward_group(
+        prefix,
+        returned,
+        enc_parts,
+        packed,
+        gathered,
+        rows,
+        qkv,
+        wide,
+        logs,
+        tokens,
+        embedded,
+        norm_gain[:1],
+        grad_after,
+        encoder,
+        stats,
+        span,
+        4,
+        4,
+    )
+    sums = outs[9]
     entries = (
         tokens.shape[0]
         * tokens.shape[1]
@@ -1369,19 +1874,11 @@
     )
     return (
         final,
-        jnp.stack(input_grads),
-        encoder_grad,
-        grad_self,
-        shards[0].T,
-        flip(shards[11:13]),
-        shards[1],
-        shards[2],
-        shards[3:7].reshape(width, piece).T,
-        shards[7:11].reshape(width, piece),
-        gain_grad,
-        bias_grad[:2],
-        bias_grad[2],
-        jnp.sqrt(square_totals / entries),
+        *outs[:9],
+        jnp.stack([sums[8], sums[4], sums[6]]),
+        jnp.stack([sums[9], sums[5]]),
+        sums[7],
+        jnp.sqrt(jnp.sum(sums[:4], -1) / entries),
     )
 
 

time: 597 us -> 437 us (0.73); the launches traced: 585 us -> 433 us
  Pallas kernels: 287 us -> 395 us
  waiting for transfers between devices: 102 us -> 0.04 us
  starting transfers between devices: 64 us -> 0.04 us
  blocking collectives: 36.7 us -> 0 us
  local copies, waits for them, and re-layouts: 42.6 us -> 20.8 us
  matrix products: 17.7 us -> 0.19 us
  other arithmetic: 19.8 us -> 2.56 us
    pallas_call x2 -> x1, Pallas kernels: 72.9 us -> 180 us  [backward_group(): pl.pallas_call(functools.partial(backward_kernel, span=span, tp=tp, fsdp=...]
    ppermute x40 -> x0, waiting for transfers between devices: 101 us -> none  [the longest x35 99.8 us: trade(): lax.ppermute(parts[k], ('ctx', 'tp'), [(i, i ^ k) for i in range(group)])]
    ppermute x40 -> x0, starting transfers between devices: 64 us -> none  [the longest x35 54.2 us: trade(): lax.ppermute(parts[k], ('ctx', 'tp'), [(i, i ^ k) for i in range(group)])]
    psum x1 -> x0, blocking collectives: 36.7 us -> none  [local_heads(): lax.psum((jnp.stack([gains_one, stats[4], stats[6]]), jnp.stack([shifts_o...]
    dot_general x21 -> x0, matrix products: 17.5 us -> none  [dot_of(): lax.dot_general(left, right, (((left_dim,), (right_dim,)), ((), ())), pre...]
    another operation x6 -> x2, other arithmetic: 8.52 us -> 1.21 us  [the longest x1 0.61 us: local_heads(): jnp.stack([sums[8], sums[4], sums[6]])]
    slice x6 -> x1, local copies, waits for them, and re-layouts: 8.69 us -> 1.46 us  [local_heads(): sums[7]]
    concatenate x3 -> x0, other arithmetic: 6.73 us -> none  [the longest x1 5.98 us: local_heads(): jnp.concatenate([packed, jnp.transpose(pair, (4, 2, 1, 0, 3, 5))], 3)]
  transfers between devices with their start and end apart: 42 -> 1, of which waited for: 16 -> 0; matrix products, arithmetic and copies ran while one was open for 10% -> 1% of each run, Pallas kernels for 39% -> 37%
where the time goes in v3:
time: 437 us; the launch traced here: 433 us
  Pallas kernels  395 us (90%)
  local copies, waits for them, and re-layouts  20.8 us (5%)
  between operations  14.2 us (3%)
    pallas_call x1, Pallas kernels, backward_group(): pl.pallas_call(functools.partial(backward_kernel, span=span, tp=tp, fsdp=...  180 us
    pallas_call x1, Pallas kernels, forward_group(): pl.pallas_call(functools.partial(forward_kernel, span=span, tp=tp, fsdp=f...  158 us
    pallas_call x1, Pallas kernels, middle(): pl.pallas_call(functools.partial(middle_kernel, tp=tp, group=group), grid...  56.5 us
    unnamed x38, local copies, waits for them, and re-layouts  12.9 us
  transfers between devices with their start and end apart: 1, of which 0 were waited for; matrix products, arithmetic and copies ran while one was open for 1% of the time, Pallas kernels for 37%

profile of v3, /device:TPU:17, one launch (start us, length us, event | category | flops | bytes accessed | tf_op | source)
XLA Modules:
  0.0 433.1 jit_solution(18183872227004142096)
XLA Ops:
  7.3 1.0 copy.33
  8.3 0.9 copy.34
  9.2 1.0 copy.35
  10.1 1.0 copy.36
  11.2 0.8 bitcast_dynamic-update-slice_fusion.4
  12.0 0.8 bitcast_dynamic-update-slice_fusion.3
  12.7 0.9 constant_dynamic-update-slice_fusion
  13.7 0.7 constant_dynamic-slice_fusion.1
  15.2 1.3 slice.31.gain_ref
  16.5 1.3 slice.32.bias_ref
  18.4 158.4 %forward_group.1 = (bf16[2,8,512,512]{3,2,1,0:T(8,128)(2,1)}, bf16[2,192,4096]{2,1,0:T(8,128)(2,1)}, f32[2,64,4096]{2,1,0:T(8,128)}, f32[2,1,4096]{2,1,0:T(1,128...) custom-call(s32[2]{0:T(128)} %prefix_ref.3, bf16[2,512,512]{2,1,0:T(8,128)(2,1)} %tokens_ref.5, ...), custom_call_target="tpu_custom_call" | custom-call | flops 60000002048 | bytes 30000000 | tf_op jit(solution)/shard_map/forward_group/pallas_call | solution.py:810
  176.8 56.5 %middle.1 = (f32[2,512,512]{2,1,0:T(8,128)}, f32[2,512,512]{2,1,0:T(8,128)}, bf16[2,8,64,512]{3,2,1,0:T(8,128)(2,1)}, bf16[2,256,1024]{2,1,0:T(8,128)(2,1)}, f32...) custom-call(bf16[4,2,4,16,64,128]{5,4,3,2,1,0:T(8,128)(2,1)} %bitcast.24, bf16[2,512,512]{2,1,0:T(8,128)(2,1)} %tokens_ref.5, ...), custom_call_target="tpu_custom_call" | custom-call | flops 30000001024 | bytes 30000000 | tf_op jit(solution)/shard_map/middle/pallas_call | solution.py:1024
  233.3 180.4 %backward_group.1 = (f32[2,512,512]{2,1,0:T(8,128)}, f32[2,32,512]{2,1,0:T(8,128)}, f32[3,128,128]{2,1,0:T(8,128)}, f32[128,128]{1,0:T(8,128)}, f32[2,128,128]{2...) custom-call(s32[2]{0:T(128)} %prefix_ref.3, ...), custom_call_target="tpu_custom_call" | custom-call | flops 99999997952 | bytes 40000000 | tf_op jit(solution)/shard_map/backward_group/pallas_call | solution.py:1692
  413.7 1.5 fusion.4
  415.2 0.8 slice_reduce_fusion
  417.8 3.2 copy.52
  421.0 0.7 copy.53
  421.6 0.7 copy.54
  422.3 0.6 copy.55
  423.0 0.7 copy.56
  423.6 0.6 copy.57
  424.3 0.6 copy.58
  424.9 0.7 copy.59
  425.6 0.7 copy.60
  (33 shorter events, 3.3 us)
Async XLA Ops:
  7.2 7.3 %copy-start = (bf16[50,512]{1,0:T(8,128)(2,1)S(1)}, bf16[50,512]{1,0:T(8,128)(2,1)}, u32[]{:S(2)}) copy-start(bf16[50,512]{1,0:T(8,128)(2,1)} %param.17) | copy-start | bytes 153604
  7.2 7.2 %copy-start.9 = (s32[2]{0:T(128)S(1)}, s32[2]{0:T(128)}, u32[]{:S(2)}) copy-start(s32[2]{0:T(128)} %param.16) | copy-start | bytes 28
  7.2 169.6 %all-gather.3.cloned.1.call-start = ((), (), s32[]{:S(2)}) async-start(), calls=%async_computation | async-start | bytes 8650752 | tf_op jit(solution)/shard_map/all_gather | solution.py:1824
  417.8 3.2 copy-start.5
  417.8 3.9 copy-start.3
  417.8 4.6 %copy-start.8 = (f32[128,128]{1,0:T(8,128)S(1)}, f32[128,128]{1,0:T(8,128)}, u32[]{:S(2)}) copy-start(f32[128,128]{1,0:T(8,128)} %get-tuple-element.80) | copy-start | bytes 196612
  417.8 5.2 %copy-start.4 = (f32[2,128,128]{2,1,0:T(8,128)S(1)}, f32[2,128,128]{2,1,0:T(8,128)}, u32[]{:S(2)}) copy-start(f32[2,128,128]{2,1,0:T(8,128)} %get-tuple-element.81) | copy-start | bytes 393220
  417.8 5.8 %copy-start.7 = (f32[128,128]{1,0:T(8,128)S(1)}, f32[128,128]{1,0:T(8,128)}, u32[]{:S(2)}) copy-start(f32[128,128]{1,0:T(8,128)} %get-tuple-element.82) | copy-start | bytes 196612
  417.8 6.5 %copy-start.6 = (f32[128,128]{1,0:T(8,128)S(1)}, f32[128,128]{1,0:T(8,128)}, u32[]{:S(2)}) copy-start(f32[128,128]{1,0:T(8,128)} %get-tuple-element.83) | copy-start | bytes 196612
  417.8 7.1 %copy-start.2 = (f32[128,512]{1,0:T(8,128)S(1)}, f32[128,512]{1,0:T(8,128)}, u32[]{:S(2)}) copy-start(f32[128,512]{1,0:T(8,128)} %get-tuple-element.84) | copy-start | bytes 786436
  417.8 7.8 %copy-start.1 = (f32[512,128]{1,0:T(8,128)S(1)}, f32[512,128]{1,0:T(8,128)}, u32[]{:S(2)}) copy-start(f32[512,128]{1,0:T(8,128)} %get-tuple-element.85) | copy-start | bytes 786436
Sparse Core Ops, SparseCore 0:
  14.6 91.1 all-gather.2

commit v4 on v3

v4 whole, which is shorter than its diff:
```python
import functools
import math

import jax
import jax.numpy as jnp
from jax import lax
from jax.experimental import pallas as pl
from jax.experimental.pallas import tpu as pltpu
from jax.sharding import PartitionSpec as P

HEAD_DIM = 64


EPS = 1e-05
NEG = -1e30
ROOT_HALF = 1.0 / math.sqrt(2.0)
INV_ROOT_TWO_PI = 1.0 / math.sqrt(2.0 * math.pi)
VMEM_LIMIT = 62 * 2**20


def norm_rows(hidden, scaling, offsets):
    centre = hidden - jnp.mean(hidden, -1, keepdims=True)
    inverse = lax.rsqrt(jnp.mean(centre * centre, -1, keepdims=True) + EPS)
    unit_rows = centre * inverse
    return (unit_rows * scaling + offsets, unit_rows, inverse)


def norm_back(upstream, unit_rows, inverse, scaling):
    scaled = upstream * scaling
    result = inverse * (
        scaled
        - jnp.mean(scaled, -1, keepdims=True)
        - unit_rows * jnp.mean(scaled * unit_rows, -1, keepdims=True)
    )
    return (result, jnp.sum(upstream * unit_rows, (0, 1)), jnp.sum(upstream, (0, 1)))


def gelu_parts(inputs):
    normal_cdf = 0.5 * (1.0 + lax.erf(inputs * ROOT_HALF))
    return (
        inputs * normal_cdf,
        normal_cdf + inputs * jnp.exp(-0.5 * inputs * inputs) * INV_ROOT_TWO_PI,
    )


def spread_rows(rows):
    return lax.all_gather(rows, "tp", axis=1, tiled=True)


def spread_grads(grad_rows):
    return lax.all_gather(grad_rows, "tp", axis=1, tiled=True)


def finish_branch(local_in, local_weight):
    return lax.psum_scatter(
        jnp.einsum("scw,wd->scd", local_in, local_weight, preferred_element_type=jnp.float32),
        "tp",
        scatter_dimension=1,
        tiled=True,
    )


def finish_grad(local_grad, local_weight):
    return lax.psum_scatter(
        jnp.einsum("scw,dw->scd", local_grad, local_weight, preferred_element_type=jnp.float32),
        "tp",
        scatter_dimension=1,
        tiled=True,
    )


def block_scores(queries, key_block, query_pos, key_pos, lengths, factor):
    scores = (
        jnp.einsum("sqhe,skhe->sqhk", queries, key_block, preferred_element_type=jnp.float32)
        * factor
    )
    visible = (key_pos[None, None, :] <= query_pos[None, :, None]) | (
        key_pos[None, None, :] < lengths[:, None, None]
    )
    return jnp.where(visible[:, :, None, :], scores, NEG)


def attend_forward(queries, key_rows, value_rows, query_pos, lengths, key_span, factor):
    length = key_rows.shape[1]

    def attend_advance(running, offset):
        highest, totals, summed = running
        key_block = lax.dynamic_slice_in_dim(key_rows, offset, key_span, 1)
        value_block = lax.dynamic_slice_in_dim(value_rows, offset, key_span, 1)
        scores = block_scores(
            queries, key_block, query_pos, offset + lax.iota(jnp.int32, key_span), lengths, factor
        )
        new_high = jnp.maximum(highest, jnp.max(scores, -1))
        weights = jnp.exp(scores - new_high[..., None])
        fading = jnp.exp(highest - new_high)
        totals = totals * fading + jnp.sum(weights, -1)
        summed = summed * fading[..., None] + jnp.einsum(
            "sqhk,skhe->sqhe",
            weights.astype(jnp.bfloat16),
            value_block,
            preferred_element_type=jnp.float32,
        )
        return ((new_high, totals, summed), None)

    stat_shape = queries.shape[:3]
    initial = (
        jnp.full(stat_shape, NEG, jnp.float32),
        jnp.zeros(stat_shape, jnp.float32),
        jnp.zeros(queries.shape, jnp.float32),
    )
    offsets = jnp.arange(length // key_span, dtype=jnp.int32) * key_span
    (highest, totals, summed), unused = lax.scan(attend_advance, initial, offsets)
    return (summed / totals[..., None], highest + jnp.log(totals))


def attend_block(
    queries,
    grad_out,
    log_rows,
    delta_rows,
    key_block,
    value_block,
    query_pos,
    key_pos,
    lengths,
    factor,
):
    scores = block_scores(queries, key_block, query_pos, key_pos, lengths, factor)
    probs = jnp.exp(scores - log_rows[..., None])
    grad_probs = jnp.einsum(
        "sqhe,skhe->sqhk", grad_out, value_block, preferred_element_type=jnp.float32
    )
    grad_scores = (probs * (grad_probs - delta_rows[..., None])).astype(jnp.bfloat16)
    return (probs.astype(jnp.bfloat16), grad_scores)


def key_sweep(
    queries,
    grad_out,
    log_rows,
    delta_rows,
    key_rows,
    value_rows,
    query_pos,
    lengths,
    key_span,
    factor,
):
    batches, row_count, head_count, head_depth = queries.shape
    length = key_rows.shape[1]

    def key_advance(grad_query, offset):
        key_block = lax.dynamic_slice_in_dim(key_rows, offset, key_span, 1)
        value_block = lax.dynamic_slice_in_dim(value_rows, offset, key_span, 1)
        key_pos = offset + lax.iota(jnp.int32, key_span)
        probs_low, grad_scores = attend_block(
            queries,
            grad_out,
            log_rows,
            delta_rows,
            key_block,
            value_block,
            query_pos,
            key_pos,
            lengths,
            factor,
        )
        grad_query = (
            grad_query
            + jnp.einsum(
                "sqhk,skhe->sqhe", grad_scores, key_block, preferred_element_type=jnp.float32
            )
            * factor
        )
        grad_key = (
            jnp.einsum("sqhk,sqhe->kshe", grad_scores, queries, preferred_element_type=jnp.float32)
            * factor
        )
        grad_value = jnp.einsum(
            "sqhk,sqhe->kshe", probs_low, grad_out, preferred_element_type=jnp.float32
        )
        return (grad_query, (grad_key, grad_value))

    offsets = jnp.arange(length // key_span, dtype=jnp.int32) * key_span
    grad_query, stacked = lax.scan(key_advance, jnp.zeros(queries.shape, jnp.float32), offsets)
    flat_shape = (length, batches, head_count * head_depth)
    return (grad_query, stacked[0].reshape(flat_shape), stacked[1].reshape(flat_shape))


def local(
    tokens,
    timesteps,
    time_table,
    prefix,
    encoder,
    self_qkv,
    cross_q,
    cross_kv,
    self_out,
    cross_out,
    ffn_up,
    ffn_down,
    norm_gain,
    norm_bias,
    cotangent,
):
    proj_self, proj_query, proj_pair, back_self, back_cross, expand_full, shrink_full = (
        lax.all_gather(self_qkv, "fsdp", axis=1, tiled=True),
        lax.all_gather(cross_q, "fsdp", axis=0, tiled=True),
        lax.all_gather(cross_kv, "fsdp", axis=1, tiled=True),
        lax.all_gather(self_out, "fsdp", axis=1, tiled=True),
        lax.all_gather(cross_out, "fsdp", axis=1, tiled=True),
        lax.all_gather(ffn_up, "fsdp", axis=0, tiled=True),
        lax.all_gather(ffn_down, "fsdp", axis=1, tiled=True),
    )
    batches = tokens.shape[0]
    model_width = tokens.shape[2]
    local_width = proj_query.shape[1]
    head_count = local_width // HEAD_DIM
    factor = HEAD_DIM ** (-0.5)
    ctx_index = lax.axis_index("ctx")
    local_stack = jnp.transpose(proj_self, (1, 0, 2)).reshape(model_width, 3 * local_width)
    steps_onehot = (timesteps[:, None] == lax.iota(jnp.int32, time_table.shape[0])[None, :]).astype(
        jnp.bfloat16
    )
    embedded = jnp.dot(steps_onehot, time_table, preferred_element_type=jnp.float32)
    start_sum = tokens.astype(jnp.float32) + embedded[:, None, :]
    normed_one, unit_one, inverse_one = norm_rows(start_sum, norm_gain[0], norm_bias[0])
    rows_self = spread_rows(normed_one.astype(jnp.bfloat16))
    row_count = rows_self.shape[1]
    head_shape = (batches, row_count, head_count, HEAD_DIM)
    projected = jnp.einsum(
        "scd,kdw->kscw", rows_self, proj_self, preferred_element_type=jnp.float32
    ).astype(jnp.bfloat16)
    queries, key_local, value_local = (projected[0], projected[1], projected[2])
    key_all, value_all = (
        lax.all_gather(key_local, "ctx", axis=1, tiled=True),
        lax.all_gather(value_local, "ctx", axis=1, tiled=True),
    )
    length = key_all.shape[1]
    key_span = min(512, length)
    query_pos = ctx_index * row_count + lax.iota(jnp.int32, row_count)
    keys_four = key_all.reshape(batches, length, head_count, HEAD_DIM)
    values_four = value_all.reshape(batches, length, head_count, HEAD_DIM)
    queries_four = queries.reshape(head_shape)
    attended, log_total = attend_forward(
        queries_four, keys_four, values_four, query_pos, prefix, key_span, factor
    )
    context_one = attended.reshape(batches, row_count, local_width).astype(jnp.bfloat16)
    branch_one = finish_branch(context_one, back_self)
    after_one = start_sum + branch_one
    normed_two, unit_two, inverse_two = norm_rows(after_one, norm_gain[1], norm_bias[1])
    rows_cross = spread_rows(normed_two.astype(jnp.bfloat16))
    cross_queries = jnp.einsum(
        "scd,dw->scw", rows_cross, proj_query, preferred_element_type=jnp.float32
    ).astype(jnp.bfloat16)
    enc_pair = jnp.einsum(
        "sed,kdw->ksew", encoder, proj_pair, preferred_element_type=jnp.float32
    ).astype(jnp.bfloat16)
    enc_count = encoder.shape[1]
    cross_keys = enc_pair[0].reshape(batches, enc_count, head_count, HEAD_DIM)
    cross_values = enc_pair[1].reshape(batches, enc_count, head_count, HEAD_DIM)
    cross_four = cross_queries.reshape(head_shape)
    cross_probs = jax.nn.softmax(
        jnp.einsum("sqhe,skhe->sqhk", cross_four, cross_keys, preferred_element_type=jnp.float32)
        * factor,
        axis=-1,
    )
    cross_low = cross_probs.astype(jnp.bfloat16)
    context_two = (
        jnp.einsum("sqhk,skhe->sqhe", cross_low, cross_values, preferred_element_type=jnp.float32)
        .reshape(batches, row_count, local_width)
        .astype(jnp.bfloat16)
    )
    branch_two = finish_branch(context_two, back_cross)
    after_two = after_one + branch_two
    normed_three, unit_three, inverse_three = norm_rows(after_two, norm_gain[2], norm_bias[2])
    rows_ffn = spread_rows(normed_three.astype(jnp.bfloat16))
    pre_act = jnp.einsum("scd,df->scf", rows_ffn, expand_full, preferred_element_type=jnp.float32)
    activated, slopes = gelu_parts(pre_act)
    hidden_low = activated.astype(jnp.bfloat16)
    branch_three = finish_branch(hidden_low, shrink_full)
    final_sum = after_two + branch_three
    grad_three = spread_grads(cotangent)
    grad_shrink = jnp.einsum(
        "scf,scd->fd", hidden_low, grad_three, preferred_element_type=jnp.float32
    )
    grad_pre = (
        jnp.einsum("scd,fd->scf", grad_three, shrink_full, preferred_element_type=jnp.float32)
        * slopes
    ).astype(jnp.bfloat16)
    grad_expand = jnp.einsum("scd,scf->df", rows_ffn, grad_pre, preferred_element_type=jnp.float32)
    back_three, gain_three, shift_three = norm_back(
        finish_grad(grad_pre, expand_full), unit_three, inverse_three, norm_gain[2]
    )
    grad_after_two = cotangent.astype(jnp.float32) + back_three
    grad_two = spread_grads(grad_after_two.astype(jnp.bfloat16))
    grad_back_cross = jnp.einsum(
        "scw,scd->wd", context_two, grad_two, preferred_element_type=jnp.float32
    )
    grad_context_two = jnp.einsum(
        "scd,wd->scw", grad_two, back_cross, preferred_element_type=jnp.float32
    ).astype(jnp.bfloat16)
    grad_cross_four = grad_context_two.reshape(head_shape)
    grad_cross_probs = jnp.einsum(
        "sqhe,skhe->sqhk", grad_cross_four, cross_values, preferred_element_type=jnp.float32
    )
    grad_cross_scores = (
        cross_probs
        * (grad_cross_probs - jnp.sum(cross_probs * grad_cross_probs, -1, keepdims=True))
    ).astype(jnp.bfloat16)
    grad_cross_q = (
        (
            jnp.einsum(
                "sqhk,skhe->sqhe", grad_cross_scores, cross_keys, preferred_element_type=jnp.float32
            )
            * factor
        )
        .reshape(batches, row_count, local_width)
        .astype(jnp.bfloat16)
    )
    part_keys = (
        jnp.einsum(
            "sqhk,sqhe->skhe", grad_cross_scores, cross_four, preferred_element_type=jnp.float32
        )
        * factor
    ).reshape(batches, enc_count, local_width)
    part_values = jnp.einsum(
        "sqhk,sqhe->skhe", cross_low, grad_cross_four, preferred_element_type=jnp.float32
    ).reshape(batches, enc_count, local_width)
    enc_keys, enc_values = (
        lax.psum_scatter(part_keys, "ctx", scatter_dimension=1, tiled=True),
        lax.psum_scatter(part_values, "ctx", scatter_dimension=1, tiled=True),
    )
    enc_keys = enc_keys.astype(jnp.bfloat16)
    enc_values = enc_values.astype(jnp.bfloat16)
    enc_share = enc_keys.shape[1]
    enc_rows = lax.dynamic_slice_in_dim(encoder, ctx_index * enc_share, enc_share, 1)
    grad_pair = jnp.stack(
        [
            jnp.einsum("sed,sew->dw", enc_rows, enc_keys, preferred_element_type=jnp.float32),
            jnp.einsum("sed,sew->dw", enc_rows, enc_values, preferred_element_type=jnp.float32),
        ]
    )
    encoder_grad = lax.psum_scatter(
        jnp.einsum("sew,dw->sed", enc_keys, proj_pair[0], preferred_element_type=jnp.float32)
        + jnp.einsum("sew,dw->sed", enc_values, proj_pair[1], preferred_element_type=jnp.float32),
        "tp",
        scatter_dimension=1,
        tiled=True,
    )
    grad_query_proj = jnp.einsum(
        "scd,scw->dw", rows_cross, grad_cross_q, preferred_element_type=jnp.float32
    )
    back_two, gain_two, shift_two = norm_back(
        finish_grad(grad_cross_q, proj_query), unit_two, inverse_two, norm_gain[1]
    )
    grad_after_one = grad_after_two + back_two
    grad_one = spread_grads(grad_after_one.astype(jnp.bfloat16))
    grad_back_self = jnp.einsum(
        "scw,scd->wd", context_one, grad_one, preferred_element_type=jnp.float32
    )
    grad_context_one = jnp.einsum(
        "scd,wd->scw", grad_one, back_self, preferred_element_type=jnp.float32
    ).astype(jnp.bfloat16)
    grad_ctx_four = grad_context_one.reshape(head_shape)
    delta_rows = jnp.sum(grad_ctx_four.astype(jnp.float32) * attended, -1)
    grad_query, grad_key_all, grad_value_all = key_sweep(
        queries_four,
        grad_ctx_four,
        log_total,
        delta_rows,
        keys_four,
        values_four,
        query_pos,
        prefix,
        key_span,
        factor,
    )
    own_keys, own_values = (
        lax.psum_scatter(grad_key_all, "ctx", scatter_dimension=0, tiled=True),
        lax.psum_scatter(grad_value_all, "ctx", scatter_dimension=0, tiled=True),
    )
    own_keys = jnp.transpose(own_keys, (1, 0, 2))
    own_values = jnp.transpose(own_values, (1, 0, 2))
    grad_joined = jnp.concatenate(
        [grad_query.reshape(batches, row_count, local_width), own_keys, own_values], -1
    ).astype(jnp.bfloat16)
    grad_proj_self = jnp.transpose(
        jnp.einsum(
            "scd,scw->dw", rows_self, grad_joined, preferred_element_type=jnp.float32
        ).reshape(model_width, 3, local_width),
        (1, 0, 2),
    )
    back_one, gain_one, shift_one = norm_back(
        finish_grad(grad_joined, local_stack), unit_one, inverse_one, norm_gain[0]
    )
    input_grad = grad_after_one + back_one
    shard_grads = (
        lax.psum_scatter(grad_proj_self, "fsdp", scatter_dimension=1, tiled=True),
        lax.psum_scatter(grad_query_proj, "fsdp", scatter_dimension=0, tiled=True),
        lax.psum_scatter(grad_pair, "fsdp", scatter_dimension=1, tiled=True),
        lax.psum_scatter(grad_back_self, "fsdp", scatter_dimension=1, tiled=True),
        lax.psum_scatter(grad_back_cross, "fsdp", scatter_dimension=1, tiled=True),
        lax.psum_scatter(grad_expand, "fsdp", scatter_dimension=0, tiled=True),
        lax.psum_scatter(grad_shrink, "fsdp", scatter_dimension=1, tiled=True),
    )
    full_grads = lax.psum(
        (
            shard_grads[0],
            shard_grads[1],
            shard_grads[2],
            shard_grads[3],
            shard_grads[4],
            shard_grads[5],
            shard_grads[6],
        ),
        "ctx",
    )
    squares = jnp.stack(
        [
            jnp.sum(final_sum * final_sum),
            jnp.sum(branch_one * branch_one),
            jnp.sum(branch_two * branch_two),
            jnp.sum(branch_three * branch_three),
        ]
    )
    gain_grad, bias_grad, square_totals = lax.psum(
        (
            jnp.stack([gain_one, gain_two, gain_three]),
            jnp.stack([shift_one, shift_two, shift_three]),
            squares,
        ),
        ("fsdp", "ctx", "tp"),
    )
    entries = (
        tokens.shape[0]
        * tokens.shape[1]
        * tokens.shape[2]
        * lax.axis_size("fsdp")
        * lax.axis_size("ctx")
        * lax.axis_size("tp")
    )
    norms = jnp.sqrt(square_totals / entries)
    return (
        final_sum,
        input_grad,
        encoder_grad,
        full_grads[0],
        full_grads[1],
        full_grads[2],
        full_grads[3],
        full_grads[4],
        full_grads[5],
        full_grads[6],
        gain_grad,
        bias_grad[:2],
        bias_grad[2],
        norms,
    )


def dot_of(left, right, left_dim, right_dim):
    return lax.dot_general(
        left, right, (((left_dim,), (right_dim,)), ((), ())), preferred_element_type=jnp.float32
    )


def bounds(prefix, start, query_span, key_span):
    whole = jnp.maximum(prefix, start + 1) // key_span
    every = (jnp.maximum(prefix, start + query_span) + key_span - 1) // key_span
    return whole, every


def hide(scores, limit, offset):
    return jnp.where(lax.broadcasted_iota(jnp.int32, scores.shape, 0) < limit - offset, scores, NEG)


def low(value):
    return value.astype(jnp.bfloat16)


STRIP = 64


def in_strips(work, *values, strip=STRIP, axis=0):
    count = values[0].shape[axis] // strip
    cut = lambda v, n: lax.slice_in_dim(v, n * strip, (n + 1) * strip, axis=axis)
    parts = [work(*[cut(v, n) for v in values]) for n in range(count)]
    return tuple(jnp.concatenate(p, axis) for p in zip(*parts))


def gelu_strip(inputs):
    activated, slopes = gelu_parts(inputs)
    return low(activated), slopes


def rows_unit(hidden):
    centre = hidden - jnp.mean(hidden, -1, keepdims=True)
    inverse = lax.rsqrt(jnp.mean(centre * centre, -1, keepdims=True) + EPS)
    return centre * inverse, inverse


def rows_norm(hidden, scaling, offsets):
    def strip(rows):
        unit_rows, inverse = rows_unit(rows)
        return low(unit_rows * scaling + offsets), unit_rows, inverse

    return in_strips(strip, hidden)


def rows_back(upstream, unit_rows, inverse, scaling):
    sums = [jnp.zeros((8, upstream.shape[1]), jnp.float32)] * 2

    def strip(rows, units, inverses):
        scaled = rows * scaling
        for n, term in enumerate((rows * units, rows)):
            sums[n] = sums[n] + jnp.sum(term.reshape(-1, 8, term.shape[1]), 0)
        return (
            inverses
            * (
                scaled
                - jnp.mean(scaled, -1, keepdims=True)
                - units * jnp.mean(scaled * units, -1, keepdims=True)
            ),
        )

    (result,) = in_strips(strip, upstream, unit_rows, inverse)
    return result, jnp.sum(sums[0], 0, keepdims=True), jnp.sum(sums[1], 0, keepdims=True)


MESH = pl.DeviceIdType.MESH


def meet(group, tp, fsdp):
    here, core, chip = lax.axis_index("fsdp"), lax.axis_index("ctx"), lax.axis_index("tp")
    me = core * tp + chip
    barrier = pltpu.get_barrier_semaphore()
    for k in range(1, group):
        other = me ^ k
        pl.semaphore_signal(
            barrier, inc=1, device_id={"ctx": other // tp, "tp": other % tp}, device_id_type=MESH
        )
    for k in range(1, fsdp):
        pl.semaphore_signal(barrier, inc=1, device_id={"fsdp": here ^ k}, device_id_type=MESH)
    pl.semaphore_wait(barrier, group - 1 + fsdp - 1)


def forward_kernel(
    prefix_ref,
    tokens_ref,
    step_ref,
    gain_ref,
    bias_ref,
    mine_ref,
    rows_out,
    qkv_ref,
    wide_ref,
    log_ref,
    ctx_ref,
    weight,
    rows_ref,
    other_ref,
    columns,
    pair_ref,
    keys_ref,
    values_ref,
    low_ref,
    landing,
    w_send,
    w_recv,
    v_send,
    v_recv,
    x_send,
    x_recv,
    c_send,
    c_recv,
    keep_sem,
    *,
    span,
    tp,
    fsdp,
):
    batches, chunk, width = tokens_ref.shape
    group = rows_ref.shape[0]
    length = group * chunk
    blocks, ratio = length // span, span // chunk
    wide_blocks = max(1, length // 2 // span)
    factor = HEAD_DIM**-0.5
    here, core, chip = lax.axis_index("fsdp"), lax.axis_index("ctx"), lax.axis_index("tp")
    me = core * tp + chip
    mine = chip // 2
    inner = (chip == 1) | (chip == 2)
    other_inner, other_outer = 2 - mine, 3 - 3 * mine
    meet(group, tp, fsdp)

    def send_to(source, target, send, recv, **place):
        return pltpu.make_async_remote_copy(
            src_ref=source,
            dst_ref=target,
            send_sem=send,
            recv_sem=recv,
            device_id=place,
            device_id_type=MESH,
        )

    v_core, v_chip = chip % 2, chip // 2 + 2 * core
    v_own = (v_core == core) & (v_chip == chip)
    v_copy = send_to(mine_ref, pair_ref, v_send.at[0], v_recv.at[0], ctx=v_core, tp=v_chip)

    @pl.when(v_own)
    def keep_pair():
        pair_ref[...] = mine_ref[...]

    @pl.when(jnp.logical_not(v_own))
    def send_pair():
        v_copy.start()

    comes = (chip // 2 != core) | (2 * (chip % 2) + core != chip)

    def w_copy(k):
        return send_to(pair_ref, columns.at[k], w_send.at[k], w_recv.at[k], fsdp=here ^ k)

    def normalise(seq, target, at):
        start_sum = tokens_ref[seq].astype(jnp.float32) + step_ref[seq]
        target[at] = rows_norm(start_sum, gain_ref[...], bias_ref[...])[0]

    def x_copy(kind):
        block = rows_ref.at[me]
        near = rows_ref.at[core * tp + (chip ^ 1)]
        second = rows_ref.at[core * tp + other_inner]
        third = rows_ref.at[core * tp + other_outer]
        source, place, target = (
            (block, me, {"tp": chip ^ 1}),
            (other_ref.at[0], me, {"tp": other_inner}),
            (block, me, {"ctx": 1 - core}),
            (near, core * tp + (chip ^ 1), {"ctx": 1 - core}),
            (second, core * tp + other_inner, {"ctx": 1 - core}),
            (third, core * tp + other_outer, {"ctx": 1 - core}),
            (second, core * tp + other_inner, {"tp": chip ^ 1}),
            (third, core * tp + other_outer, {"tp": chip ^ 1}),
            (other_ref.at[0], me, {"tp": other_outer}),
        )[kind]
        return send_to(source, rows_ref.at[place], x_send.at[kind], x_recv.at[place], **target)

    def x_wait(place):
        send_to(
            rows_ref.at[place], rows_ref.at[place], x_send.at[0], x_recv.at[place], ctx=1 - core
        ).wait_recv()

    def arrive(number):
        x_wait(core * tp + (chip ^ 1, other_inner, other_outer)[number])
        if number:

            @pl.when(inner & (core == 0))
            def onward():
                x_copy(5 + number).start()

        x_copy(3 + number).start()

    normalise(mine, rows_ref, me)
    normalise(1 - mine, other_ref, 0)

    @pl.when(core == 0)
    def first_half():
        x_copy(2).start()

        @pl.when(inner)
        def from_inner():
            x_copy(1).start()
            x_copy(0).start()

        @pl.when(jnp.logical_not(inner))
        def from_outer():
            x_copy(0).start()

    @pl.when(comes)
    def pair_here():
        v_copy.wait_recv()

    for k in range(1, fsdp):
        w_copy(k).start()
    values_ref[:, HEAD_DIM:, :] = jnp.ones_like(values_ref[:, HEAD_DIM:, :])

    def project(place, unused):
        rows = rows_ref[place]
        joined = low(dot_of(weight[...], rows, 1, 1))
        at = pl.ds(pl.multiple_of(place * chunk, chunk), chunk)
        for head in range(2):
            queries, keys, values = (
                joined[(3 * head + n) * HEAD_DIM : (3 * head + n + 1) * HEAD_DIM] for n in range(3)
            )
            qkv_ref[head, :HEAD_DIM, at] = queries * jnp.bfloat16(factor)
            qkv_ref[head, HEAD_DIM : 2 * HEAD_DIM, at] = keys
            qkv_ref[head, 2 * HEAD_DIM :, at] = values
            values_ref[head, :HEAD_DIM, at] = values
            keys_ref[head, at, :] = keys.T
        return unused

    @pl.when(core == 0)
    def first_lines():
        @pl.when(jnp.logical_not(inner))
        def then_other():
            x_copy(0).wait_send()
            x_copy(1).start()

        for number in range(3):
            arrive(number)

    @pl.when(core == 1)
    def second_lines():
        for place in range(tp):
            x_wait(place)
        for kind in (2, 1, 8, 0):
            x_copy(kind).start()

    piece = mine_ref.shape[1]
    for k in range(fsdp):
        if k:
            w_copy(k).wait_recv()
        part = columns[k] if k else pair_ref[...]
        for f in range(fsdp):

            @pl.when((here ^ k) == f)
            def place(f=f, part=part):
                weight[:, f * piece : (f + 1) * piece] = part

    lax.fori_loop(0, tp, project, 0)

    def c_copy(head, place):
        return send_to(
            low_ref.at[head, place],
            landing.at[head, me],
            c_send.at[head, place],
            c_recv.at[head, me],
            ctx=place // tp,
            tp=place % tp,
        )

    def c_wait(head, place):
        send_to(
            low_ref.at[head, place],
            landing.at[head, place],
            c_send.at[head, place],
            c_recv.at[head, place],
            ctx=place // tp,
            tp=place % tp,
        ).wait_recv()

    def attend(index, unused):
        block, head = index // 2, index % 2

        @pl.when((core == 1) & (index == 3))
        def near_lines():
            arrive(0)

        @pl.when(index == 4)
        def second_half():
            @pl.when(core == 0)
            def wait_other():
                for place in range(tp, group):
                    x_wait(place)

            @pl.when(core == 1)
            def far_lines():
                arrive(1)
                arrive(2)

            lax.fori_loop(tp, group, project, 0)

        start = pl.multiple_of(block * span, span)
        queries = qkv_ref[head, :HEAD_DIM, pl.ds(start, span)]
        limit = jnp.maximum(
            prefix_ref[mine], start + 1 + lax.broadcasted_iota(jnp.int32, (1, span), 1)
        )

        def advance(other, carry, masked):
            highest, total = carry
            offset = pl.multiple_of(other * span, span)
            scores = dot_of(keys_ref[head, pl.ds(offset, span), :], queries, 1, 0)
            if masked:
                scores = hide(scores, limit, offset)
            higher = jnp.maximum(highest, jnp.max(scores, axis=0, keepdims=True))
            weights = low(jnp.exp(scores - higher))
            fading = jnp.exp(highest - higher)
            total = total * fading + dot_of(
                values_ref[head, :, pl.ds(offset, span)], weights, 1, 0
            )
            return higher, total

        carry = (
            jnp.full((1, span), NEG, jnp.float32),
            jnp.zeros((values_ref.shape[1], span), jnp.float32),
        )
        carry = lax.fori_loop(0, block, lambda j, c: advance(j, c, False), carry)
        highest, total = lax.fori_loop(
            block, jnp.maximum(block + 1, wide_blocks), lambda j, c: advance(j, c, True), carry
        )
        weight_sum = total[HEAD_DIM : HEAD_DIM + 1, :]
        attended = total[:HEAD_DIM, :] / weight_sum
        wide_ref[head, :, pl.ds(start, span)] = attended
        log_ref[head, :, pl.ds(start, span)] = highest + jnp.log(weight_sum)
        attended = low(attended)
        for part in range(ratio):
            place = block * ratio + part
            low_ref[head, place] = attended[:, part * chunk : (part + 1) * chunk]

            @pl.when(place != me)
            def send(place=place):
                c_copy(head, place).start()

        return unused

    lax.fori_loop(0, 2 * blocks, attend, 0)
    keep = pltpu.make_async_copy(rows_ref, rows_out, keep_sem)
    keep.start()
    for head in range(2):

        def collect(k, unused, head=head):
            c_wait(head, me ^ k)
            ctx_ref[head, me ^ k] = landing[head, me ^ k]
            return unused

        lax.fori_loop(1, group, collect, 0)
        ctx_ref[head, me] = low_ref[head, me]
    for k in range(1, fsdp):
        w_copy(k).wait_send()

    @pl.when(jnp.logical_not(v_own))
    def pair_sent():
        v_copy.wait_send()

    for kind in range(1, 6):
        x_copy(kind).wait_send()

    @pl.when(inner | (core == 1))
    def own_sent():
        x_copy(0).wait_send()

    @pl.when(inner & (core == 0))
    def lines_sent():
        x_copy(6).wait_send()
        x_copy(7).wait_send()

    @pl.when(core == 1)
    def direct_sent():
        x_copy(8).wait_send()

    for head in range(2):

        def sent(k, unused, head=head):
            c_copy(head, me ^ k).wait_send()
            return unused

        lax.fori_loop(1, group, sent, 0)
    keep.wait()


def forward_group(prefix, tokens, steps, gain, bias, mine, span, group, tp, fsdp):
    batches, chunk, width = tokens.shape
    length = group * chunk
    bf16, f32 = jnp.bfloat16, jnp.float32
    struct = jax.ShapeDtypeStruct
    inside = pl.BlockSpec(memory_space=pltpu.VMEM)
    dma = pltpu.SemaphoreType.DMA
    return pl.pallas_call(
        functools.partial(forward_kernel, span=span, tp=tp, fsdp=fsdp),
        in_specs=[pl.BlockSpec(memory_space=pltpu.SMEM)] + [inside] * 5,
        out_specs=[pl.BlockSpec(memory_space=pl.ANY)] + [inside] * 5,
        out_shape=[
            struct((group, chunk, width), bf16),
            struct((2, 3 * HEAD_DIM, length), bf16),
            struct((2, HEAD_DIM, length), f32),
            struct((2, 1, length), f32),
            struct((2, group, HEAD_DIM, chunk), bf16),
            struct((6 * HEAD_DIM, width), bf16),
        ],
        scratch_shapes=[
            pltpu.VMEM((group, chunk, width), bf16),
            pltpu.VMEM((1, chunk, width), bf16),
            pltpu.VMEM((fsdp,) + mine.shape, bf16),
            pltpu.VMEM(mine.shape, bf16),
            pltpu.VMEM((2, length, HEAD_DIM), bf16),
            pltpu.VMEM((2, HEAD_DIM + 16, length), bf16),
            pltpu.VMEM((2, group, HEAD_DIM, chunk), bf16),
            pltpu.VMEM((2, group, HEAD_DIM, chunk), bf16),
            dma((fsdp,)),
            dma((fsdp,)),
            dma((1,)),
            dma((1,)),
            dma((9,)),
            dma((group,)),
            dma((2, group)),
            dma((2, group)),
            dma,
        ],
        compiler_params=pltpu.CompilerParams(
            vmem_limit_bytes=VMEM_LIMIT, collective_id=1, has_side_effects=True
        ),
        cost_estimate=pl.CostEstimate(
            flops=60_000_000_000, bytes_accessed=30_000_000, transcendentals=20_000_000
        ),
        name="forward_group",
    )(prefix, tokens, steps, gain, bias, mine)


QUERY, KEY, VALUE, SELF_OUT, CROSS_OUT, UP, DOWN = 0, 1, 2, 3, 4, 5, 9


def middle_kernel(
    gathered,
    tokens_ref,
    step_ref,
    enc_ref,
    cot_ref,
    gain_ref,
    bias_ref,
    ctx_ref,
    final_ref,
    after_ref,
    back_ref,
    enc_grad_ref,
    stats_ref,
    packed_ref,
    weights,
    totals,
    context,
    queries,
    keys,
    values,
    probs,
    context_two,
    grad_heads,
    grad_queries,
    grad_keys,
    grad_values,
    back_rows,
    landing,
    d_send,
    d_recv,
    sem,
    *,
    tp,
    fsdp,
):
    batches, chunk, width = tokens_ref.shape
    group = landing.shape[1]
    core, chip = lax.axis_index("ctx"), lax.axis_index("tp")
    me = core * tp + chip
    mine = chip // 2
    meet(group, tp, fsdp)
    piece = gathered.shape[-1]
    factor = HEAD_DIM**-0.5
    heads = width // HEAD_DIM

    copies = []
    for f in range(width // piece):
        for c in range(group // tp):
            for t in range(tp):
                head = t * (group // tp) + c
                copies.append(
                    pltpu.make_async_copy(
                        gathered.at[f, c, t, pl.ds(3, weights.shape[0])],
                        weights.at[:, pl.ds(head * HEAD_DIM, HEAD_DIM), pl.ds(f * piece, piece)],
                        sem.at[(f * group // tp + c) * tp + t],
                    )
                )
    for copy in copies:
        copy.start()
    totals[...] = jnp.zeros_like(totals)
    stats_ref[...] = jnp.zeros_like(stats_ref)
    for copy in copies:
        copy.wait()

    owners = [(2 * (2 * z + c) + n, n, c * tp + z) for z in (0, 1) for c in (0, 1) for n in (0, 1)]

    def d_copy(turn, seq, head, number, owner):
        return pltpu.make_async_remote_copy(
            src_ref=back_rows.at[turn, pl.ds(head * HEAD_DIM, HEAD_DIM)],
            dst_ref=landing.at[number, me],
            send_sem=d_send.at[turn, head],
            recv_sem=d_recv.at[number, me],
            device_id={"ctx": owner // tp, "tp": owner % tp + 2 * seq},
            device_id_type=MESH,
        )

    def one_sequence(turn, unused):
        seq = jnp.where(turn == 0, 1 - mine, mine)
        for head, number, owner in owners:
            context[head * HEAD_DIM : (head + 1) * HEAD_DIM, :] = ctx_ref[number, owner + 2 * seq]
        start_sum = tokens_ref[seq].astype(jnp.float32) + step_ref[seq]
        branch_one = dot_of(context[...], weights[SELF_OUT], 0, 0)
        after_one = start_sum + branch_one
        stats_ref[1:2, :] += jnp.sum(branch_one * branch_one, 0, keepdims=True)
        normed_two, unit_two, inverse_two = rows_norm(after_one, gain_ref[1:2], bias_ref[1:2])
        queries[...] = low(dot_of(weights[QUERY], normed_two, 1, 1))
        keys[...] = low(dot_of(weights[KEY], enc_ref[seq], 1, 1))
        values[...] = low(dot_of(weights[VALUE], enc_ref[seq], 1, 1))

        def attend(head, unused):
            rows = pl.ds(pl.multiple_of(head * HEAD_DIM, HEAD_DIM), HEAD_DIM)
            scores = dot_of(keys[rows, :].T, queries[rows, :], 1, 0) * factor

            def strip(columns):
                powers = jnp.exp(columns - jnp.max(columns, 0, keepdims=True))
                return (powers / jnp.sum(powers, 0, keepdims=True),)

            (attn,) = in_strips(strip, scores, strip=128, axis=1)
            probs[head] = attn
            context_two[rows, :] = low(dot_of(values[rows, :], low(attn), 1, 0))
            return unused

        lax.fori_loop(0, heads, attend, 0, unroll=8)
        branch_two = dot_of(context_two[...], weights[CROSS_OUT], 0, 0)
        after_two = after_one + branch_two
        stats_ref[2:3, :] += jnp.sum(branch_two * branch_two, 0, keepdims=True)
        normed_three, unit_three, inverse_three = rows_norm(after_two, gain_ref[2:3], bias_ref[2:3])
        grad_three = cot_ref[seq]

        def feed(part, carry):
            branch, grad = carry
            up, down = weights[UP + part], weights[DOWN + part]
            inputs = dot_of(up, normed_three, 1, 1)
            hidden, slopes = in_strips(gelu_strip, inputs, strip=32)
            branch = branch + dot_of(hidden, down, 0, 0)
            totals[DOWN - 2 + part] += dot_of(hidden, grad_three, 1, 0)
            grad_pre = low(dot_of(down, grad_three, 1, 1) * slopes)
            totals[UP - 2 + part] += dot_of(grad_pre, normed_three, 1, 0)
            return branch, grad + dot_of(grad_pre, up, 0, 0)

        blank = jnp.zeros((chunk, width), jnp.float32)
        branch_three, grad_norm = lax.fori_loop(0, DOWN - UP, feed, (blank, blank), unroll=4)
        final_sum = after_two + branch_three
        final_ref[seq] = final_sum
        stats_ref[0:1, :] += jnp.sum(final_sum * final_sum, 0, keepdims=True)
        stats_ref[3:4, :] += jnp.sum(branch_three * branch_three, 0, keepdims=True)
        back, gain_sum, bias_sum = rows_back(grad_norm, unit_three, inverse_three, gain_ref[2:3])
        stats_ref[6:7, :] += gain_sum
        stats_ref[7:8, :] += bias_sum
        grad_after_two = grad_three.astype(jnp.float32) + back
        grad_two = low(grad_after_two)
        totals[2] += dot_of(context_two[...], grad_two, 1, 0)
        grad_heads[...] = low(dot_of(weights[CROSS_OUT], grad_two, 1, 1))

        def attend_back(head, unused):
            rows = pl.ds(pl.multiple_of(head * HEAD_DIM, HEAD_DIM), HEAD_DIM)
            grads = grad_heads[rows, :]
            attn = probs[head]
            grad_probs = dot_of(values[rows, :].T, grads, 1, 0)

            def strip(ones, others):
                return (low(ones * (others - jnp.sum(ones * others, 0, keepdims=True))),)

            (grad_scores,) = in_strips(strip, attn, grad_probs, strip=128, axis=1)
            grad_queries[rows, :] = low(dot_of(keys[rows, :], grad_scores, 1, 0) * factor)
            grad_keys[rows, :] = dot_of(queries[rows, :], grad_scores, 1, 1) * factor
            grad_values[rows, :] = dot_of(grads, low(attn), 1, 1)
            return unused

        lax.fori_loop(0, heads, attend_back, 0, unroll=8)
        enc_grad_ref[seq, :, :width] = low(grad_keys[...].T)
        enc_grad_ref[seq, :, width:] = low(grad_values[...].T)
        totals[0] += dot_of(grad_queries[...], normed_two, 1, 0)
        upstream = dot_of(grad_queries[...], weights[QUERY], 0, 0)
        back, gain_sum, bias_sum = rows_back(upstream, unit_two, inverse_two, gain_ref[1:2])
        stats_ref[4:5, :] += gain_sum
        stats_ref[5:6, :] += bias_sum
        grad_after_one = grad_after_two + back
        after_ref[seq] = grad_after_one
        grad_one = low(grad_after_one)
        totals[1] += dot_of(context[...], grad_one, 1, 0)
        context[...] = low(dot_of(weights[SELF_OUT], grad_one, 1, 1))
        back_rows[turn] = context[...]
        for head, number, owner in owners:

            @pl.when(owner + 2 * seq != me)
            def give(head=head, number=number, owner=owner):
                d_copy(turn, seq, head, number, owner).start()

            @pl.when(owner + 2 * seq == me)
            def keep(head=head, number=number):
                back_ref[number, me] = context[head * HEAD_DIM : (head + 1) * HEAD_DIM, :]

        return unused


    lax.fori_loop(0, batches, one_sequence, 0)
    for f in range(width // piece):
        for c in range(group // tp):
            for t in range(tp):
                head = t * (group // tp) + c
                packed_ref[c, f, t] = low(
                    totals[
                        :,
                        head * HEAD_DIM : (head + 1) * HEAD_DIM,
                        f * piece : (f + 1) * piece,
                    ]
                )

    def collect(k, unused):
        place = me ^ k
        for number in range(2):
            pltpu.make_async_remote_copy(
                src_ref=landing.at[number, place],
                dst_ref=landing.at[number, place],
                send_sem=d_send.at[0, 0],
                recv_sem=d_recv.at[number, place],
                device_id={"ctx": place // tp, "tp": place % tp},
                device_id_type=MESH,
            ).wait_recv()
            back_ref[number, place] = landing[number, place]
        return unused

    lax.fori_loop(1, group, collect, 0)
    for turn in range(batches):
        seq = 1 - mine if turn == 0 else mine
        for head, number, owner in owners:

            @pl.when(owner + 2 * seq != me)
            def given(turn=turn, seq=seq, head=head, number=number, owner=owner):
                d_copy(turn, seq, head, number, owner).wait_send()


def middle(
    gathered, tokens, steps, encoder, cotangent, gains, biases, contexts, tp, fsdp
):
    batches, chunk, width = tokens.shape
    group = contexts.shape[1]
    enc_count = encoder.shape[1]
    heads = width // HEAD_DIM
    bf16, f32 = jnp.bfloat16, jnp.float32
    struct = jax.ShapeDtypeStruct
    inside = pl.BlockSpec(memory_space=pltpu.VMEM)
    dma = pltpu.SemaphoreType.DMA
    count = gathered.shape[3] - 3
    packed = (group // tp, gathered.shape[0], tp, count - 2) + gathered.shape[4:]
    return pl.pallas_call(
        functools.partial(middle_kernel, tp=tp, fsdp=fsdp),
        in_specs=[pl.BlockSpec(memory_space=pl.ANY)] + [inside] * 7,
        out_specs=[inside] * 6,
        out_shape=[
            struct((batches, chunk, width), f32),
            struct((batches, chunk, width), f32),
            struct((2, group, HEAD_DIM, chunk), bf16),
            struct((batches, enc_count, 2 * width), bf16),
            struct((8, width), f32),
            struct(packed, bf16),
        ],
        scratch_shapes=[
            pltpu.VMEM((count, width, width), bf16),
            pltpu.VMEM((count - 2, width, width), f32),
            pltpu.VMEM((width, chunk), bf16),
            pltpu.VMEM((width, chunk), bf16),
            pltpu.VMEM((width, enc_count), bf16),
            pltpu.VMEM((width, enc_count), bf16),
            pltpu.VMEM((heads, enc_count, chunk), f32),
            pltpu.VMEM((width, chunk), bf16),
            pltpu.VMEM((width, chunk), bf16),
            pltpu.VMEM((width, chunk), bf16),
            pltpu.VMEM((width, enc_count), f32),
            pltpu.VMEM((width, enc_count), f32),
            pltpu.VMEM((batches, width, chunk), bf16),
            pltpu.VMEM((2, group, HEAD_DIM, chunk), bf16),
            dma((batches, heads)),
            dma((2, group)),
            dma((32,)),
        ],
        compiler_params=pltpu.CompilerParams(
            vmem_limit_bytes=VMEM_LIMIT, collective_id=3, has_side_effects=True
        ),
        cost_estimate=pl.CostEstimate(
            flops=30_000_000_000, bytes_accessed=30_000_000, transcendentals=10_000_000
        ),
        name="middle",
    )(gathered, tokens, steps, encoder, cotangent, gains, biases, contexts)


def backward_kernel(
    prefix_ref,
    enc_parts,
    packed,
    gathered,
    rows_in,
    landing,
    weight,
    qkv_ref,
    wide_ref,
    log_ref,
    tokens_ref,
    step_ref,
    gain_ref,
    after_ref,
    enc_ref,
    stats_ref,
    input_ref,
    enc_out,
    self_out,
    query_out,
    pair_out,
    back_out,
    cross_out,
    up_out,
    down_out,
    sums_out,
    outgoing,
    core_rows,
    core_rows_landing,
    sum_rows,
    incoming,
    queries_ref,
    pairs_ref,
    grad_ref,
    delta_ref,
    grad_pairs_ref,
    rows_ref,
    pair_weights,
    enc_own,
    enc_core,
    enc_sum,
    enc_landing,
    pair_ref,
    pair_landing,
    core_landing,
    partial_ref,
    fsdp_landing,
    line_ref,
    line_landing,
    shard_ref,
    head_ref,
    head_landing,
    head_pair,
    head_two,
    sums_ref,
    sums_landing,
    sums_two,
    e_send,
    e_recv,
    x_send,
    x_recv,
    i_send,
    i_recv,
    r_send,
    r_recv,
    f_send,
    f_recv,
    t_send,
    t_recv,
    h_send,
    h_recv,
    p_send,
    p_recv,
    s_send,
    s_recv,
    local_sem,
    rows_sem,
    *,
    span,
    tp,
    fsdp,
):
    batches, chunk, width = tokens_ref.shape
    group = landing.shape[1]
    length = group * chunk
    blocks, ratio = length // span, span // chunk
    wide_blocks = max(1, length // 2 // span)
    factor = HEAD_DIM**-0.5
    here, core, chip = lax.axis_index("fsdp"), lax.axis_index("ctx"), lax.axis_index("tp")
    me = core * tp + chip
    mine = chip // 2
    cores = group // tp
    share = enc_landing.shape[2]
    piece = width // fsdp
    early = packed.shape[3]
    meet(group, tp, fsdp)

    def send_to(source, target, send, recv, **place):
        return pltpu.make_async_remote_copy(
            src_ref=source,
            dst_ref=target,
            send_sem=send,
            recv_sem=recv,
            device_id=place,
            device_id_type=MESH,
        )

    def member(place):
        return {"ctx": place // tp, "tp": place % tp}

    local = [
        pltpu.make_async_copy(
            packed.at[core], partial_ref.at[:, :, pl.ds(0, early)], local_sem.at[0]
        ),
        pltpu.make_async_copy(
            enc_parts.at[:, pl.ds(pl.multiple_of(core * tp * share, share), tp * share)],
            enc_own,
            local_sem.at[1],
        ),
    ]
    first = len(local)
    for f in range(fsdp):
        for c in range(cores):
            for t in range(tp):
                head = t * cores + c
                local.append(
                    pltpu.make_async_copy(
                        gathered.at[f, c, t, pl.ds(3 + KEY, 2)],
                        pair_weights.at[
                            :, pl.ds(head * HEAD_DIM, HEAD_DIM), pl.ds(f * piece, piece)
                        ],
                        local_sem.at[first + (f * cores + c) * tp + t],
                    )
                )
    enc_copy = send_to(
        enc_parts.at[:, pl.ds(pl.multiple_of((1 - core) * tp * share, share), tp * share)],
        enc_core,
        e_send.at[0],
        e_recv.at[0],
        ctx=1 - core,
    )
    enc_line = [
        send_to(
            enc_sum.at[chip ^ n], enc_landing.at[n - 1], e_send.at[n], e_recv.at[n], tp=chip ^ n
        )
        for n in range(1, tp)
    ]

    core_copy = send_to(
        packed.at[1 - core], core_landing, r_send.at[0], r_recv.at[0], ctx=1 - core
    )
    pair_copy = send_to(
        pair_ref.at[1 - core], pair_landing, r_send.at[1], r_recv.at[1], ctx=1 - core
    )
    shard_copy = send_to(
        shard_ref.at[core], shard_ref.at[core], r_send.at[2], r_recv.at[2], ctx=1 - core
    )
    shard_wait = send_to(
        shard_ref.at[1 - core], shard_ref.at[1 - core], r_send.at[2], r_recv.at[2], ctx=1 - core
    )
    f_copies = [
        send_to(
            partial_ref.at[here ^ n, :, pl.ds(0, early)],
            fsdp_landing.at[n - 1, :, pl.ds(0, early)],
            f_send.at[n],
            f_recv.at[n],
            fsdp=here ^ n,
        )
        for n in range(1, fsdp)
    ]
    f_pairs = [
        send_to(
            partial_ref.at[here ^ n, :, pl.ds(early, 2)],
            fsdp_landing.at[n - 1, :, pl.ds(early, 2)],
            f_send.at[fsdp + n],
            f_recv.at[fsdp + n],
            fsdp=here ^ n,
        )
        for n in range(1, fsdp)
    ]
    t_copies = [
        send_to(line_ref.at[chip ^ k], line_landing.at[k - 1], t_send.at[k], t_recv.at[k], tp=chip ^ k)
        for k in range(1, tp)
    ]
    h_copies = [
        send_to(
            head_ref.at[here ^ k], head_landing.at[k - 1], h_send.at[k], h_recv.at[k], fsdp=here ^ k
        )
        for k in range(1, fsdp)
    ]

    pair_chip = 2 * (chip % 2) + core
    p_copies = [
        send_to(head_pair, head_two.at[mine], p_send.at[c], p_recv.at[mine], ctx=c, tp=pair_chip)
        for c in range(2)
    ]
    p_waits = [
        send_to(head_pair, head_two.at[n], p_send.at[0], p_recv.at[n], ctx=c, tp=t)
        for n, c, t in ((0, chip % 2, chip // 2), (1, chip % 2, chip // 2 + 2))
    ]
    p_here = [
        (core == chip % 2) & (chip == chip // 2 + 2 * n) for n in range(2)
    ]

    def s_copy(k):
        return send_to(
            sums_ref, sums_landing.at[k], s_send.at[k], s_recv.at[k], **member(me ^ k)
        )

    s_fsdp = [
        send_to(
            sums_two, sums_landing.at[group + k], s_send.at[group + k], s_recv.at[group + k], fsdp=here ^ k
        )
        for k in range(1, fsdp)
    ]

    enc_copy.start()
    core_copy.start()
    for copy in local:
        copy.start()

    def core_rows_copy(place):
        slot = place % tp
        return send_to(
            core_rows.at[slot], core_rows_landing.at[slot], x_send.at[slot], x_recv.at[slot], ctx=1 - core
        )

    def owner_copy(place):
        slot = place % tp
        return send_to(
            sum_rows.at[slot],
            incoming.at[mine, chip % 2],
            i_send.at[slot],
            i_recv.at[mine, chip % 2],
            tp=slot,
        )

    def spread(place):
        upstream = dot_of(outgoing[place].reshape(6 * HEAD_DIM, chunk), weight[...], 0, 0)
        slot = place % tp

        @pl.when(place // tp != core)
        def hand_over():
            core_rows[slot] = low(upstream)
            core_rows_copy(place).start()

        @pl.when(place // tp == core)
        def collect():
            core_rows_copy(place).wait_recv()
            total = low(upstream + core_rows_landing[slot].astype(jnp.float32))

            @pl.when(place == me)
            def own():
                incoming[mine, chip % 2] = total

            @pl.when(place != me)
            def send():
                sum_rows[slot] = total
                owner_copy(place).start()

    def prepare(seq):
        def lay(place, unused):
            at = pl.ds(pl.multiple_of(place * chunk, chunk), chunk)
            grads = landing[seq, place]
            blank = jnp.zeros_like(grads)
            grad_ref[seq, at, :] = jnp.concatenate([blank, grads], 0).T
            delta_ref[seq, :, at] = jnp.sum(
                grads.astype(jnp.float32) * wide_ref[seq, :, at], axis=0, keepdims=True
            )
            queries_ref[seq, at, :] = jnp.concatenate([qkv_ref[seq, :HEAD_DIM, at], blank], 0).T
            pairs_ref[seq, at, :] = qkv_ref[seq, HEAD_DIM:, at].T
            return unused

        lax.fori_loop(0, group, lay, 0)
        grad_pairs_ref[seq] = jnp.zeros(grad_pairs_ref.shape[1:], jnp.float32)

    def encoder_cores():
        local[1].wait()
        enc_copy.wait_recv()
        for t in range(tp):
            lines = slice(t * share, (t + 1) * share)
            enc_sum[t] = low(
                enc_own[:, lines].astype(jnp.float32) + enc_core[:, lines].astype(jnp.float32)
            )
        for copy in enc_line:
            copy.start()

    def encoder_part():
        total = enc_sum[chip].astype(jnp.float32)
        for n, copy in enumerate(enc_line):
            copy.wait_recv()
            total = total + enc_landing[n].astype(jnp.float32)
        for copy in local[first:]:
            copy.wait()
        grads = low(total)
        enc_rows = enc_ref[:, pl.ds(pl.multiple_of(me * share, share), share), :]
        flat, enc_flat = grads.reshape(batches * share, 2 * width), enc_rows.reshape(
            batches * share, width
        )
        result = dot_of(flat[:, :width], pair_weights[0], 1, 0) + dot_of(
            flat[:, width:], pair_weights[1], 1, 0
        )
        enc_out[...] = result.reshape(batches, share, width)
        for which in range(2):
            grad = low(dot_of(flat[:, which * width : (which + 1) * width], enc_flat, 0, 0))
            for f in range(fsdp):
                for c in range(cores):
                    for t in range(tp):
                        head = t * cores + c
                        pair_ref[c, f, t, which] = grad[
                            head * HEAD_DIM : (head + 1) * HEAD_DIM, f * piece : (f + 1) * piece
                        ]
        pair_copy.start()

    def sum_cores():
        local[0].wait()
        core_copy.wait_recv()

        def one(f, unused):
            def two(t, unused):
                partial_ref[f, t, :early] = low(
                    partial_ref[f, t, :early].astype(jnp.float32)
                    + core_landing[f, t].astype(jnp.float32)
                )
                return unused

            return lax.fori_loop(0, tp, two, unused)

        lax.fori_loop(0, fsdp, one, 0)
        for copy in f_copies:
            copy.start()

    def sum_pairs():
        pair_copy.wait_recv()
        for f in range(fsdp):
            for t in range(tp):
                partial_ref[f, t, early:] = low(
                    pair_ref[core, f, t].astype(jnp.float32)
                    + pair_landing[f, t].astype(jnp.float32)
                )
        for copy in f_pairs:
            copy.start()

    def sum_fsdp():
        for copy in f_copies + f_pairs:
            copy.wait_recv()

        def one(t, unused):
            total = partial_ref[here, t].astype(jnp.float32)
            for k in range(fsdp - 1):
                total = total + fsdp_landing[k, t].astype(jnp.float32)
            line_ref[t] = low(total)
            return unused

        lax.fori_loop(0, tp, one, 0)
        for copy in t_copies:
            copy.start()

    def sum_line():
        for copy in t_copies:
            copy.wait_recv()
        total = line_ref[chip].astype(jnp.float32)
        for k in range(tp - 1):
            total = total + line_landing[k].astype(jnp.float32)
        shard_ref[core] = total
        shard_copy.start()

    for head in range(2):
        prepare(head)

    def attend(index, unused):
        block, seq = blocks - 1 - index // 2, index % 2

        def hook(at, work):
            @pl.when(index == at)
            def run():
                work()

        hook(1, encoder_cores)
        hook(1, sum_cores)
        hook(2, encoder_part)
        hook(3, sum_pairs)
        hook(5, sum_fsdp)
        start = pl.multiple_of(block * span, span)
        at = pl.ds(start, span)
        blank = jnp.zeros((HEAD_DIM, span), jnp.bfloat16)
        queries_t = jnp.concatenate([qkv_ref[seq, :HEAD_DIM, at], blank], 0)
        queries = queries_ref[seq, at, :]
        grads = grad_ref[seq, at, :]
        grads_t = jnp.concatenate(
            [landing[seq, block * ratio + part] for part in range(ratio)], 1
        )
        grads_t = jnp.concatenate([blank, grads_t], 0)
        logs, deltas = log_ref[seq, :, at], delta_ref[seq, :, at]
        limit = jnp.maximum(
            prefix_ref[mine], start + 1 + lax.broadcasted_iota(jnp.int32, (1, span), 1)
        )

        def advance(other, grad_queries, masked):
            offset = pl.multiple_of(other * span, span)
            there = pl.ds(offset, span)
            pairs = pairs_ref[seq, there, :]
            scores = dot_of(pairs, queries_t, 1, 0)
            if masked:
                scores = hide(scores, limit, offset)
            probs = jnp.exp(scores - logs)
            grad_probs = dot_of(pairs, grads_t, 1, 0)
            grad_scores = low(probs * (grad_probs - deltas))
            grad_pairs_ref[seq, there, :] += dot_of(low(probs), grads, 1, 0) + dot_of(
                grad_scores, queries, 1, 0
            )
            return grad_queries + dot_of(
                qkv_ref[seq, HEAD_DIM : 2 * HEAD_DIM, there], grad_scores, 1, 0
            )

        grad_queries = jnp.zeros((HEAD_DIM, span), jnp.float32)
        grad_queries = lax.fori_loop(0, block, lambda j, c: advance(j, c, False), grad_queries)
        grad_queries = lax.fori_loop(
            block, jnp.maximum(block + 1, wide_blocks), lambda j, c: advance(j, c, True), grad_queries
        )
        done = low(grad_queries * factor)
        for part in range(ratio):
            place = block * ratio + part
            outgoing[place, seq, :HEAD_DIM, :] = done[:, part * chunk : (part + 1) * chunk]

        lowest = jnp.where(block == 0, 0, block)
        highest = jnp.where(
            block == 0, wide_blocks, jnp.where(block >= wide_blocks, block + 1, block)
        )

        def give(place, unused):
            at = pl.ds(pl.multiple_of(place * chunk, chunk), chunk)
            outgoing[place, seq, HEAD_DIM:, :] = low(grad_pairs_ref[seq, at, :].T)
            return unused

        lax.fori_loop(lowest * ratio, highest * ratio, give, 0)

        @pl.when(seq == 1)
        def both_heads():
            def one(place, unused):
                spread(place)
                return unused

            lax.fori_loop(lowest * ratio, highest * ratio, one, 0)

        return unused

    lax.fori_loop(0, 2 * blocks, attend, 0)
    sums_ref[...] = jnp.zeros_like(sums_ref)
    sums_ref[:8, :] = stats_ref[...]

    def rows_copy(number):
        return pltpu.make_async_copy(
            rows_in.at[number],
            rows_ref.at[number % rows_ref.shape[0]],
            rows_sem.at[number % rows_ref.shape[0]],
        )

    depth = rows_ref.shape[0]
    for number in range(depth):
        rows_copy(number).start()

    def weigh(number, total):
        rows_copy(number).wait()
        total = total + dot_of(
            outgoing[number].reshape(6 * HEAD_DIM, chunk), rows_ref[number % depth], 1, 0
        )

        @pl.when(number + depth < group)
        def more():
            rows_copy(number + depth).start()

        return total

    total = lax.fori_loop(
        0, group, weigh, jnp.zeros((6 * HEAD_DIM, width), jnp.float32)
    )
    for f in range(fsdp):
        head_ref[f] = total[:, f * piece : (f + 1) * piece]
    for copy in h_copies:
        copy.start()
    sum_line()

    for copy in h_copies:
        copy.wait_recv()
    total = head_ref[here]
    for k in range(fsdp - 1):
        total = total + head_landing[k]
    head_pair[...] = low(total)
    for c in range(2):
        there = (core == c) & (pair_chip == chip)

        @pl.when(there)
        def stay():
            head_two[mine] = head_pair[...]

        @pl.when(jnp.logical_not(there))
        def leave(c=c):
            p_copies[c].start()

    def finish(seq, unused):
        for number in range(2):
            source = 2 * seq + number

            @pl.when(source != chip)
            def come(number=number, source=source):
                send_to(
                    incoming.at[seq, number],
                    incoming.at[seq, number],
                    i_send.at[0],
                    i_recv.at[seq, number],
                    tp=source,
                ).wait_recv()

        upstream = incoming[seq, 0].astype(jnp.float32) + incoming[seq, 1].astype(jnp.float32)
        start_sum = tokens_ref[seq].astype(jnp.float32) + step_ref[seq]
        unit_rows, inverse = in_strips(rows_unit, start_sum)
        back, gain_sum, bias_sum = rows_back(upstream, unit_rows, inverse, gain_ref[...])
        input_ref[seq] = after_ref[seq] + back
        sums_ref[8:9, :] += gain_sum
        sums_ref[9:10, :] += bias_sum
        return unused

    lax.fori_loop(0, batches, finish, 0)

    def start_sums(k, unused):
        s_copy(k).start()
        return unused

    lax.fori_loop(1, group, start_sums, 0)
    def arrive_sums(k, total):
        s_copy(k).wait_recv()
        return total + sums_landing[k]

    sums_two[...] = lax.fori_loop(1, group, arrive_sums, sums_ref[...])
    for copy in s_fsdp:
        copy.start()
    shard_wait.wait_recv()

    def whole(block):
        return jnp.concatenate([shard_ref[0, block], shard_ref[1, block]], 0)

    query_out[...] = whole(0).T
    back_out[...] = whole(1)
    cross_out[...] = whole(2)
    for part in range(4):
        up_out[:, part * piece : (part + 1) * piece] = whole(3 + part).T
        down_out[part * piece : (part + 1) * piece, :] = whole(7 + part)
    pair_out[0] = whole(11).T
    pair_out[1] = whole(12).T
    for n in range(2):

        @pl.when(jnp.logical_not(p_here[n]))
        def pair_come(n=n):
            p_waits[n].wait_recv()

    total = head_two[0].astype(jnp.float32) + head_two[1].astype(jnp.float32)
    for which in range(3):
        self_out[which] = jnp.concatenate(
            [
                total[(3 * n + which) * HEAD_DIM : (3 * n + which + 1) * HEAD_DIM]
                for n in range(2)
            ],
            0,
        ).T
    total = sums_two[...]
    for k, copy in enumerate(s_fsdp):
        copy.wait_recv()
        total = total + sums_landing[group + 1 + k]
    sums_out[...] = total
    core_copy.wait_send()
    pair_copy.wait_send()
    shard_copy.wait_send()
    for c in range(2):

        @pl.when(jnp.logical_not((core == c) & (pair_chip == chip)))
        def pair_sent(c=c):
            p_copies[c].wait_send()

    enc_copy.wait_send()
    for copy in enc_line + f_copies + f_pairs + t_copies + h_copies + s_fsdp:
        copy.wait_send()

    def sent(k, unused):
        s_copy(k).wait_send()
        return unused

    lax.fori_loop(1, group, sent, 0)

    def rows_sent(slot, unused):
        core_rows_copy((1 - core) * tp + slot).wait_send()

        @pl.when(slot != chip)
        def left():
            owner_copy(core * tp + slot).wait_send()

        return unused

    lax.fori_loop(0, tp, rows_sent, 0)


def backward_group(
    prefix,
    enc_parts,
    packed,
    gathered,
    rows,
    returned,
    weight,
    qkv,
    wide,
    logs,
    tokens,
    steps,
    gain,
    after,
    encoder,
    stats,
    span,
    tp,
    fsdp,
):
    batches, chunk, width = tokens.shape
    group = returned.shape[1]
    length = group * chunk
    share = encoder.shape[1] // group
    piece = width // fsdp
    count = packed.shape[3]
    tail = packed.shape[4:]
    bf16, f32 = jnp.bfloat16, jnp.float32
    struct = jax.ShapeDtypeStruct
    inside = pl.BlockSpec(memory_space=pltpu.VMEM)
    outside = pl.BlockSpec(memory_space=pl.ANY)
    dma = pltpu.SemaphoreType.DMA
    vmem = pltpu.VMEM
    parts = group * fsdp
    return pl.pallas_call(
        functools.partial(backward_kernel, span=span, tp=tp, fsdp=fsdp),
        in_specs=[pl.BlockSpec(memory_space=pltpu.SMEM)] + [outside] * 4 + [inside] * 11,
        out_specs=[inside] * 10,
        out_shape=[
            struct((batches, chunk, width), f32),
            struct((batches, share, width), f32),
            struct((3, piece, piece), f32),
            struct((piece, piece), f32),
            struct((2, piece, piece), f32),
            struct((piece, piece), f32),
            struct((piece, piece), f32),
            struct((piece, width), f32),
            struct((width, piece), f32),
            struct((16, width), f32),
        ],
        scratch_shapes=[
            vmem((group, 2, 3 * HEAD_DIM, chunk), bf16),
            vmem((tp, chunk, width), bf16),
            vmem((tp, chunk, width), bf16),
            vmem((tp, chunk, width), bf16),
            vmem((batches, 2, chunk, width), bf16),
            vmem((2, length, 2 * HEAD_DIM), bf16),
            vmem((2, length, 2 * HEAD_DIM), bf16),
            vmem((2, length, 2 * HEAD_DIM), bf16),
            vmem((2, 1, length), f32),
            vmem((2, length, 2 * HEAD_DIM), f32),
            vmem((2, chunk, width), bf16),
            vmem((2, width, width), bf16),
            vmem((batches, tp * share, 2 * width), bf16),
            vmem((batches, tp * share, 2 * width), bf16),
            vmem((tp, batches, share, 2 * width), bf16),
            vmem((tp - 1, batches, share, 2 * width), bf16),
            vmem((group // tp, fsdp, tp, 2) + tail, bf16),
            vmem((fsdp, tp, 2) + tail, bf16),
            vmem((fsdp, tp, count) + tail, bf16),
            vmem((fsdp, tp, count + 2) + tail, bf16),
            vmem((fsdp - 1, tp, count + 2) + tail, bf16),
            vmem((tp, count + 2) + tail, bf16),
            vmem((tp - 1, count + 2) + tail, bf16),
            vmem((2, count + 2) + tail, f32),
            vmem((fsdp, 6 * HEAD_DIM, piece), f32),
            vmem((fsdp - 1, 6 * HEAD_DIM, piece), f32),
            vmem((6 * HEAD_DIM, piece), bf16),
            vmem((2, 6 * HEAD_DIM, piece), bf16),
            vmem((16, width), f32),
            vmem((group + fsdp, 16, width), f32),
            vmem((16, width), f32),
            dma((tp,)),
            dma((tp,)),
            dma((tp,)),
            dma((tp,)),
            dma((tp,)),
            dma((batches, 2)),
            dma((4,)),
            dma((4,)),
            dma((2 * fsdp,)),
            dma((2 * fsdp,)),
            dma((tp,)),
            dma((tp,)),
            dma((fsdp,)),
            dma((fsdp,)),
            dma((2,)),
            dma((2,)),
            dma((group + fsdp,)),
            dma((group + fsdp,)),
            dma((2 + parts,)),
            dma((2,)),
        ],
        compiler_params=pltpu.CompilerParams(
            vmem_limit_bytes=VMEM_LIMIT, collective_id=2, has_side_effects=True
        ),
        cost_estimate=pl.CostEstimate(
            flops=100_000_000_000, bytes_accessed=40_000_000, transcendentals=20_000_000
        ),
        name="backward_group",
    )(
        prefix,
        enc_parts,
        packed,
        gathered,
        rows,
        returned,
        weight,
        qkv,
        wide,
        logs,
        tokens,
        steps,
        gain,
        after,
        encoder,
        stats,
    )


def local_heads(
    tokens,
    timesteps,
    time_table,
    prefix,
    encoder,
    self_qkv,
    cross_q,
    cross_kv,
    self_out,
    cross_out,
    ffn_up,
    ffn_down,
    norm_gain,
    norm_bias,
    cotangent,
):
    batches, chunk, width = tokens.shape
    group = 8
    length = group * chunk
    ctx_index = lax.axis_index("ctx")
    span = 1024
    piece = width // 4
    flip = lambda w: jnp.swapaxes(w, -1, -2)
    blocks = jnp.concatenate(
        [
            flip(self_qkv),
            flip(cross_q)[None],
            flip(cross_kv),
            self_out[None],
            cross_out[None],
            flip(ffn_up).reshape(4, piece, piece),
            ffn_down.reshape(4, piece, piece),
        ]
    )
    count = blocks.shape[0]
    half = piece // 2
    own_half = lax.dynamic_slice_in_dim(blocks, ctx_index * half, half, 1)
    gathered = lax.all_gather(own_half, ("fsdp", "ctx", "tp"), axis=0, tiled=False)
    gathered = gathered.reshape(4, 2, 4, count, half, piece)
    mine = blocks[:3].reshape(3, 2, HEAD_DIM, piece)
    mine = jnp.transpose(mine, (1, 0, 2, 3)).reshape(6 * HEAD_DIM, piece)
    steps_onehot = (timesteps[:, None] == lax.iota(jnp.int32, time_table.shape[0])[None, :]).astype(
        jnp.bfloat16
    )
    embedded = jnp.dot(steps_onehot, time_table, preferred_element_type=jnp.float32)[:, None, :]
    rows, qkv, wide, logs, contexts, weight = forward_group(
        prefix, tokens, embedded, norm_gain[:1], norm_bias[:1], mine, span, group, 4, 4
    )
    final, grad_after, returned, enc_parts, stats, packed = middle(
        gathered,
        tokens,
        embedded,
        encoder,
        cotangent,
        norm_gain,
        norm_bias,
        contexts,
        4,
        4,
    )
    outs = backward_group(
        prefix,
        enc_parts,
        packed,
        gathered,
        rows,
        returned,
        weight,
        qkv,
        wide,
        logs,
        tokens,
        embedded,
        norm_gain[:1],
        grad_after,
        encoder,
        stats,
        span,
        4,
        4,
    )
    sums = outs[9]
    entries = (
        tokens.shape[0]
        * tokens.shape[1]
        * tokens.shape[2]
        * lax.axis_size("fsdp")
        * lax.axis_size("ctx")
        * lax.axis_size("tp")
    )
    return (
        final,
        *outs[:9],
        jnp.stack([sums[8], sums[4], sums[6]]),
        jnp.stack([sums[9], sums[5]]),
        sums[7],
        jnp.sqrt(jnp.sum(sums[:4], -1) / entries),
    )


def solution(mesh):
    placed = (
        P("fsdp", ("ctx", "tp"), None),
        P("fsdp"),
        P(),
        P("fsdp"),
        P("fsdp", None, None),
        P(None, "fsdp", "tp"),
        P("fsdp", "tp"),
        P(None, "fsdp", "tp"),
        P("tp", "fsdp"),
        P("tp", "fsdp"),
        P("fsdp", "tp"),
        P("tp", "fsdp"),
        P(),
        P(),
        P("fsdp", ("ctx", "tp"), None),
    )
    heads_fit = dict(mesh.shape) == {"fsdp": 4, "ctx": 2, "tp": 4}
    return jax.shard_map(
        local_heads if heads_fit else local,
        mesh=mesh,
        in_specs=placed,
        out_specs=(
            P("fsdp", ("ctx", "tp"), None),
            P("fsdp", ("ctx", "tp"), None),
            P("fsdp", ("ctx", "tp"), None),
            P(None, "fsdp", "tp"),
            P("fsdp", "tp"),
            P(None, "fsdp", "tp"),
            P("tp", "fsdp"),
            P("tp", "fsdp"),
            P("fsdp", "tp"),
            P("tp", "fsdp"),
            P(),
            P(),
            P(),
            P(),
        ),
        check_vma=False,
    )
```

time: 437 us -> 391 us (0.89)
  Pallas kernels: 395 us -> 347 us
    pallas_call x1, Pallas kernels: 180 us -> 142 us  [backward_group(): pl.pallas_call(functools.partial(backward_kernel, span=span, tp=tp, fsdp=...]
    pallas_call x1, Pallas kernels: 158 us -> 144 us  [forward_group(): pl.pallas_call(functools.partial(forward_kernel, span=span, tp=tp, fsdp=f...]
    pallas_call x1, Pallas kernels: 56.5 us -> 61 us  [middle(): pl.pallas_call(functools.partial(middle_kernel, tp=tp, fsdp=fsdp), in_spe...]
    unnamed x38 -> x41, local copies, waits for them, and re-layouts: 12.9 us -> 14.3 us
where the time goes in v4:
time: 391 us; the launch traced here: 386 us
  Pallas kernels  347 us (89%)
  local copies, waits for them, and re-layouts  22.2 us (6%)
  between operations  14.2 us (4%)
    pallas_call x1, Pallas kernels, forward_group(): pl.pallas_call(functools.partial(forward_kernel, span=span, tp=tp, fsdp=f...  144 us
    pallas_call x1, Pallas kernels, backward_group(): pl.pallas_call(functools.partial(backward_kernel, span=span, tp=tp, fsdp=...  142 us
    pallas_call x1, Pallas kernels, middle(): pl.pallas_call(functools.partial(middle_kernel, tp=tp, fsdp=fsdp), in_spe...  61 us
    unnamed x41, local copies, waits for them, and re-layouts  14.3 us
  transfers between devices with their start and end apart: 1, of which 0 were waited for; matrix products, arithmetic and copies ran while one was open for 1% of the time, Pallas kernels for 37%

profile of v4, /device:TPU:17, one launch (start us, length us, event | category | flops | bytes accessed | tf_op | source)
XLA Modules:
  0.0 386.2 jit_solution(14642249859944907545)
XLA Ops:
  7.3 1.0 copy.39
  8.3 0.9 copy.40
  9.2 1.0 copy.41
  10.1 1.0 copy.42
  11.2 0.8 bitcast_dynamic-update-slice_fusion.4
  12.0 0.8 bitcast_dynamic-update-slice_fusion.3
  12.7 0.9 constant_dynamic-update-slice_fusion
  13.7 0.7 constant_dynamic-slice_fusion
  15.2 1.3 slice.28.gain_ref
  16.5 1.3 slice.29.bias_ref
  17.8 0.6 copy.43
  18.4 144.2 %forward_group.1 = (bf16[8,512,512]{2,1,0:T(8,128)(2,1)}, bf16[2,192,4096]{2,1,0:T(8,128)(2,1)}, f32[2,64,4096]{2,1,0:T(8,128)}, f32[2,1,4096]{2,1,0:T(1,128)}, ...) custom-call(s32[2]{0:T(128)} %prefix_ref.3, bf16[2,512,512]{2,1,0:T(8,128)(2,1)} %tokens_ref.5, ...), custom_call_target="tpu_custom_call" | custom-call | flops 60000002048 | bytes 30000000 | tf_op jit(solution)/shard_map/forward_group/pallas_call | solution.py:866
  162.6 61.0 %middle.1 = (f32[2,512,512]{2,1,0:T(8,128)}, f32[2,512,512]{2,1,0:T(8,128)}, bf16[2,8,64,512]{3,2,1,0:T(8,128)(2,1)}, bf16[2,256,1024]{2,1,0:T(8,128)(2,1)}, f32...) custom-call(bf16[4,2,4,16,64,128]{5,4,3,2,1,0:T(8,128)(2,1)} %bitcast.29, bf16[2,512,512]{2,1,0:T(8,128)(2,1)} %tokens_ref.5, ...), custom_call_target="tpu_custom_call" | custom-call | flops 30000001024 | bytes 30000000 | tf_op jit(solution)/shard_map/middle/pallas_call | solution.py:1137
  223.6 141.8 %backward_group.1 = (f32[2,512,512]{2,1,0:T(8,128)}, f32[2,32,512]{2,1,0:T(8,128)}, f32[3,128,128]{2,1,0:T(8,128)}, f32[128,128]{1,0:T(8,128)}, f32[2,128,128]{2...) custom-call(s32[2]{0:T(128)} %prefix_ref.3, ...), custom_call_target="tpu_custom_call" | custom-call | flops 99999997952 | bytes 40000000 | tf_op jit(solution)/shard_map/backward_group/pallas_call | solution.py:1815
  365.4 1.5 fusion.4
  366.9 0.8 slice_reduce_fusion
  369.5 3.2 copy.60
  372.7 1.3 copy.61
  374.1 0.7 copy.62
  374.7 0.7 copy.63
  376.0 0.7 copy.65
  376.7 0.6 copy.66
  378.0 0.7 copy.68
  378.7 0.7 copy.69
  (36 shorter events, 4.0 us)
Async XLA Ops:
  7.2 7.3 %copy-start = (bf16[50,512]{1,0:T(8,128)(2,1)S(1)}, bf16[50,512]{1,0:T(8,128)(2,1)}, u32[]{:S(2)}) copy-start(bf16[50,512]{1,0:T(8,128)(2,1)} %param.17) | copy-start | bytes 153604
  7.2 7.3 %copy-start.10 = (s32[2]{0:T(128)S(1)}, s32[2]{0:T(128)}, u32[]{:S(2)}) copy-start(s32[2]{0:T(128)} %param.16) | copy-start | bytes 28
  7.2 155.4 %all-gather.3.cloned.1.call-start = ((), (), s32[]{:S(2)}) async-start(), calls=%async_computation | async-start | bytes 8650752 | tf_op jit(solution)/shard_map/all_gather | solution.py:1949
  369.5 3.2 copy-start.1
  372.7 1.4 copy-start.6
  372.7 2.0 copy-start.4
  372.7 2.7 copy-start.9
  372.7 3.3 copy-start.5
  372.7 4.0 %copy-start.8 = (f32[128,128]{1,0:T(8,128)S(1)}, f32[128,128]{1,0:T(8,128)}, u32[]{:S(2)}) copy-start(f32[128,128]{1,0:T(8,128)} %get-tuple-element.84) | copy-start | bytes 196612
  372.7 4.6 %copy-start.7 = (f32[128,128]{1,0:T(8,128)S(1)}, f32[128,128]{1,0:T(8,128)}, u32[]{:S(2)}) copy-start(f32[128,128]{1,0:T(8,128)} %get-tuple-element.85) | copy-start | bytes 196612
  372.7 5.2 %copy-start.3 = (f32[128,512]{1,0:T(8,128)S(1)}, f32[128,512]{1,0:T(8,128)}, u32[]{:S(2)}) copy-start(f32[128,512]{1,0:T(8,128)} %get-tuple-element.86) | copy-start | bytes 786436
  372.7 5.9 %copy-start.2 = (f32[512,128]{1,0:T(8,128)S(1)}, f32[512,128]{1,0:T(8,128)}, u32[]{:S(2)}) copy-start(f32[512,128]{1,0:T(8,128)} %get-tuple-element.87) | copy-start | bytes 786436
Sparse Core Ops, SparseCore 0:
  14.6 93.4 all-gather.2

commit v5 on v4

--- a/solution.py
+++ b/solution.py
@@ -623,7 +623,7 @@
 
     def normalise(seq, target, at):
         start_sum = tokens_ref[seq].astype(jnp.float32) + step_ref[seq]
-        target[at] = rows_norm(start_sum, gain_ref[...], bias_ref[...])[0]
+        target[at] = rows_norm(start_sum, gain_ref[0:1], bias_ref[0:1])[0]
 
     def x_copy(kind):
         block = rows_ref.at[me]
@@ -923,15 +923,20 @@
     stats_ref,
     packed_ref,
     weights,
-    totals,
-    context,
+    hidden_all,
+    pre_all,
+    three_all,
+    two_all,
+    grad_two_all,
+    grad_one_all,
+    cross_all,
+    query_all,
+    context_all,
     queries,
     keys,
     values,
     probs,
-    context_two,
     grad_heads,
-    grad_queries,
     grad_keys,
     grad_values,
     back_rows,
@@ -960,14 +965,13 @@
                 head = t * (group // tp) + c
                 copies.append(
                     pltpu.make_async_copy(
-                        gathered.at[f, c, t, pl.ds(3, weights.shape[0])],
+                        gathered.at[f, c, t],
                         weights.at[:, pl.ds(head * HEAD_DIM, HEAD_DIM), pl.ds(f * piece, piece)],
                         sem.at[(f * group // tp + c) * tp + t],
                     )
                 )
     for copy in copies:
         copy.start()
-    totals[...] = jnp.zeros_like(totals)
     stats_ref[...] = jnp.zeros_like(stats_ref)
     for copy in copies:
         copy.wait()
@@ -986,13 +990,15 @@
 
     def one_sequence(turn, unused):
         seq = jnp.where(turn == 0, 1 - mine, mine)
+        at = pl.ds(pl.multiple_of(seq * chunk, chunk), chunk)
         for head, number, owner in owners:
-            context[head * HEAD_DIM : (head + 1) * HEAD_DIM, :] = ctx_ref[number, owner + 2 * seq]
+            context_all[head * HEAD_DIM : (head + 1) * HEAD_DIM, at] = ctx_ref[number, owner + 2 * seq]
         start_sum = tokens_ref[seq].astype(jnp.float32) + step_ref[seq]
-        branch_one = dot_of(context[...], weights[SELF_OUT], 0, 0)
+        branch_one = dot_of(context_all[:, at], weights[SELF_OUT], 0, 0)
         after_one = start_sum + branch_one
         stats_ref[1:2, :] += jnp.sum(branch_one * branch_one, 0, keepdims=True)
         normed_two, unit_two, inverse_two = rows_norm(after_one, gain_ref[1:2], bias_ref[1:2])
+        two_all[at, :] = normed_two
         queries[...] = low(dot_of(weights[QUERY], normed_two, 1, 1))
         keys[...] = low(dot_of(weights[KEY], enc_ref[seq], 1, 1))
         values[...] = low(dot_of(weights[VALUE], enc_ref[seq], 1, 1))
@@ -1007,14 +1013,15 @@
 
             (attn,) = in_strips(strip, scores, strip=128, axis=1)
             probs[head] = attn
-            context_two[rows, :] = low(dot_of(values[rows, :], low(attn), 1, 0))
+            cross_all[rows, at] = low(dot_of(values[rows, :], low(attn), 1, 0))
             return unused
 
         lax.fori_loop(0, heads, attend, 0, unroll=8)
-        branch_two = dot_of(context_two[...], weights[CROSS_OUT], 0, 0)
+        branch_two = dot_of(cross_all[:, at], weights[CROSS_OUT], 0, 0)
         after_two = after_one + branch_two
         stats_ref[2:3, :] += jnp.sum(branch_two * branch_two, 0, keepdims=True)
         normed_three, unit_three, inverse_three = rows_norm(after_two, gain_ref[2:3], bias_ref[2:3])
+        three_all[at, :] = normed_three
         grad_three = cot_ref[seq]
 
         def feed(part, carry):
@@ -1023,9 +1030,9 @@
             inputs = dot_of(up, normed_three, 1, 1)
             hidden, slopes = in_strips(gelu_strip, inputs, strip=32)
             branch = branch + dot_of(hidden, down, 0, 0)
-            totals[DOWN - 2 + part] += dot_of(hidden, grad_three, 1, 0)
+            hidden_all[part, :, at] = hidden
             grad_pre = low(dot_of(down, grad_three, 1, 1) * slopes)
-            totals[UP - 2 + part] += dot_of(grad_pre, normed_three, 1, 0)
+            pre_all[part, :, at] = grad_pre
             return branch, grad + dot_of(grad_pre, up, 0, 0)
 
         blank = jnp.zeros((chunk, width), jnp.float32)
@@ -1039,7 +1046,7 @@
         stats_ref[7:8, :] += bias_sum
         grad_after_two = grad_three.astype(jnp.float32) + back
         grad_two = low(grad_after_two)
-        totals[2] += dot_of(context_two[...], grad_two, 1, 0)
+        grad_two_all[at, :] = grad_two
         grad_heads[...] = low(dot_of(weights[CROSS_OUT], grad_two, 1, 1))
 
         def attend_back(head, unused):
@@ -1052,7 +1059,7 @@
                 return (low(ones * (others - jnp.sum(ones * others, 0, keepdims=True))),)
 
             (grad_scores,) = in_strips(strip, attn, grad_probs, strip=128, axis=1)
-            grad_queries[rows, :] = low(dot_of(keys[rows, :], grad_scores, 1, 0) * factor)
+            query_all[rows, at] = low(dot_of(keys[rows, :], grad_scores, 1, 0) * factor)
             grad_keys[rows, :] = dot_of(queries[rows, :], grad_scores, 1, 1) * factor
             grad_values[rows, :] = dot_of(grads, low(attn), 1, 1)
             return unused
@@ -1060,17 +1067,15 @@
         lax.fori_loop(0, heads, attend_back, 0, unroll=8)
         enc_grad_ref[seq, :, :width] = low(grad_keys[...].T)
         enc_grad_ref[seq, :, width:] = low(grad_values[...].T)
-        totals[0] += dot_of(grad_queries[...], normed_two, 1, 0)
-        upstream = dot_of(grad_queries[...], weights[QUERY], 0, 0)
+        upstream = dot_of(query_all[:, at], weights[QUERY], 0, 0)
         back, gain_sum, bias_sum = rows_back(upstream, unit_two, inverse_two, gain_ref[1:2])
         stats_ref[4:5, :] += gain_sum
         stats_ref[5:6, :] += bias_sum
         grad_after_one = grad_after_two + back
         after_ref[seq] = grad_after_one
         grad_one = low(grad_after_one)
-        totals[1] += dot_of(context[...], grad_one, 1, 0)
-        context[...] = low(dot_of(weights[SELF_OUT], grad_one, 1, 1))
-        back_rows[turn] = context[...]
+        grad_one_all[at, :] = grad_one
+        back_rows[turn] = low(dot_of(weights[SELF_OUT], grad_one, 1, 1))
         for head, number, owner in owners:
 
             @pl.when(owner + 2 * seq != me)
@@ -1079,23 +1084,33 @@
 
             @pl.when(owner + 2 * seq == me)
             def keep(head=head, number=number):
-                back_ref[number, me] = context[head * HEAD_DIM : (head + 1) * HEAD_DIM, :]
+                back_ref[number, me] = back_rows[turn, head * HEAD_DIM : (head + 1) * HEAD_DIM, :]
 
         return unused
 
 
     lax.fori_loop(0, batches, one_sequence, 0)
-    for f in range(width // piece):
-        for c in range(group // tp):
-            for t in range(tp):
-                head = t * (group // tp) + c
-                packed_ref[c, f, t] = low(
-                    totals[
-                        :,
-                        head * HEAD_DIM : (head + 1) * HEAD_DIM,
-                        f * piece : (f + 1) * piece,
+    def pack(block, left, right):
+        total = low(dot_of(left, right, 1, 0))
+        for f in range(width // piece):
+            for c in range(group // tp):
+                for t in range(tp):
+                    head = t * (group // tp) + c
+                    packed_ref[c, f, t, block] = total[
+                        head * HEAD_DIM : (head + 1) * HEAD_DIM, f * piece : (f + 1) * piece
                     ]
-                )
+
+    grad_three_all = cot_ref[...].reshape(batches * chunk, width)
+    pack(0, query_all[...], two_all[...])
+    pack(1, context_all[...], grad_one_all[...])
+    pack(2, cross_all[...], grad_two_all[...])
+
+    def pack_feed(part, unused):
+        pack(UP - 2 + part, pre_all[part], three_all[...])
+        pack(DOWN - 2 + part, hidden_all[part], grad_three_all)
+        return unused
+
+    lax.fori_loop(0, DOWN - UP, pack_feed, 0)
 
     def collect(k, unused):
         place = me ^ k
@@ -1132,7 +1147,7 @@
     struct = jax.ShapeDtypeStruct
     inside = pl.BlockSpec(memory_space=pltpu.VMEM)
     dma = pltpu.SemaphoreType.DMA
-    count = gathered.shape[3] - 3
+    count = gathered.shape[3]
     packed = (group // tp, gathered.shape[0], tp, count - 2) + gathered.shape[4:]
     return pl.pallas_call(
         functools.partial(middle_kernel, tp=tp, fsdp=fsdp),
@@ -1148,14 +1163,19 @@
         ],
         scratch_shapes=[
             pltpu.VMEM((count, width, width), bf16),
-            pltpu.VMEM((count - 2, width, width), f32),
-            pltpu.VMEM((width, chunk), bf16),
+            pltpu.VMEM((DOWN - UP, width, batches * chunk), bf16),
+            pltpu.VMEM((DOWN - UP, width, batches * chunk), bf16),
+            pltpu.VMEM((batches * chunk, width), bf16),
+            pltpu.VMEM((batches * chunk, width), bf16),
+            pltpu.VMEM((batches * chunk, width), bf16),
+            pltpu.VMEM((batches * chunk, width), bf16),
+            pltpu.VMEM((width, batches * chunk), bf16),
+            pltpu.VMEM((width, batches * chunk), bf16),
+            pltpu.VMEM((width, batches * chunk), bf16),
             pltpu.VMEM((width, chunk), bf16),
             pltpu.VMEM((width, enc_count), bf16),
             pltpu.VMEM((width, enc_count), bf16),
             pltpu.VMEM((heads, enc_count, chunk), f32),
-            pltpu.VMEM((width, chunk), bf16),
-            pltpu.VMEM((width, chunk), bf16),
             pltpu.VMEM((width, chunk), bf16),
             pltpu.VMEM((width, enc_count), f32),
             pltpu.VMEM((width, enc_count), f32),
@@ -1189,6 +1209,7 @@
     tokens_ref,
     step_ref,
     gain_ref,
+    bias_ref,
     after_ref,
     enc_ref,
     stats_ref,
@@ -1303,7 +1324,7 @@
                 head = t * cores + c
                 local.append(
                     pltpu.make_async_copy(
-                        gathered.at[f, c, t, pl.ds(3 + KEY, 2)],
+                        gathered.at[f, c, t, pl.ds(KEY, 2)],
                         pair_weights.at[
                             :, pl.ds(head * HEAD_DIM, HEAD_DIM), pl.ds(f * piece, piece)
                         ],
@@ -1638,21 +1659,39 @@
     for number in range(depth):
         rows_copy(number).start()
 
-    def weigh(number, total):
+    ones = jnp.ones((chunk, piece), jnp.bfloat16)
+
+    def weigh(number, totals):
         rows_copy(number).wait()
-        total = total + dot_of(
-            outgoing[number].reshape(6 * HEAD_DIM, chunk), rows_ref[number % depth], 1, 0
-        )
+        grads = outgoing[number].reshape(6 * HEAD_DIM, chunk)
+        total = totals[0] + dot_of(grads, rows_ref[number % depth], 1, 0)
 
         @pl.when(number + depth < group)
         def more():
             rows_copy(number + depth).start()
 
-        return total
-
-    total = lax.fori_loop(
-        0, group, weigh, jnp.zeros((6 * HEAD_DIM, width), jnp.float32)
-    )
+        return total, totals[1] + dot_of(grads, ones, 1, 0)
+
+    total, plain = lax.fori_loop(
+        0,
+        group,
+        weigh,
+        (
+            jnp.zeros((6 * HEAD_DIM, width), jnp.float32),
+            jnp.zeros((6 * HEAD_DIM, piece), jnp.float32),
+        ),
+    )
+    weights = weight[...].astype(jnp.float32)
+    bias_sum = jnp.sum(weights * jnp.concatenate([plain] * (width // piece), 1), 0, keepdims=True)
+    gain_sum = jnp.sum(weights * total, 0, keepdims=True) - bias_ref[0:1] * bias_sum
+    sums_ref[8:9, :] = gain_sum / gain_ref[0:1]
+    sums_ref[9:10, :] = bias_sum
+
+    def start_sums(k, unused):
+        s_copy(k).start()
+        return unused
+
+    lax.fori_loop(1, group, start_sums, 0)
     for f in range(fsdp):
         head_ref[f] = total[:, f * piece : (f + 1) * piece]
     for copy in h_copies:
@@ -1675,6 +1714,14 @@
         @pl.when(jnp.logical_not(there))
         def leave(c=c):
             p_copies[c].start()
+
+    def arrive_sums(k, total):
+        s_copy(k).wait_recv()
+        return total + sums_landing[k]
+
+    sums_two[...] = lax.fori_loop(1, group, arrive_sums, sums_ref[...])
+    for copy in s_fsdp:
+        copy.start()
 
     def finish(seq, unused):
         for number in range(2):
@@ -1693,26 +1740,13 @@
         upstream = incoming[seq, 0].astype(jnp.float32) + incoming[seq, 1].astype(jnp.float32)
         start_sum = tokens_ref[seq].astype(jnp.float32) + step_ref[seq]
         unit_rows, inverse = in_strips(rows_unit, start_sum)
-        back, gain_sum, bias_sum = rows_back(upstream, unit_rows, inverse, gain_ref[...])
-        input_ref[seq] = after_ref[seq] + back
-        sums_ref[8:9, :] += gain_sum
-        sums_ref[9:10, :] += bias_sum
+        input_ref[seq] = after_ref[seq] + rows_back(
+            upstream, unit_rows, inverse, gain_ref[0:1]
+        )[0]
         return unused
 
     lax.fori_loop(0, batches, finish, 0)
 
-    def start_sums(k, unused):
-        s_copy(k).start()
-        return unused
-
-    lax.fori_loop(1, group, start_sums, 0)
-    def arrive_sums(k, total):
-        s_copy(k).wait_recv()
-        return total + sums_landing[k]
-
-    sums_two[...] = lax.fori_loop(1, group, arrive_sums, sums_ref[...])
-    for copy in s_fsdp:
-        copy.start()
     shard_wait.wait_recv()
 
     def whole(block):
@@ -1791,6 +1825,7 @@
     tokens,
     steps,
     gain,
+    bias,
     after,
     encoder,
     stats,
@@ -1814,7 +1849,7 @@
     parts = group * fsdp
     return pl.pallas_call(
         functools.partial(backward_kernel, span=span, tp=tp, fsdp=fsdp),
-        in_specs=[pl.BlockSpec(memory_space=pltpu.SMEM)] + [outside] * 4 + [inside] * 11,
+        in_specs=[pl.BlockSpec(memory_space=pltpu.SMEM)] + [outside] * 4 + [inside] * 12,
         out_specs=[inside] * 10,
         out_shape=[
             struct((batches, chunk, width), f32),
@@ -1902,10 +1937,113 @@
         tokens,
         steps,
         gain,
+        bias,
         after,
         encoder,
         stats,
     )
+
+
+def pack_kernel(
+    scalars,
+    table_ref,
+    qkv_ref,
+    query_ref,
+    pair_ref,
+    self_ref,
+    cross_ref,
+    up_ref,
+    down_ref,
+    half_ref,
+    mine_ref,
+    steps_ref,
+    blocks,
+):
+    piece = query_ref.shape[0]
+    blocks[0] = query_ref[...].T
+    for n in range(2):
+        blocks[1 + n] = pair_ref[n].T
+    blocks[3] = self_ref[...]
+    blocks[4] = cross_ref[...]
+    for n in range(4):
+        blocks[5 + n] = up_ref[:, n * piece : (n + 1) * piece].T
+        blocks[9 + n] = down_ref[n * piece : (n + 1) * piece, :]
+    half = piece // 2
+    half_ref[...] = blocks[:, pl.ds(pl.multiple_of(scalars[0] * half, half), half), :]
+    for which in range(3):
+        flipped = qkv_ref[which].T
+        for head in range(2):
+            mine_ref[(3 * head + which) * HEAD_DIM : (3 * head + which + 1) * HEAD_DIM, :] = (
+                flipped[head * HEAD_DIM : (head + 1) * HEAD_DIM]
+            )
+    table = table_ref[...].astype(jnp.float32)
+    rows = lax.broadcasted_iota(jnp.int32, table.shape, 0)
+    for seq in range(steps_ref.shape[0]):
+        chosen = jnp.where(rows == scalars[1 + seq], table, 0.0)
+        steps_ref[seq] = jnp.sum(chosen, 0, keepdims=True)
+
+
+def pack_weights(scalars, table, self_qkv, cross_q, cross_kv, self_out, cross_out, up, down):
+    piece = cross_q.shape[0]
+    width = table.shape[1]
+    batches = scalars.shape[0] - 1
+    bf16 = jnp.bfloat16
+    struct = jax.ShapeDtypeStruct
+    inside = pl.BlockSpec(memory_space=pltpu.VMEM)
+    return pl.pallas_call(
+        pack_kernel,
+        in_specs=[pl.BlockSpec(memory_space=pltpu.SMEM)] + [inside] * 8,
+        out_specs=[inside] * 3,
+        out_shape=[
+            struct((13, piece // 2, piece), bf16),
+            struct((3 * piece, piece), bf16),
+            struct((batches, 1, width), jnp.float32),
+        ],
+        scratch_shapes=[pltpu.VMEM((13, piece, piece), bf16)],
+        name="pack_weights",
+    )(scalars, table, self_qkv, cross_q, cross_kv, self_out, cross_out, up, down)
+
+
+def collect_kernel(*refs, large, small, entries):
+    ins, outs = refs[: large + small + 1], refs[large + small + 1 :]
+    for n in range(large):
+        outs[n][...] = ins[n][...]
+
+    @pl.when(pl.program_id(0) == 0)
+    def once():
+        for n in range(large, large + small):
+            outs[n][...] = ins[n][...]
+        sums = ins[large + small]
+        gain_ref, bias_ref, feed_ref, norms_ref = outs[large + small :]
+        for n, row in enumerate((8, 4, 6)):
+            gain_ref[n : n + 1, :] = sums[row : row + 1, :]
+        for n, row in enumerate((9, 5)):
+            bias_ref[n : n + 1, :] = sums[row : row + 1, :]
+        feed_ref[...] = sums[7:8, :]
+        norms_ref[...] = jnp.sqrt(jnp.sum(sums[0:4, :], 1, keepdims=True) * (1.0 / entries))
+
+
+def collect(large, small, sums, entries):
+    width = sums.shape[1]
+    f32 = jnp.float32
+    struct = jax.ShapeDtypeStruct
+    rest = [struct(v.shape, v.dtype) for v in small]
+    extra = [struct((3, width), f32), struct((2, width), f32), struct((1, width), f32)]
+    extra = extra + [struct((4, 1), f32)]
+    still = lambda v: pl.BlockSpec(v.shape, lambda i, rank=len(v.shape): (0,) * rank)
+    steps = 4
+    moving = lambda v: pl.BlockSpec(
+        (1, v.shape[0] * v.shape[1] // steps, v.shape[2]),
+        lambda i, per=steps // v.shape[0]: (i // per, i % per, 0),
+    )
+    return pl.pallas_call(
+        functools.partial(collect_kernel, large=len(large), small=len(small), entries=entries),
+        grid=(steps,),
+        in_specs=[moving(v) for v in large] + [still(v) for v in small] + [still(sums)],
+        out_specs=[moving(v) for v in large] + [still(v) for v in rest + extra],
+        out_shape=[struct(v.shape, v.dtype) for v in large] + rest + extra,
+        name="collect",
+    )(*large, *small, sums)
 
 
 def local_heads(
@@ -1930,32 +2068,21 @@
     length = group * chunk
     ctx_index = lax.axis_index("ctx")
     span = 1024
-    piece = width // 4
-    flip = lambda w: jnp.swapaxes(w, -1, -2)
-    blocks = jnp.concatenate(
-        [
-            flip(self_qkv),
-            flip(cross_q)[None],
-            flip(cross_kv),
-            self_out[None],
-            cross_out[None],
-            flip(ffn_up).reshape(4, piece, piece),
-            ffn_down.reshape(4, piece, piece),
-        ]
-    )
-    count = blocks.shape[0]
-    half = piece // 2
-    own_half = lax.dynamic_slice_in_dim(blocks, ctx_index * half, half, 1)
+    own_half, mine, embedded = pack_weights(
+        jnp.concatenate([ctx_index[None].astype(jnp.int32), timesteps]),
+        time_table,
+        self_qkv,
+        cross_q,
+        cross_kv,
+        self_out,
+        cross_out,
+        ffn_up,
+        ffn_down,
+    )
     gathered = lax.all_gather(own_half, ("fsdp", "ctx", "tp"), axis=0, tiled=False)
-    gathered = gathered.reshape(4, 2, 4, count, half, piece)
-    mine = blocks[:3].reshape(3, 2, HEAD_DIM, piece)
-    mine = jnp.transpose(mine, (1, 0, 2, 3)).reshape(6 * HEAD_DIM, piece)
-    steps_onehot = (timesteps[:, None] == lax.iota(jnp.int32, time_table.shape[0])[None, :]).astype(
-        jnp.bfloat16
-    )
-    embedded = jnp.dot(steps_onehot, time_table, preferred_element_type=jnp.float32)[:, None, :]
+    gathered = gathered.reshape((4, 2, 4) + own_half.shape)
     rows, qkv, wide, logs, contexts, weight = forward_group(
-        prefix, tokens, embedded, norm_gain[:1], norm_bias[:1], mine, span, group, 4, 4
+        prefix, tokens, embedded, norm_gain, norm_bias, mine, span, group, 4, 4
     )
     final, grad_after, returned, enc_parts, stats, packed = middle(
         gathered,
@@ -1982,7 +2109,8 @@
         logs,
         tokens,
         embedded,
-        norm_gain[:1],
+        norm_gain,
+        norm_bias,
         grad_after,
         encoder,
         stats,
@@ -1999,14 +2127,8 @@
         * lax.axis_size("ctx")
         * lax.axis_size("tp")
     )
-    return (
-        final,
-        *outs[:9],
-        jnp.stack([sums[8], sums[4], sums[6]]),
-        jnp.stack([sums[9], sums[5]]),
-        sums[7],
-        jnp.sqrt(jnp.sum(sums[:4], -1) / entries),
-    )
+    results = collect((final, *outs[:2]), outs[2:9], sums, entries)
+    return (*results[:12], results[12].reshape(width), results[13].reshape(4))
 
 
 def solution(mesh):

time: 391 us -> 351 us (0.90)
  local copies, waits for them, and re-layouts: 22.2 us -> 0 us
  Pallas kernels: 347 us -> 330 us
    unnamed x41 -> x0, local copies, waits for them, and re-layouts: 14.3 us -> none
    pallas_call x1, Pallas kernels: 142 us -> 132 us  [backward_group(): pl.pallas_call(functools.partial(backward_kernel, span=span, tp=tp, fsdp=...]
    pallas_call x1, Pallas kernels: 144 us -> 136 us  [forward_group(): pl.pallas_call(functools.partial(forward_kernel, span=span, tp=tp, fsdp=f...]
    pallas_call x0 -> x2, Pallas kernels: none -> 7.78 us  [the longest x1 5.78 us: collect(): pl.pallas_call(functools.partial(collect_kernel, large=len(large), small=...]
    pallas_call x1, Pallas kernels: 61 us -> 55.2 us  [middle(): pl.pallas_call(functools.partial(middle_kernel, tp=tp, fsdp=fsdp), in_spe...]
    slice x3 -> x0, local copies, waits for them, and re-layouts: 4.01 us -> none  [the longest x1 1.46 us: local_heads(): sums[7]]
  transfers between devices with their start and end apart: 1 -> 1, of which waited for: 0 -> 0; matrix products, arithmetic and copies ran while one was open for 1% -> 0% of each run, Pallas kernels for 37% -> 39%
where the time goes in v5:
time: 351 us; the launch traced here: 347 us
  Pallas kernels  330 us (94%)
  between operations  14.1 us (4%)
    pallas_call x1, Pallas kernels, forward_group(): pl.pallas_call(functools.partial(forward_kernel, span=span, tp=tp, fsdp=f...  136 us
    pallas_call x1, Pallas kernels, backward_group(): pl.pallas_call(functools.partial(backward_kernel, span=span, tp=tp, fsdp=...  132 us
    pallas_call x1, Pallas kernels, middle(): pl.pallas_call(functools.partial(middle_kernel, tp=tp, fsdp=fsdp), in_spe...  55.2 us
  transfers between devices with their start and end apart: 1, of which 0 were waited for; matrix products, arithmetic and copies ran while one was open for 0% of the time, Pallas kernels for 39%

profile of v5, /device:TPU:17, one launch (start us, length us, event | category | flops | bytes accessed | tf_op | source)
XLA Modules:
  0.0 347.2 jit_solution(2247112076745206545)
XLA Ops:
  7.2 0.0 all-gather.3.cloned.1.call-start
  7.2 1.2 pad_add_fusion.scalars
  8.5 2.0 pack_weights.1
  10.5 0.0 all-gather.3.cloned.1.call-update
  10.5 135.5 %forward_group.1 = (bf16[8,512,512]{2,1,0:T(8,128)(2,1)}, bf16[2,192,4096]{2,1,0:T(8,128)(2,1)}, f32[2,64,4096]{2,1,0:T(8,128)}, f32[2,1,4096]{2,1,0:T(1,128)}, ...) custom-call(s32[2]{0:T(128)} %prefix_ref.3, bf16[2,512,512]{2,1,0:T(8,128)(2,1)} %tokens_ref.5, ...), custom_call_target="tpu_custom_call" | custom-call | flops 60000002048 | bytes 30000000 | tf_op jit(solution)/shard_map/forward_group/pallas_call | solution.py:866
  146.0 0.0 all-gather.3.cloned.1.call-done
  146.1 55.2 %middle.1 = (f32[2,512,512]{2,1,0:T(8,128)}, f32[2,512,512]{2,1,0:T(8,128)}, bf16[2,8,64,512]{3,2,1,0:T(8,128)(2,1)}, bf16[2,256,1024]{2,1,0:T(8,128)(2,1)}, f32...) custom-call(bf16[4,2,4,13,64,128]{5,4,3,2,1,0:T(8,128)(2,1)} %bitcast.3, bf16[2,512,512]{2,1,0:T(8,128)(2,1)} %tokens_ref.5, ...), custom_call_target="tpu_custom_call" | custom-call | flops 30000001024 | bytes 30000000 | tf_op jit(solution)/shard_map/middle/pallas_call | solution.py:1152
  201.3 132.0 %backward_group.1 = (f32[2,512,512]{2,1,0:T(8,128)}, f32[2,32,512]{2,1,0:T(8,128)}, f32[3,128,128]{2,1,0:T(8,128)}, f32[128,128]{1,0:T(8,128)}, f32[2,128,128]{2...) custom-call(s32[2]{0:T(128)} %prefix_ref.3, ...), custom_call_target="tpu_custom_call" | custom-call | flops 99999997952 | bytes 40000000 | tf_op jit(solution)/shard_map/backward_group/pallas_call | solution.py:1850
  333.2 5.8 %collect.1 = (f32[2,512,512]{2,1,0:T(8,128)}, f32[2,512,512]{2,1,0:T(8,128)}, f32[2,32,512]{2,1,0:T(8,128)}, f32[3,128,128]{2,1,0:T(8,128)}, f32[128,128]{1,0:T(...) custom-call(f32[2,512,512]{2,1,0:T(8,128)} %get-tuple-element.57.ref, ...), custom_call_target="tpu_custom_call" | custom-call | tf_op jit(solution)/shard_map/collect/pallas_call | solution.py:2039
  339.0 1.3 reduce
Async XLA Ops:
  7.2 138.9 %all-gather.3.cloned.1.call-start = ((), (), s32[]{:S(2)}) async-start(), calls=%async_computation | async-start | bytes 7028736 | tf_op jit(solution)/shard_map/all_gather | solution.py:2082
Sparse Core Ops, SparseCore 0:
  11.4 95.2 all-gather.2

commit v6 on v5

--- a/solution.py
+++ b/solution.py
@@ -15,7 +15,7 @@
 NEG = -1e30
 ROOT_HALF = 1.0 / math.sqrt(2.0)
 INV_ROOT_TWO_PI = 1.0 / math.sqrt(2.0 * math.pi)
-VMEM_LIMIT = 62 * 2**20
+VMEM_LIMIT = 63 * 2**20
 
 
 def norm_rows(hidden, scaling, offsets):
@@ -748,7 +748,7 @@
         ).wait_recv()
 
     def attend(index, unused):
-        block, head = index // 2, index % 2
+        block, head = (index // 2) ^ (1 - mine), index % 2
 
         @pl.when((core == 1) & (index == 3))
         def near_lines():
@@ -774,27 +774,41 @@
             prefix_ref[mine], start + 1 + lax.broadcasted_iota(jnp.int32, (1, span), 1)
         )
 
-        def advance(other, carry, masked):
+        def advance(offset, count, carry, columns=None):
             highest, total = carry
-            offset = pl.multiple_of(other * span, span)
-            scores = dot_of(keys_ref[head, pl.ds(offset, span), :], queries, 1, 0)
-            if masked:
-                scores = hide(scores, limit, offset)
+            first = 0 if columns is None else columns
+            scores = dot_of(keys_ref[head, pl.ds(offset, count), :], queries[:, first:], 1, 0)
+            if columns is not None:
+                scores = hide(scores, limit[:, first:], offset)
             higher = jnp.maximum(highest, jnp.max(scores, axis=0, keepdims=True))
             weights = low(jnp.exp(scores - higher))
             fading = jnp.exp(highest - higher)
             total = total * fading + dot_of(
-                values_ref[head, :, pl.ds(offset, span)], weights, 1, 0
+                values_ref[head, :, pl.ds(offset, count)], weights, 1, 0
             )
             return higher, total
+
+        def whole_step(other, carry):
+            return advance(pl.multiple_of(other * span, span), span, carry)
+
+        def masked_step(other, carry):
+            return advance(pl.multiple_of(other * span, span), span, carry, 0)
+
+        def diagonal_step(other, carry):
+            half = span // 2
+            carry = advance(start, half, carry, 0)
+            offset = pl.multiple_of(start + half, half)
+            upper = advance(offset, half, tuple(v[:, half:] for v in carry), half)
+            return tuple(jnp.concatenate([v[:, :half], u], 1) for v, u in zip(carry, upper))
 
         carry = (
             jnp.full((1, span), NEG, jnp.float32),
             jnp.zeros((values_ref.shape[1], span), jnp.float32),
         )
-        carry = lax.fori_loop(0, block, lambda j, c: advance(j, c, False), carry)
+        carry = lax.fori_loop(0, block, whole_step, carry)
+        carry = lax.fori_loop(block, wide_blocks, masked_step, carry)
         highest, total = lax.fori_loop(
-            block, jnp.maximum(block + 1, wide_blocks), lambda j, c: advance(j, c, True), carry
+            0, jnp.where(block >= wide_blocks, 1, 0), diagonal_step, carry
         )
         weight_sum = total[HEAD_DIM : HEAD_DIM + 1, :]
         attended = total[:HEAD_DIM, :] / weight_sum
@@ -1227,6 +1241,7 @@
     core_rows,
     core_rows_landing,
     sum_rows,
+    beside,
     incoming,
     queries_ref,
     pairs_ref,
@@ -1260,6 +1275,7 @@
     x_recv,
     i_send,
     i_recv,
+    b_recv,
     r_send,
     r_recv,
     f_send,
@@ -1288,6 +1304,7 @@
     here, core, chip = lax.axis_index("fsdp"), lax.axis_index("ctx"), lax.axis_index("tp")
     me = core * tp + chip
     mine = chip // 2
+    inner = (chip == 1) | (chip == 2)
     cores = group // tp
     share = enc_landing.shape[2]
     piece = width // fsdp
@@ -1455,7 +1472,28 @@
             @pl.when(place != me)
             def send():
                 sum_rows[slot] = total
-                owner_copy(place).start()
+
+                @pl.when((core == 0) & (slot // 2 != mine) & jnp.logical_not(inner))
+                def to_inner():
+                    beside_copy(slot).start()
+
+                @pl.when((core == 1) | (slot // 2 == mine))
+                def to_owner():
+                    owner_copy(place).start()
+
+    def beside_copy(slot):
+        return send_to(
+            sum_rows.at[slot], beside.at[slot % 2], i_send.at[slot], b_recv.at[slot % 2], tp=chip ^ 1
+        )
+
+    def pass_rows():
+        for n in range(2):
+            slot = 2 * (1 - mine) + n
+            beside_copy(slot).wait_recv()
+            sum_rows[slot] = low(
+                sum_rows[slot].astype(jnp.float32) + beside[n].astype(jnp.float32)
+            )
+            owner_copy(slot).start()
 
     def prepare(seq):
         def lay(place, unused):
@@ -1595,27 +1633,41 @@
             prefix_ref[mine], start + 1 + lax.broadcasted_iota(jnp.int32, (1, span), 1)
         )
 
-        def advance(other, grad_queries, masked):
-            offset = pl.multiple_of(other * span, span)
-            there = pl.ds(offset, span)
+        def advance(offset, count, grad_queries, columns=None):
+            first = 0 if columns is None else columns
+            there = pl.ds(offset, count)
             pairs = pairs_ref[seq, there, :]
-            scores = dot_of(pairs, queries_t, 1, 0)
-            if masked:
-                scores = hide(scores, limit, offset)
-            probs = jnp.exp(scores - logs)
-            grad_probs = dot_of(pairs, grads_t, 1, 0)
-            grad_scores = low(probs * (grad_probs - deltas))
-            grad_pairs_ref[seq, there, :] += dot_of(low(probs), grads, 1, 0) + dot_of(
-                grad_scores, queries, 1, 0
+            scores = dot_of(pairs, queries_t[:, first:], 1, 0)
+            if columns is not None:
+                scores = hide(scores, limit[:, first:], offset)
+            probs = jnp.exp(scores - logs[:, first:])
+            grad_probs = dot_of(pairs, grads_t[:, first:], 1, 0)
+            grad_scores = low(probs * (grad_probs - deltas[:, first:]))
+            grad_pairs_ref[seq, there, :] += dot_of(low(probs), grads[first:], 1, 0) + dot_of(
+                grad_scores, queries[first:], 1, 0
             )
             return grad_queries + dot_of(
                 qkv_ref[seq, HEAD_DIM : 2 * HEAD_DIM, there], grad_scores, 1, 0
             )
 
+        def whole_step(other, total):
+            return advance(pl.multiple_of(other * span, span), span, total)
+
+        def masked_step(other, total):
+            return advance(pl.multiple_of(other * span, span), span, total, 0)
+
+        def diagonal_step(other, total):
+            half = span // 2
+            total = advance(start, half, total, 0)
+            offset = pl.multiple_of(start + half, half)
+            upper = advance(offset, half, total[:, half:], half)
+            return jnp.concatenate([total[:, :half], upper], 1)
+
         grad_queries = jnp.zeros((HEAD_DIM, span), jnp.float32)
-        grad_queries = lax.fori_loop(0, block, lambda j, c: advance(j, c, False), grad_queries)
+        grad_queries = lax.fori_loop(0, block, whole_step, grad_queries)
+        grad_queries = lax.fori_loop(block, wide_blocks, masked_step, grad_queries)
         grad_queries = lax.fori_loop(
-            block, jnp.maximum(block + 1, wide_blocks), lambda j, c: advance(j, c, True), grad_queries
+            0, jnp.where(block >= wide_blocks, 1, 0), diagonal_step, grad_queries
         )
         done = low(grad_queries * factor)
         for part in range(ratio):
@@ -1645,6 +1697,11 @@
         return unused
 
     lax.fori_loop(0, 2 * blocks, attend, 0)
+
+    @pl.when((core == 0) & inner)
+    def last_rows():
+        pass_rows()
+
     sums_ref[...] = jnp.zeros_like(sums_ref)
     sums_ref[:8, :] = stats_ref[...]
 
@@ -1681,6 +1738,12 @@
             jnp.zeros((6 * HEAD_DIM, piece), jnp.float32),
         ),
     )
+    token_copies = [
+        pltpu.make_async_copy(tokens_ref.at[n], rows_ref.at[n], rows_sem.at[n])
+        for n in range(batches)
+    ]
+    for copy in token_copies:
+        copy.start()
     weights = weight[...].astype(jnp.float32)
     bias_sum = jnp.sum(weights * jnp.concatenate([plain] * (width // piece), 1), 0, keepdims=True)
     gain_sum = jnp.sum(weights * total, 0, keepdims=True) - bias_ref[0:1] * bias_sum
@@ -1723,11 +1786,20 @@
     for copy in s_fsdp:
         copy.start()
 
+    for copy in token_copies:
+        copy.wait()
+
     def finish(seq, unused):
         for number in range(2):
             source = 2 * seq + number
 
-            @pl.when(source != chip)
+            passed = (core == 0) & (seq != mine)
+
+            @pl.when(passed & ((source == 0) | (source == 3)))
+            def nothing(number=number):
+                incoming[seq, number] = jnp.zeros((chunk, width), jnp.bfloat16)
+
+            @pl.when((source != chip) & jnp.logical_not(passed & ((source == 0) | (source == 3))))
             def come(number=number, source=source):
                 send_to(
                     incoming.at[seq, number],
@@ -1738,7 +1810,7 @@
                 ).wait_recv()
 
         upstream = incoming[seq, 0].astype(jnp.float32) + incoming[seq, 1].astype(jnp.float32)
-        start_sum = tokens_ref[seq].astype(jnp.float32) + step_ref[seq]
+        start_sum = rows_ref[seq].astype(jnp.float32) + step_ref[seq]
         unit_rows, inverse = in_strips(rows_unit, start_sum)
         input_ref[seq] = after_ref[seq] + rows_back(
             upstream, unit_rows, inverse, gain_ref[0:1]
@@ -1849,7 +1921,7 @@
     parts = group * fsdp
     return pl.pallas_call(
         functools.partial(backward_kernel, span=span, tp=tp, fsdp=fsdp),
-        in_specs=[pl.BlockSpec(memory_space=pltpu.SMEM)] + [outside] * 4 + [inside] * 12,
+        in_specs=[pl.BlockSpec(memory_space=pltpu.SMEM)] + [outside] * 4 + [inside] * 5 + [outside] + [inside] * 6,
         out_specs=[inside] * 10,
         out_shape=[
             struct((batches, chunk, width), f32),
@@ -1868,6 +1940,7 @@
             vmem((tp, chunk, width), bf16),
             vmem((tp, chunk, width), bf16),
             vmem((tp, chunk, width), bf16),
+            vmem((2, chunk, width), bf16),
             vmem((batches, 2, chunk, width), bf16),
             vmem((2, length, 2 * HEAD_DIM), bf16),
             vmem((2, length, 2 * HEAD_DIM), bf16),
@@ -1901,6 +1974,7 @@
             dma((tp,)),
             dma((tp,)),
             dma((batches, 2)),
+            dma((2,)),
             dma((4,)),
             dma((4,)),
             dma((2 * fsdp,)),
@@ -1969,7 +2043,8 @@
         blocks[5 + n] = up_ref[:, n * piece : (n + 1) * piece].T
         blocks[9 + n] = down_ref[n * piece : (n + 1) * piece, :]
     half = piece // 2
-    half_ref[...] = blocks[:, pl.ds(pl.multiple_of(scalars[0] * half, half), half), :]
+    core = lax.axis_index("ctx")
+    half_ref[...] = blocks[:, pl.ds(pl.multiple_of(core * half, half), half), :]
     for which in range(3):
         flipped = qkv_ref[which].T
         for head in range(2):
@@ -1979,14 +2054,14 @@
     table = table_ref[...].astype(jnp.float32)
     rows = lax.broadcasted_iota(jnp.int32, table.shape, 0)
     for seq in range(steps_ref.shape[0]):
-        chosen = jnp.where(rows == scalars[1 + seq], table, 0.0)
+        chosen = jnp.where(rows == scalars[seq], table, 0.0)
         steps_ref[seq] = jnp.sum(chosen, 0, keepdims=True)
 
 
 def pack_weights(scalars, table, self_qkv, cross_q, cross_kv, self_out, cross_out, up, down):
     piece = cross_q.shape[0]
     width = table.shape[1]
-    batches = scalars.shape[0] - 1
+    batches = scalars.shape[0]
     bf16 = jnp.bfloat16
     struct = jax.ShapeDtypeStruct
     inside = pl.BlockSpec(memory_space=pltpu.VMEM)
@@ -2020,7 +2095,11 @@
         for n, row in enumerate((9, 5)):
             bias_ref[n : n + 1, :] = sums[row : row + 1, :]
         feed_ref[...] = sums[7:8, :]
-        norms_ref[...] = jnp.sqrt(jnp.sum(sums[0:4, :], 1, keepdims=True) * (1.0 / entries))
+        totals = jnp.sum(sums[0:4, :], 1, keepdims=True) * (1.0 / entries)
+        one = lax.broadcasted_iota(jnp.int32, (4, 128), 0) == lax.broadcasted_iota(
+            jnp.int32, (4, 128), 1
+        )
+        norms_ref[...] = jnp.sqrt(jnp.sum(jnp.where(one, totals, 0.0), 0, keepdims=True))[:, :4]
 
 
 def collect(large, small, sums, entries):
@@ -2029,7 +2108,7 @@
     struct = jax.ShapeDtypeStruct
     rest = [struct(v.shape, v.dtype) for v in small]
     extra = [struct((3, width), f32), struct((2, width), f32), struct((1, width), f32)]
-    extra = extra + [struct((4, 1), f32)]
+    extra = extra + [struct((1, 4), f32)]
     still = lambda v: pl.BlockSpec(v.shape, lambda i, rank=len(v.shape): (0,) * rank)
     steps = 4
     moving = lambda v: pl.BlockSpec(
@@ -2066,10 +2145,9 @@
     batches, chunk, width = tokens.shape
     group = 8
     length = group * chunk
-    ctx_index = lax.axis_index("ctx")
     span = 1024
     own_half, mine, embedded = pack_weights(
-        jnp.concatenate([ctx_index[None].astype(jnp.int32), timesteps]),
+        timesteps,
         time_table,
         self_qkv,
         cross_q,
@@ -2079,7 +2157,8 @@
         ffn_up,
         ffn_down,
     )
-    gathered = lax.all_gather(own_half, ("fsdp", "ctx", "tp"), axis=0, tiled=False)
+    gathered = lax.all_gather(own_half, "tp", axis=0, tiled=False)
+    gathered = lax.all_gather(gathered, ("fsdp", "ctx"), axis=0, tiled=False)
     gathered = gathered.reshape((4, 2, 4) + own_half.shape)
     rows, qkv, wide, logs, contexts, weight = forward_group(
         prefix, tokens, embedded, norm_gain, norm_bias, mine, span, group, 4, 4

time: 351 us -> 336 us (0.957)
  Pallas kernels: 330 us -> 299 us
  blocking collectives: 0 us -> 18.9 us
    pallas_call x1, Pallas kernels: 136 us -> 102 us  [forward_group(): pl.pallas_call(functools.partial(forward_kernel, span=span, tp=tp, fsdp=f...]
    all_gather x0 -> x1, blocking collectives: none -> 18.9 us  [local_heads(): gathered = lax.all_gather(own_half, 'tp', axis=0, tiled=False)]
    pallas_call x1, Pallas kernels: 55.2 us -> 63.1 us  [middle(): pl.pallas_call(functools.partial(middle_kernel, tp=tp, fsdp=fsdp), in_spe...]
    pallas_call x1, Pallas kernels: 132 us -> 126 us  [backward_group(): pl.pallas_call(functools.partial(backward_kernel, span=span, tp=tp, fsdp=...]
  transfers between devices with their start and end apart: 1 -> 1, of which waited for: 0 -> 0; matrix products, arithmetic and copies ran while one was open for 0% -> 0% of each run, Pallas kernels for 39% -> 31%
where the time goes in v6:
time: 336 us; the launch traced here: 333 us
  Pallas kernels  299 us (89%)
  blocking collectives  18.9 us (6%)
  between operations  14.3 us (4%)
    pallas_call x1, Pallas kernels, backward_group(): pl.pallas_call(functools.partial(backward_kernel, span=span, tp=tp, fsdp=...  126 us
    pallas_call x1, Pallas kernels, forward_group(): pl.pallas_call(functools.partial(forward_kernel, span=span, tp=tp, fsdp=f...  102 us
    pallas_call x1, Pallas kernels, middle(): pl.pallas_call(functools.partial(middle_kernel, tp=tp, fsdp=fsdp), in_spe...  63.1 us
    all_gather x1, blocking collectives, local_heads(): gathered = lax.all_gather(own_half, 'tp', axis=0, tiled=False)  18.9 us
  transfers between devices with their start and end apart: 1, of which 0 were waited for; matrix products, arithmetic and copies ran while one was open for 0% of the time, Pallas kernels for 31%

profile of v6, /device:TPU:17, one launch (start us, length us, event | category | flops | bytes accessed | tf_op | source)
XLA Modules:
  0.0 332.5 jit_solution(14837699961831720933)
XLA Ops:
  7.2 0.0 all-gather.4.cloned.1.call-start
  7.2 2.0 pack_weights.1
  9.3 18.9 %all-gather = bf16[52,64,128]{2,1,0:T(8,128)(2,1)} all-gather(bf16[13,64,128]{2,1,0:T(8,128)(2,1)} %get-tuple-element.53), channel_id=2, replica_groups=mesh['fsdp'=4,'ctx'=2,'tp'=4] {'tp'}, dimensions={0}, use_global_device_ids=true | all-gather | bytes 1064960 | tf_op jit(solution)/shard_map/all_gather | solution.py:2160
  28.2 0.0 all-gather.4.cloned.1.call-update
  28.2 102.4 %forward_group.1 = (bf16[8,512,512]{2,1,0:T(8,128)(2,1)}, bf16[2,192,4096]{2,1,0:T(8,128)(2,1)}, f32[2,64,4096]{2,1,0:T(8,128)}, f32[2,1,4096]{2,1,0:T(1,128)}, ...) custom-call(s32[2]{0:T(128)} %prefix_ref.3, bf16[2,512,512]{2,1,0:T(8,128)(2,1)} %tokens_ref.5, ...), custom_call_target="tpu_custom_call" | custom-call | flops 60000002048 | bytes 30000000 | tf_op jit(solution)/shard_map/forward_group/pallas_call | solution.py:880
  130.6 0.0 all-gather.4.cloned.1.call-done
  130.6 63.1 %middle.1 = (f32[2,512,512]{2,1,0:T(8,128)}, f32[2,512,512]{2,1,0:T(8,128)}, bf16[2,8,64,512]{3,2,1,0:T(8,128)(2,1)}, bf16[2,256,1024]{2,1,0:T(8,128)(2,1)}, f32...) custom-call(bf16[4,2,4,13,64,128]{5,4,3,2,1,0:T(8,128)(2,1)} %bitcast.5, bf16[2,512,512]{2,1,0:T(8,128)(2,1)} %tokens_ref.5, ...), custom_call_target="tpu_custom_call" | custom-call | flops 30000001024 | bytes 30000000 | tf_op jit(solution)/shard_map/middle/pallas_call | solution.py:1166
  193.7 125.9 %backward_group.1 = (f32[2,512,512]{2,1,0:T(8,128)}, f32[2,32,512]{2,1,0:T(8,128)}, f32[3,128,128]{2,1,0:T(8,128)}, f32[128,128]{1,0:T(8,128)}, f32[2,128,128]{2...) custom-call(s32[2]{0:T(128)} %prefix_ref.3, ...), custom_call_target="tpu_custom_call" | custom-call | flops 99999997952 | bytes 40000000 | tf_op jit(solution)/shard_map/backward_group/pallas_call | solution.py:1922
  319.7 5.8 %collect.1 = (f32[2,512,512]{2,1,0:T(8,128)}, f32[2,512,512]{2,1,0:T(8,128)}, f32[2,32,512]{2,1,0:T(8,128)}, f32[3,128,128]{2,1,0:T(8,128)}, f32[128,128]{1,0:T(...) custom-call(f32[2,512,512]{2,1,0:T(8,128)} %get-tuple-element.57.ref, ...), custom_call_target="tpu_custom_call" | custom-call | tf_op jit(solution)/shard_map/collect/pallas_call | solution.py:2118
Async XLA Ops:
  7.2 123.4 %all-gather.4.cloned.1.call-start = ((), (), s32[]{:S(2)}) async-start(), calls=%async_computation | async-start | bytes 7667712 | tf_op jit(solution)/shard_map/all_gather | solution.py:2161
Sparse Core Ops, SparseCore 0:
  28.3 51.6 all-gather.3

commit v7 on v6

--- a/solution.py
+++ b/solution.py
@@ -766,6 +766,15 @@
                 arrive(1)
                 arrive(2)
 
+            def first_results(place, unused):
+                @pl.when(place != me)
+                def send():
+                    for number in range(2):
+                        c_copy(number, place).start()
+
+                return unused
+
+            lax.fori_loop(0, tp, first_results, 0)
             lax.fori_loop(tp, group, project, 0)
 
         start = pl.multiple_of(block * span, span)
@@ -819,7 +828,7 @@
             place = block * ratio + part
             low_ref[head, place] = attended[:, part * chunk : (part + 1) * chunk]
 
-            @pl.when(place != me)
+            @pl.when((place != me) & (index >= 4))
             def send(place=place):
                 c_copy(head, place).start()
 
@@ -1617,7 +1626,7 @@
         hook(1, sum_cores)
         hook(2, encoder_part)
         hook(3, sum_pairs)
-        hook(5, sum_fsdp)
+        hook(4, sum_fsdp)
         start = pl.multiple_of(block * span, span)
         at = pl.ds(start, span)
         blank = jnp.zeros((HEAD_DIM, span), jnp.bfloat16)
@@ -1698,10 +1707,6 @@
 
     lax.fori_loop(0, 2 * blocks, attend, 0)
 
-    @pl.when((core == 0) & inner)
-    def last_rows():
-        pass_rows()
-
     sums_ref[...] = jnp.zeros_like(sums_ref)
     sums_ref[:8, :] = stats_ref[...]
 
@@ -1759,6 +1764,11 @@
         head_ref[f] = total[:, f * piece : (f + 1) * piece]
     for copy in h_copies:
         copy.start()
+
+    @pl.when((core == 0) & inner)
+    def last_rows():
+        pass_rows()
+
     sum_line()
 
     for copy in h_copies:
@@ -2110,7 +2120,7 @@
     extra = [struct((3, width), f32), struct((2, width), f32), struct((1, width), f32)]
     extra = extra + [struct((1, 4), f32)]
     still = lambda v: pl.BlockSpec(v.shape, lambda i, rank=len(v.shape): (0,) * rank)
-    steps = 4
+    steps = 2
     moving = lambda v: pl.BlockSpec(
         (1, v.shape[0] * v.shape[1] // steps, v.shape[2]),
         lambda i, per=steps // v.shape[0]: (i // per, i % per, 0),

time: 336 us -> 326 us (0.970)
  Pallas kernels: 299 us -> 290 us
    pallas_call x1, Pallas kernels: 102 us -> 96 us  [forward_group(): pl.pallas_call(functools.partial(forward_kernel, span=span, tp=tp, fsdp=f...]
  transfers between devices with their start and end apart: 1 -> 1, of which waited for: 0 -> 0; matrix products, arithmetic and copies ran while one was open for 0% -> 0% of each run, Pallas kernels for 31% -> 30%
where the time goes in v7:
time: 326 us; the launch traced here: 323 us
  Pallas kernels  290 us (89%)
  blocking collectives  18.9 us (6%)
  between operations  14.3 us (4%)
    pallas_call x1, Pallas kernels, backward_group(): pl.pallas_call(functools.partial(backward_kernel, span=span, tp=tp, fsdp=...  124 us
    pallas_call x1, Pallas kernels, forward_group(): pl.pallas_call(functools.partial(forward_kernel, span=span, tp=tp, fsdp=f...  96 us
    pallas_call x1, Pallas kernels, middle(): pl.pallas_call(functools.partial(middle_kernel, tp=tp, fsdp=fsdp), in_spe...  62.7 us
    all_gather x1, blocking collectives, local_heads(): gathered = lax.all_gather(own_half, 'tp', axis=0, tiled=False)  18.9 us
  transfers between devices with their start and end apart: 1, of which 0 were waited for; matrix products, arithmetic and copies ran while one was open for 0% of the time, Pallas kernels for 30%

profile of v7, /device:TPU:17, one launch (start us, length us, event | category | flops | bytes accessed | tf_op | source)
XLA Modules:
  0.0 323.2 jit_solution(8036859932998836914)
XLA Ops:
  7.2 0.0 all-gather.4.cloned.1.call-start
  7.2 2.0 pack_weights.1
  9.3 18.9 %all-gather = bf16[52,64,128]{2,1,0:T(8,128)(2,1)} all-gather(bf16[13,64,128]{2,1,0:T(8,128)(2,1)} %get-tuple-element.53), channel_id=2, replica_groups=mesh['fsdp'=4,'ctx'=2,'tp'=4] {'tp'}, dimensions={0}, use_global_device_ids=true | all-gather | bytes 1064960 | tf_op jit(solution)/shard_map/all_gather | solution.py:2170
  28.2 0.0 all-gather.4.cloned.1.call-update
  28.2 96.0 %forward_group.1 = (bf16[8,512,512]{2,1,0:T(8,128)(2,1)}, bf16[2,192,4096]{2,1,0:T(8,128)(2,1)}, f32[2,64,4096]{2,1,0:T(8,128)}, f32[2,1,4096]{2,1,0:T(1,128)}, ...) custom-call(s32[2]{0:T(128)} %prefix_ref.3, bf16[2,512,512]{2,1,0:T(8,128)(2,1)} %tokens_ref.5, ...), custom_call_target="tpu_custom_call" | custom-call | flops 60000002048 | bytes 30000000 | tf_op jit(solution)/shard_map/forward_group/pallas_call | solution.py:889
  124.2 0.0 all-gather.4.cloned.1.call-done
  124.2 62.7 %middle.1 = (f32[2,512,512]{2,1,0:T(8,128)}, f32[2,512,512]{2,1,0:T(8,128)}, bf16[2,8,64,512]{3,2,1,0:T(8,128)(2,1)}, bf16[2,256,1024]{2,1,0:T(8,128)(2,1)}, f32...) custom-call(bf16[4,2,4,13,64,128]{5,4,3,2,1,0:T(8,128)(2,1)} %bitcast.5, bf16[2,512,512]{2,1,0:T(8,128)(2,1)} %tokens_ref.5, ...), custom_call_target="tpu_custom_call" | custom-call | flops 30000001024 | bytes 30000000 | tf_op jit(solution)/shard_map/middle/pallas_call | solution.py:1175
  187.0 124.3 %backward_group.1 = (f32[2,512,512]{2,1,0:T(8,128)}, f32[2,32,512]{2,1,0:T(8,128)}, f32[3,128,128]{2,1,0:T(8,128)}, f32[128,128]{1,0:T(8,128)}, f32[2,128,128]{2...) custom-call(s32[2]{0:T(128)} %prefix_ref.3, ...), custom_call_target="tpu_custom_call" | custom-call | flops 99999997952 | bytes 40000000 | tf_op jit(solution)/shard_map/backward_group/pallas_call | solution.py:1932
  311.2 4.9 %collect.1 = (f32[2,512,512]{2,1,0:T(8,128)}, f32[2,512,512]{2,1,0:T(8,128)}, f32[2,32,512]{2,1,0:T(8,128)}, f32[3,128,128]{2,1,0:T(8,128)}, f32[128,128]{1,0:T(...) custom-call(f32[2,512,512]{2,1,0:T(8,128)} %get-tuple-element.57.ref, ...), custom_call_target="tpu_custom_call" | custom-call | tf_op jit(solution)/shard_map/collect/pallas_call | solution.py:2128
Async XLA Ops:
  7.2 117.1 %all-gather.4.cloned.1.call-start = ((), (), s32[]{:S(2)}) async-start(), calls=%async_computation | async-start | bytes 7667712 | tf_op jit(solution)/shard_map/all_gather | solution.py:2171
Sparse Core Ops, SparseCore 0:
  28.3 51.6 all-gather.3

commit v8 on v7

--- a/solution.py
+++ b/solution.py
@@ -532,7 +532,7 @@
 MESH = pl.DeviceIdType.MESH
 
 
-def meet(group, tp, fsdp):
+def greet(group, tp, fsdp):
     here, core, chip = lax.axis_index("fsdp"), lax.axis_index("ctx"), lax.axis_index("tp")
     me = core * tp + chip
     barrier = pltpu.get_barrier_semaphore()
@@ -543,7 +543,10 @@
         )
     for k in range(1, fsdp):
         pl.semaphore_signal(barrier, inc=1, device_id={"fsdp": here ^ k}, device_id_type=MESH)
-    pl.semaphore_wait(barrier, group - 1 + fsdp - 1)
+
+
+def meet(group, fsdp):
+    pl.semaphore_wait(pltpu.get_barrier_semaphore(), group - 1 + fsdp - 1)
 
 
 def forward_kernel(
@@ -592,7 +595,7 @@
     mine = chip // 2
     inner = (chip == 1) | (chip == 2)
     other_inner, other_outer = 2 - mine, 3 - 3 * mine
-    meet(group, tp, fsdp)
+    greet(group, tp, fsdp)
 
     def send_to(source, target, send, recv, **place):
         return pltpu.make_async_remote_copy(
@@ -604,6 +607,14 @@
             device_id_type=MESH,
         )
 
+    def normalise(seq, target, at):
+        start_sum = tokens_ref[seq].astype(jnp.float32) + step_ref[seq]
+        target[at] = rows_norm(start_sum, gain_ref[0:1], bias_ref[0:1])[0]
+
+    normalise(mine, rows_ref, me)
+    normalise(1 - mine, other_ref, 0)
+    meet(group, fsdp)
+
     v_core, v_chip = chip % 2, chip // 2 + 2 * core
     v_own = (v_core == core) & (v_chip == chip)
     v_copy = send_to(mine_ref, pair_ref, v_send.at[0], v_recv.at[0], ctx=v_core, tp=v_chip)
@@ -620,10 +631,6 @@
 
     def w_copy(k):
         return send_to(pair_ref, columns.at[k], w_send.at[k], w_recv.at[k], fsdp=here ^ k)
-
-    def normalise(seq, target, at):
-        start_sum = tokens_ref[seq].astype(jnp.float32) + step_ref[seq]
-        target[at] = rows_norm(start_sum, gain_ref[0:1], bias_ref[0:1])[0]
 
     def x_copy(kind):
         block = rows_ref.at[me]
@@ -658,8 +665,6 @@
 
         x_copy(3 + number).start()
 
-    normalise(mine, rows_ref, me)
-    normalise(1 - mine, other_ref, 0)
 
     @pl.when(core == 0)
     def first_half():
@@ -976,7 +981,7 @@
     core, chip = lax.axis_index("ctx"), lax.axis_index("tp")
     me = core * tp + chip
     mine = chip // 2
-    meet(group, tp, fsdp)
+    greet(group, tp, fsdp)
     piece = gathered.shape[-1]
     factor = HEAD_DIM**-0.5
     heads = width // HEAD_DIM
@@ -1099,6 +1104,11 @@
         grad_one = low(grad_after_one)
         grad_one_all[at, :] = grad_one
         back_rows[turn] = low(dot_of(weights[SELF_OUT], grad_one, 1, 1))
+
+        @pl.when(turn == 0)
+        def all_here():
+            meet(group, fsdp)
+
         for head, number, owner in owners:
 
             @pl.when(owner + 2 * seq != me)
@@ -1318,7 +1328,7 @@
     share = enc_landing.shape[2]
     piece = width // fsdp
     early = packed.shape[3]
-    meet(group, tp, fsdp)
+    greet(group, tp, fsdp)
 
     def send_to(source, target, send, recv, **place):
         return pltpu.make_async_remote_copy(
@@ -1439,71 +1449,6 @@
         for k in range(1, fsdp)
     ]
 
-    enc_copy.start()
-    core_copy.start()
-    for copy in local:
-        copy.start()
-
-    def core_rows_copy(place):
-        slot = place % tp
-        return send_to(
-            core_rows.at[slot], core_rows_landing.at[slot], x_send.at[slot], x_recv.at[slot], ctx=1 - core
-        )
-
-    def owner_copy(place):
-        slot = place % tp
-        return send_to(
-            sum_rows.at[slot],
-            incoming.at[mine, chip % 2],
-            i_send.at[slot],
-            i_recv.at[mine, chip % 2],
-            tp=slot,
-        )
-
-    def spread(place):
-        upstream = dot_of(outgoing[place].reshape(6 * HEAD_DIM, chunk), weight[...], 0, 0)
-        slot = place % tp
-
-        @pl.when(place // tp != core)
-        def hand_over():
-            core_rows[slot] = low(upstream)
-            core_rows_copy(place).start()
-
-        @pl.when(place // tp == core)
-        def collect():
-            core_rows_copy(place).wait_recv()
-            total = low(upstream + core_rows_landing[slot].astype(jnp.float32))
-
-            @pl.when(place == me)
-            def own():
-                incoming[mine, chip % 2] = total
-
-            @pl.when(place != me)
-            def send():
-                sum_rows[slot] = total
-
-                @pl.when((core == 0) & (slot // 2 != mine) & jnp.logical_not(inner))
-                def to_inner():
-                    beside_copy(slot).start()
-
-                @pl.when((core == 1) | (slot // 2 == mine))
-                def to_owner():
-                    owner_copy(place).start()
-
-    def beside_copy(slot):
-        return send_to(
-            sum_rows.at[slot], beside.at[slot % 2], i_send.at[slot], b_recv.at[slot % 2], tp=chip ^ 1
-        )
-
-    def pass_rows():
-        for n in range(2):
-            slot = 2 * (1 - mine) + n
-            beside_copy(slot).wait_recv()
-            sum_rows[slot] = low(
-                sum_rows[slot].astype(jnp.float32) + beside[n].astype(jnp.float32)
-            )
-            owner_copy(slot).start()
-
     def prepare(seq):
         def lay(place, unused):
             at = pl.ds(pl.multiple_of(place * chunk, chunk), chunk)
@@ -1520,6 +1465,75 @@
         lax.fori_loop(0, group, lay, 0)
         grad_pairs_ref[seq] = jnp.zeros(grad_pairs_ref.shape[1:], jnp.float32)
 
+    for copy in local:
+        copy.start()
+    for head in range(2):
+        prepare(head)
+
+    meet(group, fsdp)
+    enc_copy.start()
+    core_copy.start()
+
+    def core_rows_copy(place):
+        slot = place % tp
+        return send_to(
+            core_rows.at[slot], core_rows_landing.at[slot], x_send.at[slot], x_recv.at[slot], ctx=1 - core
+        )
+
+    def owner_copy(place):
+        slot = place % tp
+        return send_to(
+            sum_rows.at[slot],
+            incoming.at[mine, chip % 2],
+            i_send.at[slot],
+            i_recv.at[mine, chip % 2],
+            tp=slot,
+        )
+
+    def spread(place):
+        upstream = dot_of(outgoing[place].reshape(6 * HEAD_DIM, chunk), weight[...], 0, 0)
+        slot = place % tp
+
+        @pl.when(place // tp != core)
+        def hand_over():
+            core_rows[slot] = low(upstream)
+            core_rows_copy(place).start()
+
+        @pl.when(place // tp == core)
+        def collect():
+            core_rows_copy(place).wait_recv()
+            total = low(upstream + core_rows_landing[slot].astype(jnp.float32))
+
+            @pl.when(place == me)
+            def own():
+                incoming[mine, chip % 2] = total
+
+            @pl.when(place != me)
+            def send():
+                sum_rows[slot] = total
+
+                @pl.when((core == 0) & (slot // 2 != mine) & jnp.logical_not(inner))
+                def to_inner():
+                    beside_copy(slot).start()
+
+                @pl.when((core == 1) | (slot // 2 == mine))
+                def to_owner():
+                    owner_copy(place).start()
+
+    def beside_copy(slot):
+        return send_to(
+            sum_rows.at[slot], beside.at[slot % 2], i_send.at[slot], b_recv.at[slot % 2], tp=chip ^ 1
+        )
+
+    def pass_rows():
+        for n in range(2):
+            slot = 2 * (1 - mine) + n
+            beside_copy(slot).wait_recv()
+            sum_rows[slot] = low(
+                sum_rows[slot].astype(jnp.float32) + beside[n].astype(jnp.float32)
+            )
+            owner_copy(slot).start()
+
     def encoder_cores():
         local[1].wait()
         enc_copy.wait_recv()
@@ -1610,9 +1624,6 @@
             total = total + line_landing[k].astype(jnp.float32)
         shard_ref[core] = total
         shard_copy.start()
-
-    for head in range(2):
-        prepare(head)
 
     def attend(index, unused):
         block, seq = blocks - 1 - index // 2, index % 2

time: 326 us -> 320 us (0.982)
  Pallas kernels: 290 us -> 286 us
    pallas_call x1, Pallas kernels: 62.7 us -> 59.3 us  [middle(): pl.pallas_call(functools.partial(middle_kernel, tp=tp, fsdp=fsdp), in_spe...]
where the time goes in v8:
time: 320 us; the launch traced here: 319 us
  Pallas kernels  286 us (89%)
  blocking collectives  18.9 us (6%)
  between operations  14.3 us (4%)
    pallas_call x1, Pallas kernels, backward_group(): pl.pallas_call(functools.partial(backward_kernel, span=span, tp=tp, fsdp=...  124 us
    pallas_call x1, Pallas kernels, forward_group(): pl.pallas_call(functools.partial(forward_kernel, span=span, tp=tp, fsdp=f...  95.2 us
    pallas_call x1, Pallas kernels, middle(): pl.pallas_call(functools.partial(middle_kernel, tp=tp, fsdp=fsdp), in_spe...  59.3 us
    all_gather x1, blocking collectives, local_heads(): gathered = lax.all_gather(own_half, 'tp', axis=0, tiled=False)  18.9 us
  transfers between devices with their start and end apart: 1, of which 0 were waited for; matrix products, arithmetic and copies ran while one was open for 0% of the time, Pallas kernels for 30%

profile of v8, /device:TPU:17, one launch (start us, length us, event | category | flops | bytes accessed | tf_op | source)
XLA Modules:
  0.0 318.8 jit_solution(15109272974802214203)
XLA Ops:
  7.2 0.0 all-gather.4.cloned.1.call-start
  7.2 2.0 pack_weights.1
  9.3 18.9 %all-gather = bf16[52,64,128]{2,1,0:T(8,128)(2,1)} all-gather(bf16[13,64,128]{2,1,0:T(8,128)(2,1)} %get-tuple-element.53), channel_id=2, replica_groups=mesh['fsdp'=4,'ctx'=2,'tp'=4] {'tp'}, dimensions={0}, use_global_device_ids=true | all-gather | bytes 1064960 | tf_op jit(solution)/shard_map/all_gather | solution.py:2181
  28.2 0.0 all-gather.4.cloned.1.call-update
  28.2 95.2 %forward_group.1 = (bf16[8,512,512]{2,1,0:T(8,128)(2,1)}, bf16[2,192,4096]{2,1,0:T(8,128)(2,1)}, f32[2,64,4096]{2,1,0:T(8,128)}, f32[2,1,4096]{2,1,0:T(1,128)}, ...) custom-call(s32[2]{0:T(128)} %prefix_ref.3, bf16[2,512,512]{2,1,0:T(8,128)(2,1)} %tokens_ref.5, ...), custom_call_target="tpu_custom_call" | custom-call | flops 60000002048 | bytes 30000000 | tf_op jit(solution)/shard_map/forward_group/pallas_call | solution.py:894
  123.4 0.0 all-gather.4.cloned.1.call-done
  123.4 59.3 %middle.1 = (f32[2,512,512]{2,1,0:T(8,128)}, f32[2,512,512]{2,1,0:T(8,128)}, bf16[2,8,64,512]{3,2,1,0:T(8,128)(2,1)}, bf16[2,256,1024]{2,1,0:T(8,128)(2,1)}, f32...) custom-call(bf16[4,2,4,13,64,128]{5,4,3,2,1,0:T(8,128)(2,1)} %bitcast.5, bf16[2,512,512]{2,1,0:T(8,128)(2,1)} %tokens_ref.5, ...), custom_call_target="tpu_custom_call" | custom-call | flops 30000001024 | bytes 30000000 | tf_op jit(solution)/shard_map/middle/pallas_call | solution.py:1185
  182.7 124.2 %backward_group.1 = (f32[2,512,512]{2,1,0:T(8,128)}, f32[2,32,512]{2,1,0:T(8,128)}, f32[3,128,128]{2,1,0:T(8,128)}, f32[128,128]{1,0:T(8,128)}, f32[2,128,128]{2...) custom-call(s32[2]{0:T(128)} %prefix_ref.3, ...), custom_call_target="tpu_custom_call" | custom-call | flops 99999997952 | bytes 40000000 | tf_op jit(solution)/shard_map/backward_group/pallas_call | solution.py:1943
  306.9 4.9 %collect.1 = (f32[2,512,512]{2,1,0:T(8,128)}, f32[2,512,512]{2,1,0:T(8,128)}, f32[2,32,512]{2,1,0:T(8,128)}, f32[3,128,128]{2,1,0:T(8,128)}, f32[128,128]{1,0:T(...) custom-call(f32[2,512,512]{2,1,0:T(8,128)} %get-tuple-element.57.ref, ...), custom_call_target="tpu_custom_call" | custom-call | tf_op jit(solution)/shard_map/collect/pallas_call | solution.py:2139
Async XLA Ops:
  7.2 116.2 %all-gather.4.cloned.1.call-start = ((), (), s32[]{:S(2)}) async-start(), calls=%async_computation | async-start | bytes 7667712 | tf_op jit(solution)/shard_map/all_gather | solution.py:2182
Sparse Core Ops, SparseCore 0:
  28.3 52.3 all-gather.3
